TPU v7x, 32 devices: a whole 2x2x4 slice. The times are simulated.
32 devices in a mesh: dp: 8 (over z, y), tensor: 4 (over x, core).
Axes of the slice: x: 2, y: 2, z: 4, core: 2. Of those that a mesh axis runs over, the one named last changes fastest.
Arguments:
- block_input: bfloat16 [32, 512, 1024], P('dp'), may hold values from -6 to 6
- segment_ids: int32 [32, 512], P('dp'), may hold values from 0 to 3, never falling along the last dimension, each value on 1 to 256 neighbouring positions
- query_weight: bfloat16 [1024, 1024], P(None, 'tensor')
- key_weight: bfloat16 [1024, 1024], P(None, 'tensor'), may hold values from -0.1875 to 0.1875
- value_weight: bfloat16 [1024, 1024], P(None, 'tensor'), may hold values from -0.1875 to 0.1875
- output_weight: bfloat16 [1024, 1024], P('tensor'), may hold values from -0.375 to 0.375
- first_gain: float32 [1024], replicated, may hold values from 0.1 to 1.9
- first_shift: float32 [1024], replicated, may hold values from -3 to 3
- up_weight: bfloat16 [1024, 4096], P(None, 'tensor'), may hold values from -0.1875 to 0.1875
- down_weight: bfloat16 [4096, 1024], P('tensor'), may hold values from -0.125 to 0.125
- second_gain: float32 [1024], replicated, may hold values from 0.1 to 1.9
- second_shift: float32 [1024], replicated, may hold values from -3 to 3
- out_grad: bfloat16 [32, 512, 1024], P('dp'), may hold values from -6 to 6
Outputs:
- layer_out: bfloat16 [32, 512, 1024], P('dp')
- input_grad: bfloat16 [32, 512, 1024], P('dp')
- query_grad: float32 [1024, 1024], P('dp', 'tensor')
- key_grad: float32 [1024, 1024], P('dp', 'tensor')
- value_grad: float32 [1024, 1024], P('dp', 'tensor')
- output_grad: float32 [1024, 1024], P('tensor', 'dp')
- first_gain_grad: float32 [1024], P('dp')
- first_shift_grad: float32 [1024], P('dp')
- up_grad: float32 [1024, 4096], P('dp', 'tensor')
- down_grad: float32 [4096, 1024], P('tensor', 'dp')
- second_gain_grad: float32 [1024], P('dp')
- second_shift_grad: float32 [1024], P('dp')
- query_clipped: float32 [1024, 1024], P(None, 'tensor')
- key_clipped: float32 [1024, 1024], P(None, 'tensor')
Inputs may be any that keep to these rules, and one draw needn't show every extreme that they name: `segment_ids`: ids within a sequence never fall; each document has 1 to 256 tokens.
All inputs are finite; a program needn't handle non-finite values.
Results may differ from a plain program's by a relative error of at most 0.014.
The roundings to bfloat16 on the way count: a program that leaves them out, or rounds other values in their place, can miss the bound.
Values sent between devices are 32-bit elements; how exact they have to be, the bound alone decides.
No kernel may reach another device: no remote copies, remote signals or barrier semaphores. Data moves between devices by JAX's collectives and lax.ppermute only.
A program may use at most 192 MiB of HBM per device.

v0:
```python
import jax
import jax.numpy as jnp
from jax import lax
from jax.sharding import PartitionSpec as P

HEAD_DIM = 64
WINDOW = 256


far_score = -1e30
eps_norm = 1e-06
clip_limit = 10.0


def normalize(total):
    average = jnp.mean(total, axis=-1, keepdims=True)
    centred = total - average
    variance = jnp.mean(centred * centred, axis=-1, keepdims=True)
    scaled = lax.rsqrt(variance + eps_norm)
    return (centred * scaled, scaled)


def norm_back(upstream, normed, scaled, gain):
    weighted = upstream * gain
    first_mean = jnp.mean(weighted, axis=-1, keepdims=True)
    second_mean = jnp.mean(weighted * normed, axis=-1, keepdims=True)
    return scaled * (weighted - first_mean - normed * second_mean)


def exact_gelu(inputs):
    return jax.nn.gelu(inputs, approximate=False)


def window_mask(segments):
    places = jnp.arange(segments.shape[0])
    nearby = jnp.abs(places[:, None] - places[None, :]) < WINDOW
    return nearby & (segments[:, None] == segments[None, :])


def score_block(queries, keys, segments):
    score_scale = queries.shape[-1] ** (-0.5)
    scores = (
        jnp.einsum("qhd,khd->hqk", queries, keys, preferred_element_type=jnp.float32) * score_scale
    )
    return jnp.where(window_mask(segments)[None], scores, far_score)


def attend_forward(pieces):
    queries, keys, values, segments = pieces
    masked = score_block(queries, keys, segments)
    row_top = jnp.max(masked, axis=-1, keepdims=True)
    raised = jnp.exp(masked - row_top)
    totals = jnp.sum(raised, axis=-1, keepdims=True)
    chances = (raised / totals).astype(jnp.bfloat16)
    mixed = jnp.einsum("hqk,khd->qhd", chances, values, preferred_element_type=jnp.float32).astype(
        jnp.bfloat16
    )
    log_total = row_top[:, :, 0] + jnp.log(totals[:, :, 0])
    return (mixed, log_total, jnp.max(row_top, axis=(1, 2)))


def attend_back(pieces):
    queries, keys, values, upstream, log_total, segments = pieces
    score_scale = queries.shape[-1] ** (-0.5)
    masked = score_block(queries, keys, segments)
    chances = jnp.exp(masked - log_total[:, :, None])
    drift = jnp.einsum("qhd,khd->hqk", upstream, values, preferred_element_type=jnp.float32)
    slopes = chances * (drift - jnp.sum(drift * chances, axis=-1, keepdims=True))
    slopes_low = slopes.astype(jnp.bfloat16)
    query_slope = (
        jnp.einsum("hqk,khd->qhd", slopes_low, keys, preferred_element_type=jnp.float32)
        * score_scale
    )
    key_slope = (
        jnp.einsum("hqk,qhd->khd", slopes_low, queries, preferred_element_type=jnp.float32)
        * score_scale
    )
    value_slope = jnp.einsum(
        "hqk,qhd->khd", chances.astype(jnp.bfloat16), upstream, preferred_element_type=jnp.float32
    )
    return (query_slope, key_slope, value_slope)


def settle(partial_sum, residual, section):
    if section == 1:
        total = lax.psum(partial_sum, "tensor")
    else:
        total = lax.psum(partial_sum, "tensor")
    return normalize(residual + total)


def reduce_grads(row_terms, column_terms):
    summed_rows = (
        lax.psum_scatter(row_terms[0], "dp", scatter_dimension=0, tiled=True),
        lax.psum_scatter(row_terms[1], "dp", scatter_dimension=0, tiled=True),
        lax.psum_scatter(row_terms[2], "dp", scatter_dimension=0, tiled=True),
        lax.psum_scatter(row_terms[3], "dp", scatter_dimension=0, tiled=True),
        lax.psum_scatter(row_terms[4], "dp", scatter_dimension=0, tiled=True),
        lax.psum_scatter(row_terms[5], "dp", scatter_dimension=0, tiled=True),
        lax.psum_scatter(row_terms[6], "dp", scatter_dimension=0, tiled=True),
        lax.psum_scatter(row_terms[7], "dp", scatter_dimension=0, tiled=True),
    )
    summed_cols = (
        lax.psum_scatter(column_terms[0], "dp", scatter_dimension=1, tiled=True),
        lax.psum_scatter(column_terms[1], "dp", scatter_dimension=1, tiled=True),
    )
    return (summed_rows, summed_cols)


def body(
    block_input,
    segment_ids,
    query_weight,
    key_weight,
    value_weight,
    output_weight,
    first_gain,
    first_shift,
    up_weight,
    down_weight,
    second_gain,
    second_shift,
    out_grad,
):
    seq_count, seq_len, model_width = block_input.shape
    row_count = seq_count * seq_len
    head_dim = HEAD_DIM
    local_heads = query_weight.shape[1] // head_dim
    flat_input = block_input.reshape(row_count, model_width)

    def heads_of(weight):
        product = jnp.dot(flat_input, weight, preferred_element_type=jnp.float32)
        return product.astype(jnp.bfloat16).reshape(seq_count, seq_len, local_heads, head_dim)

    queries = heads_of(query_weight)
    keys = heads_of(key_weight)
    values = heads_of(value_weight)
    mixed, log_totals, head_tops = lax.map(attend_forward, (queries, keys, values, segment_ids))
    head_peak = lax.pmax(jnp.max(head_tops, axis=0), "dp")
    mixed_rows = mixed.reshape(row_count, local_heads * head_dim)
    branch_one = jnp.dot(mixed_rows, output_weight, preferred_element_type=jnp.float32).reshape(
        seq_count, seq_len, model_width
    )
    residual_one = block_input.astype(jnp.float32)
    normed_one, scaled_one = settle(branch_one, residual_one, 1)
    hidden = normed_one * first_gain + first_shift
    hidden_low = hidden.astype(jnp.bfloat16).reshape(row_count, model_width)
    before = jnp.dot(hidden_low, up_weight, preferred_element_type=jnp.float32)
    active = exact_gelu(before).astype(jnp.bfloat16)
    branch_two = jnp.dot(active, down_weight, preferred_element_type=jnp.float32).reshape(
        seq_count, seq_len, model_width
    )
    normed_two, scaled_two = settle(branch_two, hidden, 2)
    layer_out = (normed_two * second_gain + second_shift).astype(jnp.bfloat16)
    upstream = out_grad.astype(jnp.float32)
    second_gain_part = jnp.sum(upstream * normed_two, axis=(0, 1))
    second_shift_part = jnp.sum(upstream, axis=(0, 1))
    slope_two = norm_back(upstream, normed_two, scaled_two, second_gain)
    slope_two_low = slope_two.astype(jnp.bfloat16).reshape(row_count, model_width)
    down_part = jnp.einsum("rf,rd->fd", active, slope_two_low, preferred_element_type=jnp.float32)
    active_slope = jnp.einsum(
        "rd,fd->rf", slope_two_low, down_weight, preferred_element_type=jnp.float32
    )
    gelu_value, gelu_pull = jax.vjp(exact_gelu, before)
    before_slope = gelu_pull(active_slope)[0].astype(jnp.bfloat16)
    up_part = jnp.einsum("rd,rf->df", hidden_low, before_slope, preferred_element_type=jnp.float32)
    hidden_part = jnp.einsum(
        "rf,df->rd", before_slope, up_weight, preferred_element_type=jnp.float32
    )
    hidden_sum = lax.psum(hidden_part, "tensor")
    hidden_slope = slope_two + hidden_sum.reshape(seq_count, seq_len, model_width)
    first_gain_part = jnp.sum(hidden_slope * normed_one, axis=(0, 1))
    first_shift_part = jnp.sum(hidden_slope, axis=(0, 1))
    slope_one = norm_back(hidden_slope, normed_one, scaled_one, first_gain)
    slope_one_low = slope_one.astype(jnp.bfloat16).reshape(row_count, model_width)
    output_part = jnp.einsum(
        "re,rd->ed", mixed_rows, slope_one_low, preferred_element_type=jnp.float32
    )
    mixed_slope = jnp.einsum(
        "rd,ed->re", slope_one_low, output_weight, preferred_element_type=jnp.float32
    )
    mixed_slope = mixed_slope.astype(jnp.bfloat16).reshape(
        seq_count, seq_len, local_heads, head_dim
    )
    query_slope, key_slope, value_slope = lax.map(
        attend_back, (queries, keys, values, mixed_slope, log_totals, segment_ids)
    )

    def flat_heads(slope):
        return slope.astype(jnp.bfloat16).reshape(row_count, local_heads * head_dim)

    query_low = flat_heads(query_slope)
    key_low = flat_heads(key_slope)
    value_low = flat_heads(value_slope)
    query_part = jnp.einsum("rd,re->de", flat_input, query_low, preferred_element_type=jnp.float32)
    key_part = jnp.einsum("rd,re->de", flat_input, key_low, preferred_element_type=jnp.float32)
    value_part = jnp.einsum("rd,re->de", flat_input, value_low, preferred_element_type=jnp.float32)
    input_part = jnp.einsum(
        "re,de->rd", query_low, query_weight, preferred_element_type=jnp.float32
    )
    input_part = input_part + jnp.einsum(
        "re,de->rd", key_low, key_weight, preferred_element_type=jnp.float32
    )
    input_part = input_part + jnp.einsum(
        "re,de->rd", value_low, value_weight, preferred_element_type=jnp.float32
    )
    input_sum = lax.psum(input_part, "tensor")
    input_grad = (slope_one + input_sum.reshape(seq_count, seq_len, model_width)).astype(
        jnp.bfloat16
    )
    summed_rows, summed_cols = reduce_grads(
        (
            query_part,
            key_part,
            value_part,
            first_gain_part,
            first_shift_part,
            up_part,
            second_gain_part,
            second_shift_part,
        ),
        (output_part, down_part),
    )
    (
        query_grad,
        key_grad,
        value_grad,
        first_gain_grad,
        first_shift_grad,
        up_grad,
        second_gain_grad,
        second_shift_grad,
    ) = summed_rows
    output_grad, down_grad = summed_cols
    factor = jnp.sqrt(clip_limit / jnp.maximum(head_peak, clip_limit))
    column_factor = jnp.repeat(factor, head_dim)
    query_clipped = query_weight.astype(jnp.float32) * column_factor[None, :]
    key_clipped = key_weight.astype(jnp.float32) * column_factor[None, :]
    return (
        layer_out,
        input_grad,
        query_grad,
        key_grad,
        value_grad,
        output_grad,
        first_gain_grad,
        first_shift_grad,
        up_grad,
        down_grad,
        second_gain_grad,
        second_shift_grad,
        query_clipped,
        key_clipped,
    )


def solution(mesh):
    in_specs = (
        P("dp", None, None),
        P("dp", None),
        P(None, "tensor"),
        P(None, "tensor"),
        P(None, "tensor"),
        P("tensor", None),
        P(),
        P(),
        P(None, "tensor"),
        P("tensor", None),
        P(),
        P(),
        P("dp", None, None),
    )
    out_specs = (
        P("dp", None, None),
        P("dp", None, None),
        P("dp", "tensor"),
        P("dp", "tensor"),
        P("dp", "tensor"),
        P("tensor", "dp"),
        P("dp"),
        P("dp"),
        P("dp", "tensor"),
        P("tensor", "dp"),
        P("dp"),
        P("dp"),
        P(None, "tensor"),
        P(None, "tensor"),
    )
    return jax.shard_map(body, mesh=mesh, in_specs=in_specs, out_specs=out_specs, check_vma=False)
```

profile of v0, /device:TPU:0, one launch (start us, length us, event | category | flops | bytes accessed | tf_op | source)
XLA Modules:
  0.0 1335.6 jit_solution(15093317186258666803)
XLA Ops:
  7.3 3.7 convolution_convert_fusion.1
  12.8 2.9 copy.74
  15.7 4.5 convolution_convert_fusion.2
  20.2 4.4 reshape.256
  24.6 4.0 copy.73
  28.7 4.5 convolution_convert_fusion.3
  33.2 4.4 reshape.255
  37.6 4.0 copy.72
  41.6 36.5 %while.28 = (s32[]{:T(128)}, bf16[4,512,4,64]{1,3,2,0:T(8,128)(2,1)}, f32[4,4,512]{2,1,0:T(4,128)}, f32[4,4]{1,0:T(4,128)}, bf16[4,512,4,64]{1,3,2,0:T(8,128)(2,...) while((s32[]{:T(128)}, ...), condition=%wide.region_4.5_spmd, body=%wide.region_0.4_spmd.sunk | while | flops 283506688 | bytes 14753961 | solution.py:138
  42.6 1.9 fusion.146
  45.8 3.0 fusion.148
  51.8 1.9 fusion.146
  55.0 3.0 fusion.148
  60.9 1.9 fusion.146
  64.1 3.0 fusion.148
  70.0 1.9 fusion.146
  73.2 3.0 fusion.148
  78.2 6.2 fusion.75
  84.5 155.7 %all-reduce.10.cloned.1.call-done = f32[4,512,1024]{2,1,0:T(8,128)} async-done(((f32[4,512,1024]{2,1,0:T(8,128)}), f32[4,512,1024]{2,1,0:T(8,128)}) %all-reduce.10.cloned.1.call-update) | async-done | bytes 8388624 | tf_op jit(solution)/shard_map/psum | solution.py:86
  240.1 5.5 fusion.81
  248.8 24.0 %multiply_convert_fusion.1 = (bf16[2048,1024]{1,0:T(8,128)(2,1)S(1)}, f32[2048,1024]{1,0:T(8,128)}, f32[2048,1024]{1,0:T(8,128)}) fusion(bf16[2048,1024]{1,0:T(8,128)(2,1)S(1)} %bitcast.201, bf16[1024,1024]{1,0:T(8,128)(2,1)S(1)} %copy-done), kind=kOutput, calls=%fused_computation.86 | convolution fusion | flops 4431282176 | bytes 27262976 | tf_op jit(solution)/shard_map/dot_general | solution.py:148
  272.8 6.6 fusion.82
  279.5 153.1 %all-reduce.12.cloned.1.call-done = f32[4,512,1024]{2,1,0:T(8,128)} async-done(((f32[4,512,1024]{2,1,0:T(8,128)}), f32[4,512,1024]{2,1,0:T(8,128)}) %all-reduce.12.cloned.1.call-update) | async-done | bytes 8388624 | tf_op jit(solution)/shard_map/psum | solution.py:88
  432.7 6.9 fusion.78
  440.8 4.0 copy-done.4
  444.8 4.8 fusion.64
  449.7 2.7 fusion.73
  452.4 12.6 add_convert_fusion.1
  465.1 7.0 fusion.83
  472.2 153.1 %all-reduce.14.cloned.1.call-done = f32[4,512,1024]{2,1,0:T(8,128)} async-done(((f32[4,512,1024]{2,1,0:T(8,128)}), f32[4,512,1024]{2,1,0:T(8,128)}) %all-reduce.14.cloned.1.call-update) | async-done | bytes 8388624 | tf_op jit(solution)/shard_map/psum | solution.py:170
  625.3 14.4 %multiply_reduce_fusion.1 = (f32[1024]{0:T(1024)S(1)}, f32[4,512]{1,0:T(4,128)S(1)}, f32[4,512]{1,0:T(4,128)S(1)}, f32[1024]{0:T(1024)S(1)}, f32[4,512,1024]{2,1,0:T(8,128)S(1)}, /*index=5*/bf16[4,512,1024]{2,1,0:T(8,128)(2,1)}) fusion(f32[4,512,1024]{2,1,0:T(8,128)} %copy-done.1, f32[4,512]{1,0:T(4,128)S(1)} %add_rsqrt_fusion.1, ...), kind=kLoop, calls=%fused_computation.78 | loop fusion | flops 44034048 | bytes 42029056 | tf_op jit(solution)/shard_map/reduce_sum | solution.py:172
  639.7 7.7 fusion.74
  647.4 2.0 copy-done.13
  649.4 2.3 convolution_convert_fusion
  651.8 4.5 reshape.250
  656.2 4.1 copy.79
  660.3 55.9 %while.29 = (s32[]{:T(128)}, bf16[4,512,4,64]{1,3,2,0:T(8,128)(2,1)}, bf16[4,512,4,64]{1,3,2,0:T(8,128)(2,1)}, bf16[4,512,4,64]{1,3,2,0:T(8,128)(2,1)}, bf16[4,5...) while((s32[]{:T(128)}, ...), condition=%wide.region_18.19_spmd, body=%wide.region_16.18_spmd.sunk | while | flops 688388096 | bytes 52759788 | solution.py:185
  663.7 2.9 fusion.161
  666.6 2.6 multiply_reduce_fusion.7
  677.6 2.9 fusion.161
  680.5 2.6 multiply_reduce_fusion.7
  691.6 2.9 fusion.161
  694.4 2.6 multiply_reduce_fusion.7
  705.5 2.9 fusion.161
  708.4 2.6 multiply_reduce_fusion.7
  716.3 2.1 copy.83
  719.7 4.4 convolution_bitcast_fusion
  725.3 4.4 convolution_bitcast_fusion.2
  729.8 2.0 copy.82
  733.0 4.5 convolution_bitcast_fusion.1
  737.6 2.7 fusion.85
  741.7 4.6 add_add_fusion
  748.6 4.5 fusion.86
  753.1 10.1 fusion.87
  763.4 10.0 fusion.88
  773.5 21.4 %pmax.7 = f32[4]{0:T(128)S(1)} all-reduce(f32[4]{0:T(128)S(1)} %reduce_max.27), channel_id=1, replica_groups=mesh['dp'=8,'tensor'=4] {'dp'}, use_global_device_ids=true, to_apply=%region_35.36 | all-reduce | flops 4 | bytes 32 | tf_op jit(solution)/shard_map/pmax | solution.py:139
  797.9 33.2 %all-reduce.4 = (f32[1024]{0:T(1024)S(1)}, f32[1024]{0:T(1024)S(1)}, f32[1024]{0:T(1024)S(1)}, f32[1024]{0:T(1024)S(1)}) all-reduce(f32[1024]{0:T(1024)S(1)} %get-tuple-element.216, f32[1024]{0:T(1024)S(1)} %get-tuple-element.221, f32[1024]{0:T(1024)S(1)} %copy-done.26, ...), channel_id=6, replica_groups=mesh['dp'=8,'tensor'=4] {'dp'}, use_global_device_ids=true, to_apply=%region_25.26.clone | all-reduce | flops 4096 | bytes 32768
  835.1 20.1 %reduce-scatter.7.cloned.1.call-done = f32[128,256]{0,1:T(8,128)} async-done(((f32[1024,256]{0,1:T(8,128)}), f32[128,256]{0,1:T(8,128)}) %reduce-scatter.7.cloned.1.call-update) | async-done | bytes 131088 | tf_op jit(solution)/shard_map/reduce_scatter | solution.py:94
  856.8 64.6 %reduce-scatter.9.cloned.1.call-done = f32[128,256]{0,1:T(8,128)} async-done(((f32[1024,256]{0,1:T(8,128)}), f32[128,256]{0,1:T(8,128)}) %reduce-scatter.9.cloned.1.call-update) | async-done | bytes 131088 | tf_op jit(solution)/shard_map/reduce_scatter | solution.py:95
  923.1 152.8 %all-reduce.16.cloned.1.call-done = f32[4,512,1024]{2,1,0:T(8,128)} async-done(((f32[4,512,1024]{2,1,0:T(8,128)}), f32[4,512,1024]{2,1,0:T(8,128)}) %all-reduce.16.cloned.1.call-update) | async-done | bytes 8388624 | tf_op jit(solution)/shard_map/psum | solution.py:207
  1075.9 11.6 add_convert_fusion
  1087.5 56.8 %reduce-scatter.13.cloned.1.call-done = f32[256,128]{1,0:T(8,128)} async-done(((f32[256,1024]{1,0:T(8,128)}), f32[256,128]{1,0:T(8,128)}) %reduce-scatter.13.cloned.1.call-update) | async-done | bytes 131088 | tf_op jit(solution)/shard_map/reduce_scatter | solution.py:104
  1144.3 91.3 %reduce-scatter.15.cloned.1.call-done = f32[128,1024]{1,0:T(8,128)} async-done(((f32[1024,1024]{1,0:T(8,128)}), f32[128,1024]{1,0:T(8,128)}) %reduce-scatter.15.cloned.1.call-update) | async-done | bytes 524304 | tf_op jit(solution)/shard_map/reduce_scatter | solution.py:99
  1235.6 92.7 %reduce-scatter.17.cloned.1.call-done = f32[1024,128]{1,0:T(8,128)} async-done(((f32[1024,1024]{1,0:T(8,128)}), f32[1024,128]{1,0:T(8,128)}) %reduce-scatter.17.cloned.1.call-update) | async-done | bytes 524304 | tf_op jit(solution)/shard_map/reduce_scatter | solution.py:105
  (200 shorter events, 73.7 us)
Async XLA Ops:
  7.2 241.6 %copy-start = (bf16[1024,1024]{1,0:T(8,128)(2,1)S(1)}, bf16[1024,1024]{1,0:T(8,128)(2,1)}, u32[]{:S(2)}) copy-start(bf16[1024,1024]{1,0:T(8,128)(2,1)} %param.25) | copy-start | bytes 6291460
  7.2 232.9 %all-reduce.10.cloned.1.call-start = ((), (), s32[]{:S(2)}) async-start(), calls=%async_computation.6 | async-start | bytes 16777216 | tf_op jit(solution)/shard_map/psum | solution.py:86
  78.2 6.3 copy-start.5
  84.4 348.2 %all-reduce.12.cloned.1.call-start = ((), (), s32[]{:S(2)}) async-start(), calls=%async_computation.7 | async-start | bytes 16777216 | tf_op jit(solution)/shard_map/psum | solution.py:88
  245.6 3.2 copy-start.1
  245.6 1.5 copy-start.24
  245.6 1.5 copy-start.28
  248.8 24.0 %copy-start.12 = (bf16[4,512,1024]{2,1,0:T(8,128)(2,1)}, bf16[4,512,1024]{2,1,0:T(8,128)(2,1)S(1)}, u32[]{:S(2)}) copy-start(bf16[4,512,1024]{2,1,0:T(8,128)(2,1)S(1)} %fusion.71) | copy-start | bytes 12582916
  248.8 24.0 %copy-start.31 = (bf16[1024,1024]{1,0:T(8,128)(2,1)S(1)}, bf16[1024,1024]{1,0:T(8,128)(2,1)}, u32[]{:S(2)}) copy-start(bf16[1024,1024]{1,0:T(8,128)(2,1)} %param.26) | copy-start | bytes 6291460
  272.8 6.6 copy-start.34
  279.5 345.8 %all-reduce.14.cloned.1.call-start = ((), (), s32[]{:S(2)}) async-start(), calls=%async_computation.8 | async-start | bytes 16777216 | tf_op jit(solution)/shard_map/psum | solution.py:170
  439.6 10.1 copy-start.2
  439.6 5.2 copy-start.4
  439.6 5.2 copy-start.25
  449.7 2.8 copy-start.32
  452.4 12.7 copy-start.9
  465.1 7.0 copy-start.35
  472.1 153.2 %copy-start.29 = (f32[1024]{0:T(1024)S(1)}, f32[1024]{0:T(1024)}, u32[]{:S(2)}) copy-start(f32[1024]{0:T(1024)} %param.28) | copy-start | bytes 12292
  472.1 361.3 %reduce-scatter.11.cloned.1.call-start = ((), (), s32[]{:S(2)}) async-start(), calls=%async_computation.12 | async-start | bytes 1179648 | tf_op jit(solution)/shard_map/reduce_scatter | solution.py:96
  639.7 7.7 copy-start.3
  639.7 9.7 copy-start.22
  647.4 2.0 copy-start.13
  647.4 12.9 copy-start.6
  666.6 3.9 copy-start.17
  669.2 3.0 copy-start.19
  672.2 1.0 copy-start.18
  673.3 1.0 copy-start.20
  680.5 3.9 copy-start.17
  683.2 3.0 copy-start.19
  686.2 1.0 copy-start.18
  687.2 1.0 copy-start.20
  694.4 3.9 copy-start.17
  697.1 3.0 copy-start.19
  700.1 1.0 copy-start.18
  701.1 1.0 copy-start.20
  708.4 3.9 copy-start.17
  711.1 3.0 copy-start.19
  714.1 1.0 copy-start.18
  715.1 1.0 copy-start.20
  716.2 7.9 copy-start.21
  718.7 1.0 copy-start.10
  724.1 131.1 %reduce-scatter.7.cloned.1.call-start = ((), (), s32[]{:S(2)}) async-start(), calls=%async_computation.10 | async-start | bytes 1179648 | tf_op jit(solution)/shard_map/reduce_scatter | solution.py:94
  729.7 191.7 %reduce-scatter.9.cloned.1.call-start = ((), (), s32[]{:S(2)}) async-start(), calls=%async_computation.11 | async-start | bytes 1179648 | tf_op jit(solution)/shard_map/reduce_scatter | solution.py:95
  732.1 1.0 copy-start.8
  737.5 338.4 %all-reduce.16.cloned.1.call-start = ((), (), s32[]{:S(2)}) async-start(), calls=%async_computation.9 | async-start | bytes 16777216 | tf_op jit(solution)/shard_map/psum | solution.py:207
  737.6 2.7 copy-start.14
  740.3 1.3 copy-start.11
  740.3 1.4 copy-start.23
  746.3 1.2 copy-start.7
  746.3 398.0 %reduce-scatter.13.cloned.1.call-start = ((), (), s32[]{:S(2)}) async-start(), calls=%async_computation.13 | async-start | bytes 1179648 | tf_op jit(solution)/shard_map/reduce_scatter | solution.py:104
  753.1 482.5 %reduce-scatter.15.cloned.1.call-start = ((), (), s32[]{:S(2)}) async-start(), calls=%async_computation.14 | async-start | bytes 4718592 | tf_op jit(solution)/shard_map/reduce_scatter | solution.py:99
  763.3 10.2 copy-start.30
  763.3 31.8 %copy-start.33 = (u32[32]{0:T(128)S(1)}, u32[32]{0:T(128)}, u32[]{:S(2)}) copy-start(u32[32]{0:T(128)} %constant.143) | copy-start | bytes 388
  763.3 33.0 %copy-start.15 = (bf16[1024,256]{1,0:T(8,128)(2,1)S(1)}, bf16[1024,256]{1,0:T(8,128)(2,1)}, u32[]{:S(2)}) copy-start(bf16[1024,256]{1,0:T(8,128)(2,1)} %param.19) | copy-start | bytes 1572868
  763.3 33.0 %copy-start.16 = (bf16[1024,256]{1,0:T(8,128)(2,1)S(1)}, bf16[1024,256]{1,0:T(8,128)(2,1)}, u32[]{:S(2)}) copy-start(bf16[1024,256]{1,0:T(8,128)(2,1)} %param.20) | copy-start | bytes 1572868
  763.4 34.5 %copy-start.26 = (f32[1024]{0:T(1024)S(1)}, f32[1024]{0:T(1024)}, u32[]{:S(2)}) copy-start(f32[1024]{0:T(1024)} %get-tuple-element.218) | copy-start | bytes 12292
  763.4 34.5 %copy-start.27 = (f32[1024]{0:T(1024)S(1)}, f32[1024]{0:T(1024)}, u32[]{:S(2)}) copy-start(f32[1024]{0:T(1024)} %get-tuple-element.223) | copy-start | bytes 12292
  763.4 565.0 %reduce-scatter.17.cloned.1.call-start = ((), (), s32[]{:S(2)}) async-start(), calls=%async_computation.15 | async-start | bytes 4718592 | tf_op jit(solution)/shard_map/reduce_scatter | solution.py:105
Sparse Core Ops, SparseCore 0:
  84.5 155.5 all-reduce.9
  279.6 153.0 all-reduce.11
  472.2 153.0 all-reduce.13
  724.3 64.1 reduce-scatter.10
  792.1 63.0 reduce-scatter.6
  858.4 62.9 reduce-scatter.8
  924.0 151.8 all-reduce.15
  1080.2 63.9 reduce-scatter.12
  1148.5 87.0 reduce-scatter.14
  1240.1 88.2 reduce-scatter.16
where the time goes:
time: 1350 us; the launch traced here: 1340 us
  waiting for transfers between devices  940 us (70%)
  matrix products  175 us (13%)
  other arithmetic  74.3 us (6%)
  local copies, waits for them, and re-layouts  73.9 us (5%)
  blocking collectives  54.6 us (4%)
  between operations  15.8 us (1%)
    psum x2, waiting for transfers between devices, settle(): total = lax.psum(partial_sum, 'tensor')  309 us
    psum x1, waiting for transfers between devices, body(): hidden_sum = lax.psum(hidden_part, 'tensor')  153 us
    psum x1, waiting for transfers between devices, body(): input_sum = lax.psum(input_part, 'tensor')  153 us
    reduce_scatter x1, waiting for transfers between devices, reduce_grads(): lax.psum_scatter(column_terms[1], 'dp', scatter_dimension=1, tiled=True)  92.7 us
    reduce_scatter x1, waiting for transfers between devices, reduce_grads(): lax.psum_scatter(row_terms[5], 'dp', scatter_dimension=0, tiled=True)  91.3 us
    reduce_scatter x1, waiting for transfers between devices, reduce_grads(): lax.psum_scatter(row_terms[1], 'dp', scatter_dimension=0, tiled=True)  64.6 us
    reduce_scatter x1, waiting for transfers between devices, reduce_grads(): lax.psum_scatter(column_terms[0], 'dp', scatter_dimension=1, tiled=True)  56.8 us
    unnamed x1, blocking collectives  33.2 us
  transfers between devices with their start and end apart: 10, of which 9 were waited for; matrix products, arithmetic and copies ran while one was open for 5% of the time, Pallas kernels for 0%

commit v1 on v0

v1 whole, which is shorter than its diff:
```python
import jax
import jax.numpy as jnp
from jax import lax
from jax.experimental import pallas as pl
from jax.experimental.pallas import tpu as pltpu
from jax.sharding import PartitionSpec as P

F32 = jnp.float32
BF16 = jnp.bfloat16
HEAD_DIM = 64
FAR = -1e30
EPS = 1e-06
CLIP = 10.0
SCALE = HEAD_DIM**-0.5
ROOT_HALF = 0.5**0.5
BELL = 0.3989422804014327
MIB = 1 << 20


def dot(left, right, left_dim=1, right_dim=0):
    return lax.dot_general(
        left, right, (((left_dim,), (right_dim,)), ((), ())), preferred_element_type=F32
    )


def normalize(total):
    average = jnp.mean(total, axis=-1, keepdims=True)
    centred = total - average
    variance = jnp.mean(centred * centred, axis=-1, keepdims=True)
    scaled = lax.rsqrt(variance + EPS)
    return centred * scaled, scaled


def norm_back(upstream, normed, scaled, gain):
    weighted = upstream * gain
    first = jnp.mean(weighted, axis=-1, keepdims=True)
    second = jnp.mean(weighted * normed, axis=-1, keepdims=True)
    return scaled * (weighted - first - normed * second)


def head_of(width):
    return lax.broadcasted_iota(jnp.int32, (1, width), 1) // HEAD_DIM


def params(vmem_mib, dims=1):
    return pltpu.CompilerParams(
        vmem_limit_bytes=vmem_mib * MIB,
        dimension_semantics=("arbitrary",) * dims if dims else None,
    )


def cost(flops, bytes_accessed, transcendentals=0):
    return pl.CostEstimate(
        flops=int(flops), bytes_accessed=int(bytes_accessed), transcendentals=int(transcendentals)
    )


def attend_kernel(x_ref, wq_ref, wk_ref, wv_ref, row_ref, col_ref, o_ref, top_ref):
    x = x_ref[0]
    queries = (dot(x, wq_ref[...]).astype(BF16) * SCALE).astype(BF16)
    keys = dot(x, wk_ref[...]).astype(BF16)
    values = dot(x, wv_ref[...]).astype(BF16)
    width = queries.shape[1]
    owner = head_of(width)
    same = col_ref[0][:, 0:1] == row_ref[0][0:1, :]
    total = jnp.zeros(queries.shape, F32)
    zero = jnp.zeros((), BF16)
    for head in range(width // HEAD_DIM):
        mine = owner == head
        scores = dot(jnp.where(mine, queries, zero), keys, 1, 1)
        scores = jnp.where(same, scores, FAR)
        top = jnp.max(scores, axis=-1, keepdims=True)
        raised = jnp.exp(scores - top)
        chances = raised * (1.0 / jnp.sum(raised, axis=-1, keepdims=True))
        total = total + dot(chances.astype(BF16), jnp.where(mine, values, zero))
        top_ref[head : head + 1, :] = jnp.broadcast_to(
            jnp.max(top, axis=0, keepdims=True), (1, top_ref.shape[1])
        )
    o_ref[...] = total.astype(BF16).astype(F32)


def attend(s, block_input, wq, wk, wv, seg_row, seg_col):
    _, length, depth = block_input.shape
    width = wq.shape[1]
    heads = width // HEAD_DIM
    return pl.pallas_call(
        attend_kernel,
        grid=(1,),
        in_specs=[
            pl.BlockSpec((1, length, depth), lambda i: (s, 0, 0)),
            pl.BlockSpec((depth, width), lambda i: (0, 0)),
            pl.BlockSpec((depth, width), lambda i: (0, 0)),
            pl.BlockSpec((depth, width), lambda i: (0, 0)),
            pl.BlockSpec((1, 8, length), lambda i: (s, 0, 0)),
            pl.BlockSpec((1, length, 128), lambda i: (s, 0, 0)),
        ],
        out_specs=[
            pl.BlockSpec((length, width), lambda i: (0, 0)),
            pl.BlockSpec((heads, 128), lambda i: (0, 0)),
        ],
        out_shape=[
            jax.ShapeDtypeStruct((length, width), F32),
            jax.ShapeDtypeStruct((heads, 128), F32),
        ],
        compiler_params=params(32),
        cost_estimate=cost(
            2 * length * depth * 3 * width + 4 * length * length * width,
            2 * length * depth + 6 * depth * width,
            heads * length * length,
        ),
        name="attend",
    )(block_input, wq, wk, wv, seg_row, seg_col)


def widen_kernel(where_ref, wq_ref, wk_ref, wv_ref, wo_ref, slice_ref, out_ref):
    width = wq_ref.shape[1]
    for index, ref in enumerate((wq_ref, wk_ref, wv_ref)):
        slice_ref[:, index * width : (index + 1) * width] = ref[...].astype(F32)
    out_ref[...] = wo_ref[...].astype(F32)


def widen(where, wq, wk, wv, wo, part):
    width = wq.shape[1]
    rows = pl.BlockSpec((part, width), lambda i, w: (w[3], 0))
    whole = lambda i, w: (0, 0)
    return pl.pallas_call(
        widen_kernel,
        grid_spec=pltpu.PrefetchScalarGridSpec(
            num_scalar_prefetch=1,
            grid=(1,),
            in_specs=[rows, rows, rows, pl.BlockSpec(wo.shape, whole)],
            out_specs=[pl.BlockSpec((part, 3 * width), whole), pl.BlockSpec(wo.shape, whole)],
        ),
        out_shape=[
            jax.ShapeDtypeStruct((part, 3 * width), F32),
            jax.ShapeDtypeStruct(wo.shape, F32),
        ],
        compiler_params=params(16),
        cost_estimate=cost(0, 6 * wo.size + 18 * part * width),
        name="widen",
    )(where, wq, wk, wv, wo)


def pair_kernel(where_ref, wq_ref, wk_ref, wv_ref, wo_ref, others_ref, far_ref, *out_refs):
    index = pl.program_id(0)
    width = wq_ref.shape[1]
    mine = index == where_ref[2]
    for place, (own, out) in enumerate(zip((wq_ref, wk_ref, wv_ref), out_refs)):
        other = others_ref[:, place * width : (place + 1) * width].astype(BF16)
        out[...] = jnp.where(mine, own[...], other)
    out_refs[3][...] = jnp.where(mine, wo_ref[...], far_ref[...].astype(BF16))


def pair(where, wq, wk, wv, wo, others, far):
    depth, width = wq.shape
    whole = lambda i, w: (0, 0)
    column = pl.BlockSpec((depth, width), lambda i, w: (0, i))
    return pl.pallas_call(
        pair_kernel,
        grid_spec=pltpu.PrefetchScalarGridSpec(
            num_scalar_prefetch=1,
            grid=(2,),
            in_specs=[pl.BlockSpec(a.shape, whole) for a in (wq, wk, wv, wo, others, far)],
            out_specs=[column, column, column, pl.BlockSpec(wo.shape, lambda i, w: (i, 0))],
        ),
        out_shape=[jax.ShapeDtypeStruct((depth, 2 * width), BF16)] * 3
        + [jax.ShapeDtypeStruct((2 * wo.shape[0], wo.shape[1]), BF16)],
        compiler_params=params(32),
        cost_estimate=cost(0, 32 * depth * width),
        name="pair",
    )(where, wq, wk, wv, wo, others, far)


def finish_kernel(where_ref, own_ref, near_ref, *rest):
    out_ref = rest[-1]
    mine = pl.program_id(0) == where_ref[1]
    out_ref[0] = jnp.where(mine, own_ref[...], near_ref[...]).astype(BF16)


def finish(s, count, where, own, near, input_grad):
    half, depth = own.shape
    whole = pl.BlockSpec((half, depth), lambda i, w: (0, 0))
    carried = [] if input_grad is None else [input_grad]
    return pl.pallas_call(
        finish_kernel,
        grid_spec=pltpu.PrefetchScalarGridSpec(
            num_scalar_prefetch=1,
            grid=(2,),
            in_specs=[whole, whole, *[pl.BlockSpec(memory_space=pl.ANY)] * len(carried)],
            out_specs=pl.BlockSpec((1, half, depth), lambda i, w: (s, i, 0)),
        ),
        out_shape=jax.ShapeDtypeStruct((count, 2 * half, depth), BF16),
        input_output_aliases={3: 0} if carried else {},
        compiler_params=params(16),
        cost_estimate=cost(0, 12 * half * depth),
        name="finish",
    )(where, own, near, *carried)


def assemble_kernel(where_ref, own_ref, far_ref, near_ref, both_ref, out_ref):
    place = pl.program_id(0) ^ where_ref[0]

    @pl.when(place == 0)
    def _():
        out_ref[...] = own_ref[...].astype(BF16)

    @pl.when(place == 2)
    def _():
        out_ref[...] = far_ref[...].astype(BF16)

    @pl.when(place == 1)
    def _():
        out_ref[...] = near_ref[...].astype(BF16)

    @pl.when(place == 3)
    def _():
        out_ref[...] = both_ref[...].astype(BF16)


def assemble(where, own, far, near, both):
    rows, columns = own.shape
    whole = lambda i, w: (0, 0)
    return pl.pallas_call(
        assemble_kernel,
        grid_spec=pltpu.PrefetchScalarGridSpec(
            num_scalar_prefetch=1,
            grid=(4,),
            in_specs=[pl.BlockSpec((rows, columns), whole)] * 4,
            out_specs=pl.BlockSpec((rows, columns), lambda i, w: (i, 0)),
        ),
        out_shape=jax.ShapeDtypeStruct((4 * rows, columns), BF16),
        compiler_params=params(24),
        cost_estimate=cost(0, 20 * rows * columns),
        name="assemble",
    )(where, own, far, near, both)


def forward_kernel(
    where_ref, x_ref, own_ref, near_ref, far_ref, both_ref, wo_ref, gain_ref, shift_ref,
    up_ref, down_ref,
    normed_ref, scaled_ref, low_ref, active_ref, pull_ref, send_ref, keep_ref,
    mixed_ref,
):
    step = pl.program_id(0)
    me = where_ref[0]
    width = own_ref.shape[1]
    for flip, piece in enumerate((own_ref, near_ref, far_ref, both_ref)):
        start = pl.multiple_of((me ^ flip) * width, width)
        mixed_ref[:, pl.ds(start, width)] = piece[...].astype(BF16)
    branch = dot(mixed_ref[...], wo_ref[...])
    normed, scaled = normalize(x_ref[0].astype(F32) + branch)
    normed_ref[...] = normed
    scaled_ref[...] = jnp.broadcast_to(scaled, scaled_ref.shape)
    low = (normed * gain_ref[...] + shift_ref[...]).astype(BF16)
    low_ref[...] = low
    before = dot(low, up_ref[...])
    chance = 0.5 * (1.0 + lax.erf(before * ROOT_HALF))
    active = (before * chance).astype(BF16)
    active_ref[...] = active
    pull_ref[...] = chance + before * (jnp.exp(-0.5 * before * before) * BELL)
    part = dot(active, down_ref[...])

    @pl.when(step == 0)
    def _():
        send_ref[...] = part

    @pl.when(step == 1)
    def _():
        keep_ref[...] = part


def half_of(step, where):
    return (1 - where[1] + step) % 2


def forward(s, where, block_input, pieces, wo, gain, shift, up, down):
    _, length, depth = block_input.shape
    width = pieces[0].shape[1]
    hidden = up.shape[1]
    half = length // 2
    rows = lambda i, w: (half_of(i, w), 0)
    whole = lambda i, w: (0, 0)
    return pl.pallas_call(
        forward_kernel,
        grid_spec=pltpu.PrefetchScalarGridSpec(
            num_scalar_prefetch=1,
            grid=(2,),
            in_specs=[
                pl.BlockSpec((1, half, depth), lambda i, w: (s, half_of(i, w), 0)),
                *[pl.BlockSpec((half, width), rows)] * 4,
                pl.BlockSpec((4 * width, depth), whole),
                pl.BlockSpec((1, depth), whole),
                pl.BlockSpec((1, depth), whole),
                pl.BlockSpec((depth, hidden), whole),
                pl.BlockSpec((hidden, depth), whole),
            ],
            out_specs=[
                pl.BlockSpec((half, depth), rows),
                pl.BlockSpec((half, 128), rows),
                pl.BlockSpec((half, depth), rows),
                pl.BlockSpec((half, hidden), rows),
                pl.BlockSpec((half, hidden), rows),
                pl.BlockSpec((half, depth), whole),
                pl.BlockSpec((half, depth), whole),
            ],
            scratch_shapes=[pltpu.VMEM((half, 4 * width), BF16)],
        ),
        out_shape=[
            jax.ShapeDtypeStruct((length, depth), F32),
            jax.ShapeDtypeStruct((length, 128), F32),
            jax.ShapeDtypeStruct((length, depth), BF16),
            jax.ShapeDtypeStruct((length, hidden), BF16),
            jax.ShapeDtypeStruct((length, hidden), F32),
            jax.ShapeDtypeStruct((half, depth), F32),
            jax.ShapeDtypeStruct((half, depth), F32),
        ],
        compiler_params=params(40),
        cost_estimate=cost(
            2 * length * depth * (4 * width + 2 * hidden),
            2 * depth * (4 * width + 2 * hidden) + 20 * length * depth,
            2 * length * hidden,
        ),
        name="forward",
    )(where, block_input, *pieces, wo, gain, shift, up, down)


def backward_kernel(
    where_ref, normed_ref, gain_ref, shift_ref, own_ref, near_ref, grad_ref, second_gain_ref,
    second_shift_ref, pull_ref, up_ref, down_ref, *rest,
):
    out_ref, slope_ref, slope_low_ref, before_ref, send_ref, keep_ref, sums_ref = rest[-7:]
    step = pl.program_id(0)
    total = jnp.where(step == 0, near_ref[...], own_ref[...])
    hidden = normed_ref[...] * gain_ref[...] + shift_ref[...]
    normed, scaled = normalize(hidden + total)
    out_ref[0] = (normed * second_gain_ref[...] + second_shift_ref[...]).astype(BF16)
    upstream = grad_ref[0].astype(F32)
    gain_part = jnp.sum(upstream * normed, axis=0, keepdims=True)
    shift_part = jnp.sum(upstream, axis=0, keepdims=True)

    @pl.when(step == 0)
    def _():
        sums_ref[...] = jnp.zeros_like(sums_ref)

    sums_ref[0:1, :] += gain_part
    sums_ref[1:2, :] += shift_part
    slope = norm_back(upstream, normed, scaled, second_gain_ref[...])
    slope_ref[...] = slope
    low = slope.astype(BF16)
    slope_low_ref[...] = low
    before = (dot(low, down_ref[...], 1, 1) * pull_ref[...]).astype(BF16)
    before_ref[...] = before
    part = dot(before, up_ref[...], 1, 1)

    @pl.when(step == 0)
    def _():
        send_ref[...] = part

    @pl.when(step == 1)
    def _():
        keep_ref[...] = part


def backward(
    s, where, normed, gain, shift, own, near, out_grad, second_gain, second_shift, pull, up, down,
    layer_out,
):
    count, length, depth = out_grad.shape
    hidden = up.shape[1]
    half = length // 2
    rows = lambda i, w: (half_of(i, w), 0)
    whole = lambda i, w: (0, 0)
    block = lambda i, w: (s, half_of(i, w), 0)
    vector = pl.BlockSpec((1, depth), whole)
    carried = [] if layer_out is None else [layer_out]
    return pl.pallas_call(
        backward_kernel,
        grid_spec=pltpu.PrefetchScalarGridSpec(
            num_scalar_prefetch=1,
            grid=(2,),
            in_specs=[
                pl.BlockSpec((half, depth), rows),
                vector,
                vector,
                pl.BlockSpec((half, depth), whole),
                pl.BlockSpec((half, depth), whole),
                pl.BlockSpec((1, half, depth), block),
                vector,
                vector,
                pl.BlockSpec((half, hidden), rows),
                pl.BlockSpec((depth, hidden), whole),
                pl.BlockSpec((hidden, depth), whole),
                *[pl.BlockSpec(memory_space=pl.ANY)] * len(carried),
            ],
            out_specs=[
                pl.BlockSpec((1, half, depth), block),
                pl.BlockSpec((half, depth), rows),
                pl.BlockSpec((half, depth), rows),
                pl.BlockSpec((half, hidden), rows),
                pl.BlockSpec((half, depth), whole),
                pl.BlockSpec((half, depth), whole),
                pl.BlockSpec((8, depth), whole),
            ],
        ),
        out_shape=[
            jax.ShapeDtypeStruct((count, length, depth), BF16),
            jax.ShapeDtypeStruct((length, depth), F32),
            jax.ShapeDtypeStruct((length, depth), BF16),
            jax.ShapeDtypeStruct((length, hidden), BF16),
            jax.ShapeDtypeStruct((half, depth), F32),
            jax.ShapeDtypeStruct((half, depth), F32),
            jax.ShapeDtypeStruct((8, depth), F32),
        ],
        input_output_aliases={12: 0} if carried else {},
        compiler_params=params(40),
        cost_estimate=cost(4 * length * depth * hidden, 4 * depth * hidden + 22 * length * depth),
        name="backward",
    )(
        where, normed, gain, shift, own, near, out_grad, second_gain, second_shift, pull, up, down,
        *carried,
    )


def products_kernel(*refs):
    *terms, out_ref = refs
    count = len(terms) // 2
    total = dot(terms[0][...], terms[count][...], 0, 0)
    for left, right in zip(terms[1:count], terms[count + 1 :]):
        total = total + dot(left[...], right[...], 0, 0)
    out_ref[...] = total


def products(lefts, rights, tile=256):
    length, depth = lefts[0].shape
    width = rights[0].shape[1]
    count = len(lefts)
    return pl.pallas_call(
        products_kernel,
        grid=(depth // tile,),
        in_specs=[pl.BlockSpec((length, tile), lambda i: (0, i))] * count
        + [pl.BlockSpec((length, width), lambda i: (0, 0))] * count,
        out_specs=pl.BlockSpec((tile, width), lambda i: (i, 0)),
        out_shape=jax.ShapeDtypeStruct((depth, width), F32),
        compiler_params=params(32),
        cost_estimate=cost(
            2 * count * length * depth * width,
            2 * count * length * (depth + width) + 4 * depth * width,
        ),
        name="products",
    )(*lefts, *rights)


def project_kernel(x_ref, wq_ref, wk_ref, wv_ref, q_ref, k_ref, v_ref):
    x = x_ref[0]
    q_ref[0] = (dot(x, wq_ref[...]).astype(BF16) * SCALE).astype(BF16)
    k_ref[0] = dot(x, wk_ref[...]).astype(BF16)
    v_ref[0] = dot(x, wv_ref[...]).astype(BF16)


def project(block_input, wq, wk, wv):
    count, length, depth = block_input.shape
    width = wq.shape[1]
    weight = pl.BlockSpec((depth, width), lambda s: (0, 0))
    out = pl.BlockSpec((1, length, width), lambda s: (s, 0, 0))
    return pl.pallas_call(
        project_kernel,
        grid=(count,),
        in_specs=[pl.BlockSpec((1, length, depth), lambda s: (s, 0, 0)), weight, weight, weight],
        out_specs=[out] * 3,
        out_shape=[jax.ShapeDtypeStruct((count, length, width), BF16)] * 3,
        compiler_params=params(32),
        cost_estimate=cost(
            6 * count * length * depth * width, 2 * count * length * (depth + 3 * width)
        ),
        name="project",
    )(block_input, wq, wk, wv)


def first_kernel(
    where_ref, own_ref, near_ref, slope_ref, normed_ref, scaled_ref, gain_ref, wo_ref,
    one_ref, low_ref, mixed_ref, sums_ref,
):
    step = pl.program_id(0)
    total = jnp.where(step == 0, near_ref[...], own_ref[...])
    upstream = slope_ref[...] + total
    normed = normed_ref[...]

    @pl.when(step == 0)
    def _():
        sums_ref[...] = jnp.zeros_like(sums_ref)

    sums_ref[0:1, :] += jnp.sum(upstream * normed, axis=0, keepdims=True)
    sums_ref[1:2, :] += jnp.sum(upstream, axis=0, keepdims=True)
    slope = norm_back(upstream, normed, scaled_ref[:, 0:1], gain_ref[...])
    low = slope.astype(BF16)
    low_ref[...] = low
    mixed_ref[...] = dot(low, wo_ref[...], 1, 1).astype(BF16)

    @pl.when(step == 1)
    def _():
        one_ref[...] = slope


def first(where, own, near, slope, normed, scaled, gain, wo):
    length, depth = slope.shape
    width = wo.shape[0]
    half = length // 2
    rows = lambda i, w: (half_of(i, w), 0)
    whole = lambda i, w: (0, 0)
    return pl.pallas_call(
        first_kernel,
        grid_spec=pltpu.PrefetchScalarGridSpec(
            num_scalar_prefetch=1,
            grid=(2,),
            in_specs=[
                pl.BlockSpec((half, depth), whole),
                pl.BlockSpec((half, depth), whole),
                pl.BlockSpec((half, depth), rows),
                pl.BlockSpec((half, depth), rows),
                pl.BlockSpec((half, 128), rows),
                pl.BlockSpec((1, depth), whole),
                pl.BlockSpec((width, depth), whole),
            ],
            out_specs=[
                pl.BlockSpec((half, depth), whole),
                pl.BlockSpec((half, depth), rows),
                pl.BlockSpec((half, width), rows),
                pl.BlockSpec((8, depth), whole),
            ],
        ),
        out_shape=[
            jax.ShapeDtypeStruct((half, depth), F32),
            jax.ShapeDtypeStruct((length, depth), BF16),
            jax.ShapeDtypeStruct((length, width), BF16),
            jax.ShapeDtypeStruct((8, depth), F32),
        ],
        compiler_params=params(32),
        cost_estimate=cost(2 * length * depth * width, 18 * length * depth),
        name="first",
    )(where, own, near, slope, normed, scaled, gain, wo)


def attend_back_kernel(
    where_ref, q_ref, k_ref, v_ref, go_ref, row_ref, col_ref, wq_ref, wk_ref, wv_ref, one_ref,
    gq_ref, gk_ref, gv_ref, send_ref, keep_ref,
    key_slope, value_slope, part_ref,
):
    group = pl.program_id(0)
    queries, keys, values, upstream = q_ref[0], k_ref[0], v_ref[0], go_ref[...]
    width = queries.shape[1]
    half = queries.shape[0] // 2
    owner = head_of(width)
    same = col_ref[0][:, 0:1] == row_ref[0][0:1, :]
    zero = jnp.zeros((), BF16)
    queries_t = queries.T
    upstream_t = upstream.T
    query_slope = jnp.zeros(queries.shape, F32)
    for head in range(width // HEAD_DIM):
        mine = owner == head
        place = slice(head * HEAD_DIM, (head + 1) * HEAD_DIM)
        scores = dot(jnp.where(mine, queries, zero), keys, 1, 1)
        scores = jnp.where(same, scores, FAR)
        top = jnp.max(scores, axis=-1, keepdims=True)
        raised = jnp.exp(scores - top)
        chances = raised * (1.0 / jnp.sum(raised, axis=-1, keepdims=True))
        drift = dot(jnp.where(mine, upstream, zero), values, 1, 1)
        slopes = chances * (drift - jnp.sum(drift * chances, axis=-1, keepdims=True))
        slopes = slopes.astype(BF16)
        query_slope = query_slope + dot(slopes, jnp.where(mine, keys, zero))
        key_slope[place, :] = dot(queries_t[place, :], slopes)
        value_slope[place, :] = dot(upstream_t[place, :], chances.astype(BF16))
    gq = (query_slope * SCALE).astype(BF16)
    gk = key_slope[...].T.astype(BF16)
    gv = value_slope[...].T.astype(BF16)
    gq_ref[...] = gq
    gk_ref[...] = gk
    gv_ref[...] = gv
    part = dot(gq, wq_ref[...], 1, 1) + dot(gk, wk_ref[...], 1, 1) + dot(gv, wv_ref[...], 1, 1)

    @pl.when(group == 0)
    def _():
        part_ref[...] = part

    @pl.when(group == 1)
    def _():
        part_ref[...] += part
        core = where_ref[1]
        kept = pl.multiple_of(core * half, half)
        sent = pl.multiple_of((1 - core) * half, half)
        keep_ref[...] = part_ref[pl.ds(kept, half), :] + one_ref[...]
        send_ref[...] = part_ref[pl.ds(sent, half), :]


def attend_back(s, where, q, k, v, mixed_slope, seg_row, seg_col, wq, wk, wv, one):
    _, length, both = q.shape
    depth = wq.shape[0]
    width = both // 2
    half = length // 2
    piece = pl.BlockSpec((1, length, width), lambda g, w: (s, 0, g))
    flat = pl.BlockSpec((length, width), lambda g, w: (0, g))
    weight = pl.BlockSpec((depth, width), lambda g, w: (0, g))
    whole = lambda g, w: (0, 0)
    return pl.pallas_call(
        attend_back_kernel,
        grid_spec=pltpu.PrefetchScalarGridSpec(
            num_scalar_prefetch=1,
            grid=(2,),
            in_specs=[
                piece,
                piece,
                piece,
                flat,
                pl.BlockSpec((1, 8, length), lambda g, w: (s, 0, 0)),
                pl.BlockSpec((1, length, 128), lambda g, w: (s, 0, 0)),
                weight,
                weight,
                weight,
                pl.BlockSpec((half, depth), whole),
            ],
            out_specs=[
                flat,
                flat,
                flat,
                pl.BlockSpec((half, depth), whole),
                pl.BlockSpec((half, depth), whole),
            ],
            scratch_shapes=[
                pltpu.VMEM((width, length), F32),
                pltpu.VMEM((width, length), F32),
                pltpu.VMEM((length, depth), F32),
            ],
        ),
        out_shape=[
            jax.ShapeDtypeStruct((length, both), BF16),
            jax.ShapeDtypeStruct((length, both), BF16),
            jax.ShapeDtypeStruct((length, both), BF16),
            jax.ShapeDtypeStruct((half, depth), F32),
            jax.ShapeDtypeStruct((half, depth), F32),
        ],
        compiler_params=params(40),
        cost_estimate=cost(
            10 * length * length * both + 6 * length * depth * both,
            6 * depth * both + 12 * length * depth,
            length * length * both // HEAD_DIM,
        ),
        name="attend_back",
    )(where, q, k, v, mixed_slope, seg_row, seg_col, wq, wk, wv, one)


def head_products_kernel(where_ref, *refs):
    *terms, out_ref = refs
    count = len(terms) // 2
    total = dot(terms[0][0], terms[count][...], 0, 0)
    for left, right in zip(terms[1:count], terms[count + 1 :]):
        total = total + dot(left[0], right[...], 0, 0)
    out_ref[...] = total


def head_products(where, block_input, rights, tile=256):
    count, length, depth = block_input.shape
    width = rights[0].shape[1] // 2
    return pl.pallas_call(
        head_products_kernel,
        grid_spec=pltpu.PrefetchScalarGridSpec(
            num_scalar_prefetch=1,
            grid=(depth // tile,),
            in_specs=[
                pl.BlockSpec((1, length, tile), lambda i, w, s=s: (s, 0, i)) for s in range(count)
            ]
            + [pl.BlockSpec((length, width), lambda i, w: (0, w[2]))] * count,
            out_specs=pl.BlockSpec((tile, width), lambda i, w: (i, 0)),
        ),
        out_shape=jax.ShapeDtypeStruct((depth, width), F32),
        compiler_params=params(32),
        cost_estimate=cost(
            2 * count * length * depth * width,
            2 * count * length * (depth + width) + 4 * depth * width,
        ),
        name="head_products",
    )(where, *[block_input] * count, *rights)


def solution(mesh):
    ranks = mesh.shape["dp"]
    group = mesh.shape["tensor"]
    assert group == 4
    near_pairs = [(t, t ^ 1) for t in range(group)]
    far_pairs = [(t, t ^ 2) for t in range(group)]

    def near(value):
        return lax.ppermute(value, "tensor", near_pairs)

    def far(value):
        return lax.ppermute(value, "tensor", far_pairs)

    def gather_pieces(own):
        beside = near(own)
        across = far(own)
        return own, beside, across, near(across)

    def sum_halves(send, keep):
        chip = keep + near(send)
        total = chip + far(chip)
        return total, near(total)

    def scatter(value):
        return lax.psum_scatter(value, "dp", scatter_dimension=0, tiled=True)

    def body(
        block_input, segment_ids, query_weight, key_weight, value_weight, output_weight,
        first_gain, first_shift, up_weight, down_weight, second_gain, second_shift, out_grad,
    ):
        count, length, depth = block_input.shape
        width = query_weight.shape[1]
        me = lax.axis_index("tensor")
        rank = lax.axis_index("dp")
        core = me % 2
        chip = me // 2
        where = jnp.stack([me, core, chip, rank]).astype(jnp.int32)
        seg_row = jnp.broadcast_to(segment_ids[:, None, :], (count, 8, length))
        seg_col = jnp.broadcast_to(segment_ids[:, :, None], (count, length, 128))
        gain_one, shift_one = first_gain[None], first_shift[None]
        gain_two, shift_two = second_gain[None], second_shift[None]

        part = depth // ranks
        slices, wo_wide = widen(
            where, query_weight, key_weight, value_weight, output_weight, part
        )
        wo_own, wo_near, wo_far, wo_both = gather_pieces(wo_wide)
        wo = assemble(where, wo_own, wo_far, wo_near, wo_both)

        others = lax.all_gather(far(slices), "dp", axis=0, tiled=True)
        wq, wk, wv, wo_pair = pair(
            where, query_weight, key_weight, value_weight, output_weight, others, wo_far
        )

        tops, mixed, kept, sums = [], [], [], []
        for s in range(count):
            own, top = attend(
                s, block_input, query_weight, key_weight, value_weight, seg_row, seg_col
            )
            tops.append(top)
            mixed.append(own)
            pieces = gather_pieces(own)
            normed, scaled, low, active, pull, send, keep = forward(
                s, where, block_input, pieces, wo, gain_one, shift_one, up_weight, down_weight
            )
            kept.append((normed, scaled, low, active, pull))
            sums.append(sum_halves(send, keep))

        layer_out = None
        slopes, slope_lows, befores, hidden_sums, second_sums = [], [], [], [], []
        for s in range(count):
            normed, scaled, low, active, pull = kept[s]
            layer_out, slope, slope_low, before, send, keep, second = backward(
                s, where, normed, gain_one, shift_one, *sums[s], out_grad, gain_two, shift_two,
                pull, up_weight, down_weight, layer_out,
            )
            slopes.append(slope)
            slope_lows.append(slope_low)
            befores.append(before)
            second_sums.append(second)
            hidden_sums.append(sum_halves(send, keep))

        up_part = products([k[2] for k in kept], befores)
        down_part = products(slope_lows, [k[3] for k in kept])
        up_grad = scatter(up_part)
        down_grad = scatter(down_part).T

        q, k, v = project(block_input, wq, wk, wv)
        input_grad = None
        ones, gqs, gks, gvs, first_sums = [], [], [], [], []
        for s in range(count):
            normed, scaled = kept[s][:2]
            one, one_low, mixed_slope, first_sum = first(
                where, *hidden_sums[s], slopes[s], normed, scaled, gain_one, wo_pair
            )
            ones.append(one_low)
            first_sums.append(first_sum)
            gq, gk, gv, send, keep = attend_back(
                s, where, q, k, v, mixed_slope, seg_row, seg_col, wq, wk, wv, one
            )
            gqs.append(gq)
            gks.append(gk)
            gvs.append(gv)
            mine = keep + near(send)
            input_grad = finish(s, count, where, mine, near(mine), input_grad)

        output_part = products(ones, [m.astype(BF16) for m in mixed])
        query_part = head_products(where, block_input, gqs)
        key_part = head_products(where, block_input, gks)
        value_part = head_products(where, block_input, gvs)
        output_grad = scatter(output_part).T
        query_grad = scatter(query_part)
        key_grad = scatter(key_part)
        value_grad = scatter(value_part)

        gains = jnp.concatenate(
            [sum(x[0:2] for x in first_sums), sum(x[0:2] for x in second_sums)], axis=0
        )
        gains = lax.all_gather(gains, "dp", axis=0, tiled=False)
        gains = jnp.sum(
            lax.dynamic_slice_in_dim(gains, rank * part, part, 2), axis=0
        )
        peak = jnp.max(jnp.stack([t[:, 0] for t in tops]), axis=0)
        peak = jnp.max(lax.all_gather(peak, "dp", axis=0, tiled=False), axis=0)
        factor = jnp.sqrt(CLIP / jnp.maximum(peak, CLIP))
        column_factor = jnp.repeat(factor, HEAD_DIM)
        query_clipped = query_weight.astype(F32) * column_factor[None, :]
        key_clipped = key_weight.astype(F32) * column_factor[None, :]
        return (
            layer_out, input_grad, query_grad, key_grad, value_grad, output_grad,
            gains[0], gains[1], up_grad, down_grad, gains[2], gains[3],
            query_clipped, key_clipped,
        )

    batch = P("dp", None, None)
    in_specs = (
        batch, P("dp", None), P(None, "tensor"), P(None, "tensor"), P(None, "tensor"),
        P("tensor", None), P(), P(), P(None, "tensor"), P("tensor", None), P(), P(), batch,
    )
    out_specs = (
        batch, batch, P("dp", "tensor"), P("dp", "tensor"), P("dp", "tensor"), P("tensor", "dp"),
        P("dp"), P("dp"), P("dp", "tensor"), P("tensor", "dp"), P("dp"), P("dp"),
        P(None, "tensor"), P(None, "tensor"),
    )
    return jax.shard_map(body, mesh=mesh, in_specs=in_specs, out_specs=out_specs, check_vma=False)
```

time: 1350 us -> 886 us (0.66)
  waiting for transfers between devices: 940 us -> 446 us
  Pallas kernels: 0 us -> 196 us
  matrix products: 175 us -> 0 us
  other arithmetic: 74.3 us -> 32.5 us
  local copies, waits for them, and re-layouts: 73.9 us -> 105 us
  starting transfers between devices: 0.67 us -> 26.1 us
    psum x4 -> x0, waiting for transfers between devices: 615 us -> none  [the longest x2 309 us: settle(): total = lax.psum(partial_sum, 'tensor')]
    ppermute x0 -> x48, waiting for transfers between devices: none -> 208 us  [the longest x14 208 us: far(): return lax.ppermute(value, 'tensor', far_pairs)]
    pallas_call x0 -> x34, Pallas kernels: none -> 196 us  [the longest x4 48.6 us: attend_back(): pl.pallas_call(attend_back_kernel, grid_spec=pltpu.PrefetchScalarGridSpec...]
    dot_general x46 -> x0, matrix products: 175 us -> none  [the longest x1 24 us: body(): before = jnp.dot(hidden_low, up_weight, preferred_element_type=jnp.float32)]
    reduce_scatter x6, waiting for transfers between devices: 326 us -> 237 us  [scatter(): return lax.psum_scatter(value, 'dp', scatter_dimension=0, tiled=True)]
    unnamed x76 -> x341, local copies, waits for them, and re-layouts: 18.2 us -> 104 us
    reduce_sum x6 -> x1, other arithmetic: 34.2 us -> 0.02 us  [body(): jnp.sum(lax.dynamic_slice_in_dim(gains, rank * part, part, 2), axis=0)]
    all_gather x0 -> x1, blocking collectives: none -> 30.6 us  [body(): gains = lax.all_gather(gains, 'dp', axis=0, tiled=False)]
  transfers between devices with their start and end apart: 10 -> 55, of which waited for: 9 -> 17; matrix products, arithmetic and copies ran while one was open for 5% -> 4% of each run, Pallas kernels for 0% -> 21%
where the time goes in v1:
time: 886 us; the launch traced here: 875 us
  waiting for transfers between devices  446 us (50%)
  Pallas kernels  196 us (22%)
  local copies, waits for them, and re-layouts  105 us (12%)
  blocking collectives  53.1 us (6%)
  other arithmetic  32.5 us (4%)
  starting transfers between devices  26.1 us (3%)
  between operations  16.3 us (2%)
    reduce_scatter x6, waiting for transfers between devices, scatter(): return lax.psum_scatter(value, 'dp', scatter_dimension=0, tiled=True)  237 us
    ppermute x14, waiting for transfers between devices, far(): return lax.ppermute(value, 'tensor', far_pairs)  208 us
    unnamed x341, local copies, waits for them, and re-layouts  104 us
    pallas_call x4, Pallas kernels, attend_back(): pl.pallas_call(attend_back_kernel, grid_spec=pltpu.PrefetchScalarGridSpec...  48.6 us
    pallas_call x4, Pallas kernels, forward(): pl.pallas_call(forward_kernel, grid_spec=pltpu.PrefetchScalarGridSpec(num...  35.4 us
    pallas_call x4, Pallas kernels, backward(): pl.pallas_call(backward_kernel, grid_spec=pltpu.PrefetchScalarGridSpec(nu...  34.6 us
    all_gather x1, blocking collectives, body(): gains = lax.all_gather(gains, 'dp', axis=0, tiled=False)  30.6 us
    unnamed x1, blocking collectives  22.5 us
  transfers between devices with their start and end apart: 55, of which 17 were waited for; matrix products, arithmetic and copies ran while one was open for 4% of the time, Pallas kernels for 21%

profile of v1, /device:TPU:0, one launch (start us, length us, event | category | flops | bytes accessed | tf_op | source)
XLA Modules:
  0.0 874.6 jit_solution(2615403623618257441)
XLA Ops:
  12.2 3.0 collective-permute-start.3
  15.2 23.2 %collective-permute-done.3.far_ref = f32[256,1024]{1,0:T(8,128)S(1)} collective-permute-done((f32[256,1024]{1,0:T(8,128)S(1)}, f32[256,1024]{1,0:T(8,128)S(1)}, u32[]{:S(2)}, u32[]{:S(2)}) %collective-permute-start.3) | collective-permute-done | bytes 1048608 | tf_op jit(solution)/shard_map/ppermute | solution.py:694
  38.7 2.2 copy-done
  40.9 3.2 attend.7
  44.2 1.8 collective-permute-start.22
  46.2 3.2 attend.6
  49.8 3.2 attend.5
  53.7 5.3 collective-permute-done.22.far_ref
  60.7 3.6 attend.4
  64.3 5.9 collective-permute-done.16.far_ref
  70.2 1.8 collective-permute-start.1
  73.1 8.3 collective-permute-done.10.far_ref
  81.9 8.4 forward.7
  94.9 8.4 forward.6
  107.5 9.3 %forward.5 = (f32[512,1024]{1,0:T(8,128)S(1)}, f32[512,128]{1,0:T(8,128)S(1)}, bf16[512,1024]{1,0:T(8,128)(2,1)S(1)}, bf16[512,1024]{1,0:T(8,128)(2,1)S(1)}, f32...) custom-call(s32[4]{0:T(128)S(1)} %pad_add_fusion.where_ref, bf16[4,512,1024]{2,1,0:T(8,128)(2,1)} %refs_3_.5, ...), custom_call_target="tpu_custom_call" | custom-call | flops 3221225472 | bytes 16777216 | tf_op jit(solution)/shard_map/forward/pallas_call | solution.py:283
  122.6 9.3 %forward.4 = (f32[512,1024]{1,0:T(8,128)S(1)}, f32[512,128]{1,0:T(8,128)S(1)}, bf16[512,1024]{1,0:T(8,128)(2,1)S(1)}, bf16[512,1024]{1,0:T(8,128)(2,1)S(1)}, f32...) custom-call(s32[4]{0:T(128)S(1)} %pad_add_fusion.where_ref, bf16[4,512,1024]{2,1,0:T(8,128)(2,1)} %refs_3_.5, ...), custom_call_target="tpu_custom_call" | custom-call | flops 3221225472 | bytes 16777216 | tf_op jit(solution)/shard_map/forward/pallas_call | solution.py:283
  136.2 2.4 add.105
  139.7 2.4 add.103
  143.1 3.3 collective-permute-done.27
  147.3 1.8 add.101
  149.1 1.8 collective-permute-start.13
  152.6 16.4 %collective-permute-done.25 = f32[256,1024]{1,0:T(8,128)} collective-permute-done((f32[256,1024]{1,0:T(8,128)}, f32[256,1024]{1,0:T(8,128)}, u32[]{:S(2)}, u32[]{:S(2)}) %collective-permute-start.25) | collective-permute-done | bytes 1048608 | tf_op jit(solution)/shard_map/ppermute | solution.py:694
  170.8 20.7 %collective-permute-done.19 = f32[256,1024]{1,0:T(8,128)} collective-permute-done((f32[256,1024]{1,0:T(8,128)}, f32[256,1024]{1,0:T(8,128)}, u32[]{:S(2)}, u32[]{:S(2)}) %collective-permute-start.19) | collective-permute-done | bytes 1048608 | tf_op jit(solution)/shard_map/ppermute | solution.py:694
  193.3 20.6 %collective-permute-done.13 = f32[256,1024]{1,0:T(8,128)S(1)} collective-permute-done((f32[256,1024]{1,0:T(8,128)S(1)}, f32[256,1024]{1,0:T(8,128)S(1)}, u32[]{:S(2)}, u32[]{:S(2)}) %collective-permute-start.13) | collective-permute-done | bytes 1048608 | tf_op jit(solution)/shard_map/ppermute | solution.py:694
  214.1 21.3 %collective-permute-done.7 = f32[256,1024]{1,0:T(8,128)S(1)} collective-permute-done((f32[256,1024]{1,0:T(8,128)S(1)}, f32[256,1024]{1,0:T(8,128)S(1)}, u32[]{:S(2)}, u32[]{:S(2)}) %collective-permute-start.7) | collective-permute-done | bytes 1048608 | tf_op jit(solution)/shard_map/ppermute | solution.py:694
  235.8 8.7 backward.4
  247.3 8.9 %backward.5 = (bf16[4,512,1024]{2,1,0:T(8,128)(2,1)}, f32[512,1024]{1,0:T(8,128)S(1)}, bf16[512,1024]{1,0:T(8,128)(2,1)S(1)}, bf16[512,1024]{1,0:T(8,128)(2,1)S(...) custom-call(s32[4]{0:T(128)S(1)} %pad_add_fusion.where_ref, ...), custom_call_target="tpu_custom_call", output_to_operand_aliasing={{0}: (12, {})} | custom-call | flops 2147483648 | bytes 15728640 | tf_op jit(solution)/shard_map/backward/pallas_call | solution.py:376
  262.5 8.8 %backward.6 = (bf16[4,512,1024]{2,1,0:T(8,128)(2,1)}, f32[512,1024]{1,0:T(8,128)S(1)}, bf16[512,1024]{1,0:T(8,128)(2,1)S(1)}, bf16[512,1024]{1,0:T(8,128)(2,1)S(...) custom-call(s32[4]{0:T(128)S(1)} %pad_add_fusion.where_ref, ...), custom_call_target="tpu_custom_call", output_to_operand_aliasing={{0}: (12, {})} | custom-call | flops 2147483648 | bytes 15728640 | tf_op jit(solution)/shard_map/backward/pallas_call | solution.py:376
  273.3 8.2 backward.7
  282.7 2.8 add.116
  285.4 1.8 collective-permute-start.44
  289.2 1.8 collective-permute-start.34
  291.6 19.9 %collective-permute-done.44 = f32[256,1024]{1,0:T(8,128)S(1)} collective-permute-done((f32[256,1024]{1,0:T(8,128)S(1)}, f32[256,1024]{1,0:T(8,128)S(1)}, u32[]{:S(2)}, u32[]{:S(2)}) %collective-permute-start.44) | collective-permute-done | bytes 1048608 | tf_op jit(solution)/shard_map/ppermute | solution.py:694
  312.7 21.3 %collective-permute-done.39 = f32[256,1024]{1,0:T(8,128)S(1)} collective-permute-done((f32[256,1024]{1,0:T(8,128)S(1)}, f32[256,1024]{1,0:T(8,128)S(1)}, u32[]{:S(2)}, u32[]{:S(2)}) %collective-permute-start.39) | collective-permute-done | bytes 1048608 | tf_op jit(solution)/shard_map/ppermute | solution.py:694
  335.2 21.3 %collective-permute-done.34 = f32[256,1024]{1,0:T(8,128)S(1)} collective-permute-done((f32[256,1024]{1,0:T(8,128)S(1)}, f32[256,1024]{1,0:T(8,128)S(1)}, u32[]{:S(2)}, u32[]{:S(2)}) %collective-permute-start.34) | collective-permute-done | bytes 1048608 | tf_op jit(solution)/shard_map/ppermute | solution.py:694
  357.8 20.6 %collective-permute-done.29 = f32[256,1024]{1,0:T(8,128)S(1)} collective-permute-done((f32[256,1024]{1,0:T(8,128)S(1)}, f32[256,1024]{1,0:T(8,128)S(1)}, u32[]{:S(2)}, u32[]{:S(2)}) %collective-permute-start.29) | collective-permute-done | bytes 1048608 | tf_op jit(solution)/shard_map/ppermute | solution.py:694
  383.0 1.9 copy-done.39
  389.3 5.3 first.7
  396.0 5.0 first.6
  402.5 5.0 first.5
  408.6 4.7 first.4
  415.7 3.3 products.3
  428.9 5.7 products.5
  434.6 1.9 copy-done.37
  436.6 2.2 copy-done.1
  442.6 7.6 project.1
  451.5 12.0 %attend_back.7 = (bf16[512,512]{1,0:T(8,128)(2,1)S(1)}, bf16[512,512]{1,0:T(8,128)(2,1)S(1)}, bf16[512,512]{1,0:T(8,128)(2,1)S(1)}, f32[256,1024]{1,0:T(8,128)S(1)}, f32[256,1024]{1,0:T(8,128)S(1)}) custom-call(s32[4]{0:T(128)S(1)} %pad_add_fusion.where_ref, bf16[4,512,512]{2,1,0:T(8,128)(2,1)S(1)} %get-tuple-element.152.q_ref, ...), custom_call_target="tpu_custom_call" | custom-call | flops 2952790016 | bytes 9437184 | tf_op jit(solution)/shard_map/attend_back/pallas_call | solution.py:603
  467.2 12.0 %attend_back.6 = (bf16[512,512]{1,0:T(8,128)(2,1)S(1)}, bf16[512,512]{1,0:T(8,128)(2,1)S(1)}, bf16[512,512]{1,0:T(8,128)(2,1)S(1)}, f32[256,1024]{1,0:T(8,128)S(1)}, f32[256,1024]{1,0:T(8,128)S(1)}) custom-call(s32[4]{0:T(128)S(1)} %pad_add_fusion.where_ref, bf16[4,512,512]{2,1,0:T(8,128)(2,1)S(1)} %get-tuple-element.152.q_ref, ...), custom_call_target="tpu_custom_call" | custom-call | flops 2952790016 | bytes 9437184 | tf_op jit(solution)/shard_map/attend_back/pallas_call | solution.py:603
  481.9 12.3 %attend_back.5 = (bf16[512,512]{1,0:T(8,128)(2,1)S(1)}, bf16[512,512]{1,0:T(8,128)(2,1)S(1)}, bf16[512,512]{1,0:T(8,128)(2,1)S(1)}, f32[256,1024]{1,0:T(8,128)S(1)}, f32[256,1024]{1,0:T(8,128)S(1)}) custom-call(s32[4]{0:T(128)S(1)} %pad_add_fusion.where_ref, bf16[4,512,512]{2,1,0:T(8,128)(2,1)S(1)} %get-tuple-element.152.q_ref, ...), custom_call_target="tpu_custom_call" | custom-call | flops 2952790016 | bytes 9437184 | tf_op jit(solution)/shard_map/attend_back/pallas_call | solution.py:603
  496.8 12.3 %attend_back.4 = (bf16[512,512]{1,0:T(8,128)(2,1)S(1)}, bf16[512,512]{1,0:T(8,128)(2,1)S(1)}, bf16[512,512]{1,0:T(8,128)(2,1)S(1)}, f32[256,1024]{1,0:T(8,128)S(1)}, f32[256,1024]{1,0:T(8,128)S(1)}) custom-call(s32[4]{0:T(128)S(1)} %pad_add_fusion.where_ref, bf16[4,512,512]{2,1,0:T(8,128)(2,1)S(1)} %get-tuple-element.152.q_ref, ...), custom_call_target="tpu_custom_call" | custom-call | flops 2952790016 | bytes 9437184 | tf_op jit(solution)/shard_map/attend_back/pallas_call | solution.py:603
  511.7 4.0 head_products.5
  515.8 2.2 copy-done.3
  522.1 4.0 head_products.4
  526.3 2.2 copy-done.4
  530.6 4.2 head_products.3
  544.8 5.7 products.4
  550.5 2.0 copy-done.38
  555.4 22.5 %all-reduce = f32[32]{0:T(128)S(1)} all-reduce(f32[32]{0:T(128)S(1)} %dynamic-update-slice), channel_id=3, replica_groups=mesh['dp'=8,'tensor'=4] {'dp'}, use_global_device_ids=true, to_apply=%add | all-reduce | flops 32 | bytes 256
  588.4 30.6 %all-gather.2 = f32[8,4,1024]{2,1,0:T(4,128)S(1)} all-gather(f32[1,4,1024]{2,1,0:T(4,128)S(1)} %maximum_bitcast_fusion), channel_id=2, replica_groups=mesh['dp'=8,'tensor'=4] {'dp'}, dimensions={0}, use_global_device_ids=true | all-gather | bytes 147456 | tf_op jit(solution)/shard_map/all_gather | solution.py:801
  628.1 2.0 copy.38
  630.1 12.9 %reduce-scatter.11.cloned.1.call-done = f32[128,256]{1,0:T(8,128)} async-done(((f32[1024,256]{1,0:T(8,128)}), f32[128,256]{1,0:T(8,128)}) %reduce-scatter.11.cloned.1.call-update) | async-done | bytes 131088 | tf_op jit(solution)/shard_map/reduce_scatter | solution.py:707
  643.0 66.6 %reduce-scatter.9.cloned.1.call-done = f32[128,256]{1,0:T(8,128)} async-done(((f32[1024,256]{1,0:T(8,128)}), f32[128,256]{1,0:T(8,128)}) %reduce-scatter.9.cloned.1.call-update) | async-done | bytes 131088 | tf_op jit(solution)/shard_map/reduce_scatter | solution.py:707
  709.6 66.2 %reduce-scatter.7.cloned.1.call-done = f32[128,256]{1,0:T(8,128)} async-done(((f32[1024,256]{1,0:T(8,128)}), f32[128,256]{1,0:T(8,128)}) %reduce-scatter.7.cloned.1.call-update) | async-done | bytes 131088 | tf_op jit(solution)/shard_map/reduce_scatter | solution.py:707
  775.9 91.6 %reduce-scatter.15.cloned.1.call-done = f32[128,1024]{1,0:T(8,128)} async-done(((f32[1024,1024]{1,0:T(8,128)}), f32[128,1024]{1,0:T(8,128)}) %reduce-scatter.15.cloned.1.call-update) | async-done | bytes 524304 | tf_op jit(solution)/shard_map/reduce_scatter | solution.py:707
  (469 shorter events, 135.4 us)
Async XLA Ops:
  7.2 31.2 %copy-start.166 = (s32[4,512]{1,0:T(4,128)S(1)}, s32[4,512]{1,0:T(4,128)}, u32[]{:S(2)}) copy-start(s32[4,512]{1,0:T(4,128)} %param.14) | copy-start | bytes 24580
  7.2 374.6 %all-gather.5.cloned.1.call-start = ((), (), s32[]{:S(2)}) async-start(), calls=%async_computation.6 | async-start | bytes 3538944 | tf_op jit(solution)/shard_map/all_gather | solution.py:732
  11.5 27.2 %copy-start.13 = (bf16[1024,256]{1,0:T(8,128)(2,1)S(1)}, bf16[1024,256]{1,0:T(8,128)(2,1)}, u32[]{:S(2)}) copy-start(bf16[1024,256]{1,0:T(8,128)(2,1)} %wv_ref.11) | copy-start | bytes 1572868
  12.1 32.0 %copy-start.163 = (f32[128,768]{1,0:T(8,128)}, f32[128,768]{1,0:T(8,128)S(1)}, u32[]{:S(2)}) copy-start(f32[128,768]{1,0:T(8,128)S(1)} %get-tuple-element.148) | copy-start | bytes 1179652
  12.2 26.2 %collective-permute-start.3 = (f32[256,1024]{1,0:T(8,128)S(1)}, f32[256,1024]{1,0:T(8,128)S(1)}, u32[]{:S(2)}, u32[]{:S(2)}) collective-permute-start(f32[256,1024]{1,0:T(8,128)S(1)} %get-tuple-element.124.own_ref), channel_id=1, source_target_pairs={{0,2},{1,3},{2,0},{3,1},{4,6},{5,7},{6,4},{7,5},{8,10},{9,11},{10,... | collective-permute-start | bytes 3145736 | tf_op jit(solution)/shard_map/ppermute | solution.py:694
  15.2 55.0 %collective-permute-start.4 = (f32[256,1024]{1,0:T(8,128)S(1)}, f32[256,1024]{1,0:T(8,128)S(1)}, u32[]{:S(2)}, u32[]{:S(2)}) collective-permute-start(f32[256,1024]{1,0:T(8,128)S(1)} %get-tuple-element.124.own_ref), channel_id=1, source_target_pairs={{0,1},{1,0},{2,3},{3,2},{4,5},{5,4},{6,7},{7,6},{8,9},{9,8},{10,11... | collective-permute-start | bytes 3145736 | tf_op jit(solution)/shard_map/ppermute | solution.py:691
  38.3 33.8 %copy-start.35 = (f32[256,1024]{1,0:T(8,128)}, f32[256,1024]{1,0:T(8,128)S(1)}, u32[]{:S(2)}) copy-start(f32[256,1024]{1,0:T(8,128)S(1)} %collective-permute-done.3.far_ref) | copy-start | bytes 3145732
  38.3 33.7 %collective-permute-start.5 = (f32[256,1024]{1,0:T(8,128)S(1)}, f32[256,1024]{1,0:T(8,128)S(1)}, u32[]{:S(2)}, u32[]{:S(2)}) collective-permute-start(f32[256,1024]{1,0:T(8,128)S(1)} %collective-permute-done.3.far_ref), channel_id=1, source_target_pairs={{0,1},{1,0},{2,3},{3,2},{4,5},{5,4},{6,7},{7,6},{8,9},{9,8},{10,11... | collective-permute-start | bytes 3145736 | tf_op jit(solution)/shard_map/ppermute | solution.py:691
  44.1 37.8 %copy-start.58 = (f32[512,256]{1,0:T(8,128)}, f32[512,256]{1,0:T(8,128)S(1)}, u32[]{:S(2)}) copy-start(f32[512,256]{1,0:T(8,128)S(1)} %get-tuple-element.139.own_ref) | copy-start | bytes 1572868
  44.2 14.8 %collective-permute-start.22 = (f32[512,256]{1,0:T(8,128)S(1)}, f32[512,256]{1,0:T(8,128)S(1)}, u32[]{:S(2)}, u32[]{:S(2)}) collective-permute-start(f32[512,256]{1,0:T(8,128)S(1)} %get-tuple-element.139.own_ref), channel_id=1, source_target_pairs={{0,2},{1,3},{2,0},{3,1},{4,6},{5,7},{6,4},{7,5},{8,10},{9,11},{10,... | collective-permute-start | bytes 1572872 | tf_op jit(solution)/shard_map/ppermute | solution.py:694
  46.0 14.7 %collective-permute-start.21 = (f32[512,256]{1,0:T(8,128)S(1)}, f32[512,256]{1,0:T(8,128)S(1)}, u32[]{:S(2)}, u32[]{:S(2)}) collective-permute-start(f32[512,256]{1,0:T(8,128)S(1)} %get-tuple-element.139.own_ref), channel_id=1, source_target_pairs={{0,1},{1,0},{2,3},{3,2},{4,5},{5,4},{6,7},{7,6},{8,9},{9,8},{10,11... | collective-permute-start | bytes 1572872 | tf_op jit(solution)/shard_map/ppermute | solution.py:691
  49.4 45.5 %copy-start.60 = (f32[512,256]{1,0:T(8,128)}, f32[512,256]{1,0:T(8,128)S(1)}, u32[]{:S(2)}) copy-start(f32[512,256]{1,0:T(8,128)S(1)} %get-tuple-element.134.own_ref) | copy-start | bytes 1572868
  49.4 20.7 %collective-permute-start.16 = (f32[512,256]{1,0:T(8,128)S(1)}, f32[512,256]{1,0:T(8,128)S(1)}, u32[]{:S(2)}, u32[]{:S(2)}) collective-permute-start(f32[512,256]{1,0:T(8,128)S(1)} %get-tuple-element.134.own_ref), channel_id=1, source_target_pairs={{0,2},{1,3},{2,0},{3,1},{4,6},{5,7},{6,4},{7,5},{8,10},{9,11},{10,... | collective-permute-start | bytes 1572872 | tf_op jit(solution)/shard_map/ppermute | solution.py:694
  53.7 53.8 %copy-start.62 = (f32[512,256]{1,0:T(8,128)}, f32[512,256]{1,0:T(8,128)S(1)}, u32[]{:S(2)}) copy-start(f32[512,256]{1,0:T(8,128)S(1)} %get-tuple-element.129.own_ref) | copy-start | bytes 1572868
  58.9 22.5 %collective-permute-start.10 = (f32[512,256]{1,0:T(8,128)S(1)}, f32[512,256]{1,0:T(8,128)S(1)}, u32[]{:S(2)}, u32[]{:S(2)}) collective-permute-start(f32[512,256]{1,0:T(8,128)S(1)} %get-tuple-element.129.own_ref), channel_id=1, source_target_pairs={{0,2},{1,3},{2,0},{3,1},{4,6},{5,7},{6,4},{7,5},{8,10},{9,11},{10,... | collective-permute-start | bytes 1572872 | tf_op jit(solution)/shard_map/ppermute | solution.py:694
  60.7 20.7 %collective-permute-start.23 = (f32[512,256]{1,0:T(8,128)S(1)}, f32[512,256]{1,0:T(8,128)S(1)}, u32[]{:S(2)}, u32[]{:S(2)}) collective-permute-start(f32[512,256]{1,0:T(8,128)S(1)} %collective-permute-done.22.far_ref), channel_id=1, source_target_pairs={{0,1},{1,0},{2,3},{3,2},{4,5},{5,4},{6,7},{7,6},{8,9},{9,8},{10,11... | collective-permute-start | bytes 1572872 | tf_op jit(solution)/shard_map/ppermute | solution.py:691
  64.3 58.3 %copy-start.64 = (f32[512,256]{1,0:T(8,128)}, f32[512,256]{1,0:T(8,128)S(1)}, u32[]{:S(2)}) copy-start(f32[512,256]{1,0:T(8,128)S(1)} %get-tuple-element.123.own_ref) | copy-start | bytes 1572868
  70.2 24.1 %collective-permute-start.15 = (f32[512,256]{1,0:T(8,128)S(1)}, f32[512,256]{1,0:T(8,128)S(1)}, u32[]{:S(2)}, u32[]{:S(2)}) collective-permute-start(f32[512,256]{1,0:T(8,128)S(1)} %get-tuple-element.134.own_ref), channel_id=1, source_target_pairs={{0,1},{1,0},{2,3},{3,2},{4,5},{5,4},{6,7},{7,6},{8,9},{9,8},{10,11... | collective-permute-start | bytes 1572872 | tf_op jit(solution)/shard_map/ppermute | solution.py:691
  70.2 24.2 %collective-permute-start.1 = (f32[512,256]{1,0:T(8,128)S(1)}, f32[512,256]{1,0:T(8,128)S(1)}, u32[]{:S(2)}, u32[]{:S(2)}) collective-permute-start(f32[512,256]{1,0:T(8,128)S(1)} %get-tuple-element.123.own_ref), channel_id=1, source_target_pairs={{0,2},{1,3},{2,0},{3,1},{4,6},{5,7},{6,4},{7,5},{8,10},{9,11},{10,... | collective-permute-start | bytes 1572872 | tf_op jit(solution)/shard_map/ppermute | solution.py:694
  72.0 22.8 %collective-permute-start.17 = (f32[512,256]{1,0:T(8,128)S(1)}, f32[512,256]{1,0:T(8,128)S(1)}, u32[]{:S(2)}, u32[]{:S(2)}) collective-permute-start(f32[512,256]{1,0:T(8,128)S(1)} %collective-permute-done.16.far_ref), channel_id=1, source_target_pairs={{0,1},{1,0},{2,3},{3,2},{4,5},{5,4},{6,7},{7,6},{8,9},{9,8},{10,11... | collective-permute-start | bytes 1572872 | tf_op jit(solution)/shard_map/ppermute | solution.py:691
  81.4 25.7 %collective-permute-start.9 = (f32[512,256]{1,0:T(8,128)S(1)}, f32[512,256]{1,0:T(8,128)S(1)}, u32[]{:S(2)}, u32[]{:S(2)}) collective-permute-start(f32[512,256]{1,0:T(8,128)S(1)} %get-tuple-element.129.own_ref), channel_id=1, source_target_pairs={{0,1},{1,0},{2,3},{3,2},{4,5},{5,4},{6,7},{7,6},{8,9},{9,8},{10,11... | collective-permute-start | bytes 1572872 | tf_op jit(solution)/shard_map/ppermute | solution.py:691
  81.4 26.1 %collective-permute-start.11 = (f32[512,256]{1,0:T(8,128)S(1)}, f32[512,256]{1,0:T(8,128)S(1)}, u32[]{:S(2)}, u32[]{:S(2)}) collective-permute-start(f32[512,256]{1,0:T(8,128)S(1)} %collective-permute-done.10.far_ref), channel_id=1, source_target_pairs={{0,1},{1,0},{2,3},{3,2},{4,5},{5,4},{6,7},{7,6},{8,9},{9,8},{10,11... | collective-permute-start | bytes 1572872 | tf_op jit(solution)/shard_map/ppermute | solution.py:691
  94.3 28.3 %collective-permute-start = (f32[512,256]{1,0:T(8,128)S(1)}, f32[512,256]{1,0:T(8,128)S(1)}, u32[]{:S(2)}, u32[]{:S(2)}) collective-permute-start(f32[512,256]{1,0:T(8,128)S(1)} %get-tuple-element.123.own_ref), channel_id=1, source_target_pairs={{0,1},{1,0},{2,3},{3,2},{4,5},{5,4},{6,7},{7,6},{8,9},{9,8},{10,11... | collective-permute-start | bytes 1572872 | tf_op jit(solution)/shard_map/ppermute | solution.py:691
  94.3 28.3 %collective-permute-start.2 = (f32[512,256]{1,0:T(8,128)S(1)}, f32[512,256]{1,0:T(8,128)S(1)}, u32[]{:S(2)}, u32[]{:S(2)}) collective-permute-start(f32[512,256]{1,0:T(8,128)S(1)} %collective-permute-done.1.far_ref), channel_id=1, source_target_pairs={{0,1},{1,0},{2,3},{3,2},{4,5},{5,4},{6,7},{7,6},{8,9},{9,8},{10,11... | collective-permute-start | bytes 1572872 | tf_op jit(solution)/shard_map/ppermute | solution.py:691
  94.8 41.4 %collective-permute-start.24 = (f32[256,1024]{1,0:T(8,128)S(1)}, f32[256,1024]{1,0:T(8,128)}, u32[]{:S(2)}, u32[]{:S(2)}) collective-permute-start(f32[256,1024]{1,0:T(8,128)S(1)} %get-tuple-element.142), channel_id=1, source_target_pairs={{0,1},{1,0},{2,3},{3,2},{4,5},{5,4},{6,7},{7,6},{8,9},{9,8},{10,11... | collective-permute-start | bytes 3145736 | tf_op jit(solution)/shard_map/ppermute | solution.py:691
  107.1 32.6 %collective-permute-start.18 = (f32[256,1024]{1,0:T(8,128)S(1)}, f32[256,1024]{1,0:T(8,128)}, u32[]{:S(2)}, u32[]{:S(2)}) collective-permute-start(f32[256,1024]{1,0:T(8,128)S(1)} %get-tuple-element.137), channel_id=1, source_target_pairs={{0,1},{1,0},{2,3},{3,2},{4,5},{5,4},{6,7},{7,6},{8,9},{9,8},{10,11... | collective-permute-start | bytes 3145736 | tf_op jit(solution)/shard_map/ppermute | solution.py:691
  122.5 24.7 %collective-permute-start.12 = (f32[256,1024]{1,0:T(8,128)}, f32[256,1024]{1,0:T(8,128)}, u32[]{:S(2)}, u32[]{:S(2)}) collective-permute-start(f32[256,1024]{1,0:T(8,128)} %get-tuple-element.132), channel_id=1, source_target_pairs={{0,1},{1,0},{2,3},{3,2},{4,5},{5,4},{6,7},{7,6},{8,9},{9,8},{10,11... | collective-permute-start | bytes 3145736 | tf_op jit(solution)/shard_map/ppermute | solution.py:691
  133.9 17.0 %collective-permute-start.6 = (f32[256,1024]{1,0:T(8,128)}, f32[256,1024]{1,0:T(8,128)}, u32[]{:S(2)}, u32[]{:S(2)}) collective-permute-start(f32[256,1024]{1,0:T(8,128)} %get-tuple-element.127), channel_id=1, source_target_pairs={{0,1},{1,0},{2,3},{3,2},{4,5},{5,4},{6,7},{7,6},{8,9},{9,8},{10,11... | collective-permute-start | bytes 3145736 | tf_op jit(solution)/shard_map/ppermute | solution.py:691
  134.4 12.0 %collective-permute-start.27 = (f32[128,768]{1,0:T(8,128)S(1)}, f32[128,768]{1,0:T(8,128)S(1)}, u32[]{:S(2)}, u32[]{:S(2)}) collective-permute-start(f32[128,768]{1,0:T(8,128)S(1)} %copy-done.164), channel_id=1, source_target_pairs={{0,2},{1,3},{2,0},{3,1},{4,6},{5,7},{6,4},{7,5},{8,10},{9,11},{10,... | collective-permute-start | bytes 1179656 | tf_op jit(solution)/shard_map/ppermute | solution.py:694
  138.6 30.4 %collective-permute-start.25 = (f32[256,1024]{1,0:T(8,128)}, f32[256,1024]{1,0:T(8,128)}, u32[]{:S(2)}, u32[]{:S(2)}) collective-permute-start(f32[256,1024]{1,0:T(8,128)} %add.105), channel_id=1, source_target_pairs={{0,2},{1,3},{2,0},{3,1},{4,6},{5,7},{6,4},{7,5},{8,10},{9,11},{10,... | collective-permute-start | bytes 3145736 | tf_op jit(solution)/shard_map/ppermute | solution.py:694
  142.1 49.4 %collective-permute-start.19 = (f32[256,1024]{1,0:T(8,128)}, f32[256,1024]{1,0:T(8,128)}, u32[]{:S(2)}, u32[]{:S(2)}) collective-permute-start(f32[256,1024]{1,0:T(8,128)} %add.103), channel_id=1, source_target_pairs={{0,2},{1,3},{2,0},{3,1},{4,6},{5,7},{6,4},{7,5},{8,10},{9,11},{10,... | collective-permute-start | bytes 3145736 | tf_op jit(solution)/shard_map/ppermute | solution.py:694
  147.2 479.2 %reduce-scatter.13.cloned.1.call-start = ((), (), s32[]{:S(2)}) async-start(), calls=%async_computation.10 | async-start | bytes 1179648 | tf_op jit(solution)/shard_map/reduce_scatter | solution.py:707
  149.1 64.7 %collective-permute-start.13 = (f32[256,1024]{1,0:T(8,128)S(1)}, f32[256,1024]{1,0:T(8,128)S(1)}, u32[]{:S(2)}, u32[]{:S(2)}) collective-permute-start(f32[256,1024]{1,0:T(8,128)S(1)} %add.101), channel_id=1, source_target_pairs={{0,2},{1,3},{2,0},{3,1},{4,6},{5,7},{6,4},{7,5},{8,10},{9,11},{10,... | collective-permute-start | bytes 3145736 | tf_op jit(solution)/shard_map/ppermute | solution.py:694
  152.3 83.2 %collective-permute-start.7 = (f32[256,1024]{1,0:T(8,128)S(1)}, f32[256,1024]{1,0:T(8,128)S(1)}, u32[]{:S(2)}, u32[]{:S(2)}) collective-permute-start(f32[256,1024]{1,0:T(8,128)S(1)} %add.99), channel_id=1, source_target_pairs={{0,2},{1,3},{2,0},{3,1},{4,6},{5,7},{6,4},{7,5},{8,10},{9,11},{10,... | collective-permute-start | bytes 3145736 | tf_op jit(solution)/shard_map/ppermute | solution.py:694
  170.7 65.0 %collective-permute-start.26 = (f32[256,1024]{1,0:T(8,128)S(1)}, f32[256,1024]{1,0:T(8,128)S(1)}, u32[]{:S(2)}, u32[]{:S(2)}) collective-permute-start(f32[256,1024]{1,0:T(8,128)S(1)} %add.106.own_ref), channel_id=1, source_target_pairs={{0,1},{1,0},{2,3},{3,2},{4,5},{5,4},{6,7},{7,6},{8,9},{9,8},{10,11... | collective-permute-start | bytes 3145736 | tf_op jit(solution)/shard_map/ppermute | solution.py:691
  193.2 54.1 %collective-permute-start.20 = (f32[256,1024]{1,0:T(8,128)S(1)}, f32[256,1024]{1,0:T(8,128)}, u32[]{:S(2)}, u32[]{:S(2)}) collective-permute-start(f32[256,1024]{1,0:T(8,128)S(1)} %add.104.own_ref), channel_id=1, source_target_pairs={{0,1},{1,0},{2,3},{3,2},{4,5},{5,4},{6,7},{7,6},{8,9},{9,8},{10,11... | collective-permute-start | bytes 3145736 | tf_op jit(solution)/shard_map/ppermute | solution.py:691
  214.0 46.8 %collective-permute-start.14 = (f32[256,1024]{1,0:T(8,128)S(1)}, f32[256,1024]{1,0:T(8,128)}, u32[]{:S(2)}, u32[]{:S(2)}) collective-permute-start(f32[256,1024]{1,0:T(8,128)S(1)} %add.102.own_ref), channel_id=1, source_target_pairs={{0,1},{1,0},{2,3},{3,2},{4,5},{5,4},{6,7},{7,6},{8,9},{9,8},{10,11... | collective-permute-start | bytes 3145736 | tf_op jit(solution)/shard_map/ppermute | solution.py:691
  235.6 37.7 %collective-permute-start.8 = (f32[256,1024]{1,0:T(8,128)S(1)}, f32[256,1024]{1,0:T(8,128)S(1)}, u32[]{:S(2)}, u32[]{:S(2)}) collective-permute-start(f32[256,1024]{1,0:T(8,128)S(1)} %add.100.own_ref), channel_id=1, source_target_pairs={{0,1},{1,0},{2,3},{3,2},{4,5},{5,4},{6,7},{7,6},{8,9},{9,8},{10,11... | collective-permute-start | bytes 3145736 | tf_op jit(solution)/shard_map/ppermute | solution.py:691
  246.8 35.9 %collective-permute-start.43 = (f32[256,1024]{1,0:T(8,128)S(1)}, f32[256,1024]{1,0:T(8,128)}, u32[]{:S(2)}, u32[]{:S(2)}) collective-permute-start(f32[256,1024]{1,0:T(8,128)S(1)} %get-tuple-element.181), channel_id=1, source_target_pairs={{0,1},{1,0},{2,3},{3,2},{4,5},{5,4},{6,7},{7,6},{8,9},{9,8},{10,11... | collective-permute-start | bytes 3145736 | tf_op jit(solution)/shard_map/ppermute | solution.py:691
  260.5 26.7 %collective-permute-start.38 = (f32[256,1024]{1,0:T(8,128)}, f32[256,1024]{1,0:T(8,128)}, u32[]{:S(2)}, u32[]{:S(2)}) collective-permute-start(f32[256,1024]{1,0:T(8,128)} %get-tuple-element.173), channel_id=1, source_target_pairs={{0,1},{1,0},{2,3},{3,2},{4,5},{5,4},{6,7},{7,6},{8,9},{9,8},{10,11... | collective-permute-start | bytes 3145736 | tf_op jit(solution)/shard_map/ppermute | solution.py:691
  273.2 15.9 %collective-permute-start.33 = (f32[256,1024]{1,0:T(8,128)S(1)}, f32[256,1024]{1,0:T(8,128)S(1)}, u32[]{:S(2)}, u32[]{:S(2)}) collective-permute-start(f32[256,1024]{1,0:T(8,128)S(1)} %get-tuple-element.165), channel_id=1, source_target_pairs={{0,1},{1,0},{2,3},{3,2},{4,5},{5,4},{6,7},{7,6},{8,9},{9,8},{10,11... | collective-permute-start | bytes 3145736 | tf_op jit(solution)/shard_map/ppermute | solution.py:691
  282.2 8.8 %collective-permute-start.28 = (f32[256,1024]{1,0:T(8,128)S(1)}, f32[256,1024]{1,0:T(8,128)S(1)}, u32[]{:S(2)}, u32[]{:S(2)}) collective-permute-start(f32[256,1024]{1,0:T(8,128)S(1)} %get-tuple-element.156), channel_id=1, source_target_pairs={{0,1},{1,0},{2,3},{3,2},{4,5},{5,4},{6,7},{7,6},{8,9},{9,8},{10,11... | collective-permute-start | bytes 3145736 | tf_op jit(solution)/shard_map/ppermute | solution.py:691
  285.4 26.1 %collective-permute-start.44 = (f32[256,1024]{1,0:T(8,128)S(1)}, f32[256,1024]{1,0:T(8,128)S(1)}, u32[]{:S(2)}, u32[]{:S(2)}) collective-permute-start(f32[256,1024]{1,0:T(8,128)S(1)} %add.116), channel_id=1, source_target_pairs={{0,2},{1,3},{2,0},{3,1},{4,6},{5,7},{6,4},{7,5},{8,10},{9,11},{10,... | collective-permute-start | bytes 3145736 | tf_op jit(solution)/shard_map/ppermute | solution.py:694
  288.7 45.3 %collective-permute-start.39 = (f32[256,1024]{1,0:T(8,128)S(1)}, f32[256,1024]{1,0:T(8,128)S(1)}, u32[]{:S(2)}, u32[]{:S(2)}) collective-permute-start(f32[256,1024]{1,0:T(8,128)S(1)} %add.113), channel_id=1, source_target_pairs={{0,2},{1,3},{2,0},{3,1},{4,6},{5,7},{6,4},{7,5},{8,10},{9,11},{10,... | collective-permute-start | bytes 3145736 | tf_op jit(solution)/shard_map/ppermute | solution.py:694
  289.2 67.2 %collective-permute-start.34 = (f32[256,1024]{1,0:T(8,128)S(1)}, f32[256,1024]{1,0:T(8,128)S(1)}, u32[]{:S(2)}, u32[]{:S(2)}) collective-permute-start(f32[256,1024]{1,0:T(8,128)S(1)} %add.110), channel_id=1, source_target_pairs={{0,2},{1,3},{2,0},{3,1},{4,6},{5,7},{6,4},{7,5},{8,10},{9,11},{10,... | collective-permute-start | bytes 3145736 | tf_op jit(solution)/shard_map/ppermute | solution.py:694
  291.2 87.1 %collective-permute-start.29 = (f32[256,1024]{1,0:T(8,128)S(1)}, f32[256,1024]{1,0:T(8,128)S(1)}, u32[]{:S(2)}, u32[]{:S(2)}) collective-permute-start(f32[256,1024]{1,0:T(8,128)S(1)} %add.107), channel_id=1, source_target_pairs={{0,2},{1,3},{2,0},{3,1},{4,6},{5,7},{6,4},{7,5},{8,10},{9,11},{10,... | collective-permute-start | bytes 3145736 | tf_op jit(solution)/shard_map/ppermute | solution.py:694
  312.7 76.5 %collective-permute-start.45 = (f32[256,1024]{1,0:T(8,128)}, f32[256,1024]{1,0:T(8,128)}, u32[]{:S(2)}, u32[]{:S(2)}) collective-permute-start(f32[256,1024]{1,0:T(8,128)} %add.117.own_ref), channel_id=1, source_target_pairs={{0,1},{1,0},{2,3},{3,2},{4,5},{5,4},{6,7},{7,6},{8,9},{9,8},{10,11... | collective-permute-start | bytes 3145736 | tf_op jit(solution)/shard_map/ppermute | solution.py:691
  335.2 60.8 %collective-permute-start.40 = (f32[256,1024]{1,0:T(8,128)}, f32[256,1024]{1,0:T(8,128)}, u32[]{:S(2)}, u32[]{:S(2)}) collective-permute-start(f32[256,1024]{1,0:T(8,128)} %add.114.own_ref), channel_id=1, source_target_pairs={{0,1},{1,0},{2,3},{3,2},{4,5},{5,4},{6,7},{7,6},{8,9},{9,8},{10,11... | collective-permute-start | bytes 3145736 | tf_op jit(solution)/shard_map/ppermute | solution.py:691
  357.7 44.7 %collective-permute-start.35 = (f32[256,1024]{1,0:T(8,128)}, f32[256,1024]{1,0:T(8,128)}, u32[]{:S(2)}, u32[]{:S(2)}) collective-permute-start(f32[256,1024]{1,0:T(8,128)} %add.111.own_ref), channel_id=1, source_target_pairs={{0,1},{1,0},{2,3},{3,2},{4,5},{5,4},{6,7},{7,6},{8,9},{9,8},{10,11... | collective-permute-start | bytes 3145736 | tf_op jit(solution)/shard_map/ppermute | solution.py:691
  379.5 29.0 %collective-permute-start.30 = (f32[256,1024]{1,0:T(8,128)}, f32[256,1024]{1,0:T(8,128)}, u32[]{:S(2)}, u32[]{:S(2)}) collective-permute-start(f32[256,1024]{1,0:T(8,128)} %add.108.own_ref), channel_id=1, source_target_pairs={{0,1},{1,0},{2,3},{3,2},{4,5},{5,4},{6,7},{7,6},{8,9},{9,8},{10,11... | collective-permute-start | bytes 3145736 | tf_op jit(solution)/shard_map/ppermute | solution.py:691
  419.1 209.0 %reduce-scatter.17.cloned.1.call-start = ((), (), s32[]{:S(2)}) async-start(), calls=%async_computation.12 | async-start | bytes 4718592 | tf_op jit(solution)/shard_map/reduce_scatter | solution.py:707
  436.6 206.5 %reduce-scatter.11.cloned.1.call-start = ((), (), s32[]{:S(2)}) async-start(), calls=%async_computation.9 | async-start | bytes 1179648 | tf_op jit(solution)/shard_map/reduce_scatter | solution.py:707
  515.7 193.9 %reduce-scatter.9.cloned.1.call-start = ((), (), s32[]{:S(2)}) async-start(), calls=%async_computation.8 | async-start | bytes 1179648 | tf_op jit(solution)/shard_map/reduce_scatter | solution.py:707
  526.2 249.7 %reduce-scatter.7.cloned.1.call-start = ((), (), s32[]{:S(2)}) async-start(), calls=%async_computation.7 | async-start | bytes 1179648 | tf_op jit(solution)/shard_map/reduce_scatter | solution.py:707
  534.8 332.7 %reduce-scatter.15.cloned.1.call-start = ((), (), s32[]{:S(2)}) async-start(), calls=%async_computation.11 | async-start | bytes 4718592 | tf_op jit(solution)/shard_map/reduce_scatter | solution.py:707
  552.5 27.5 %copy-start.67 = (f32[256,1024]{1,0:T(8,128)S(1)}, f32[256,1024]{1,0:T(8,128)}, u32[]{:S(2)}) copy-start(f32[256,1024]{1,0:T(8,128)} %copy-done.66) | copy-start | bytes 3145732
  552.5 25.6 %collective-permute-start.46 = (f32[256,1024]{1,0:T(8,128)}, f32[256,1024]{1,0:T(8,128)}, u32[]{:S(2)}, u32[]{:S(2)}) collective-permute-start(f32[256,1024]{1,0:T(8,128)} %copy-done.162), channel_id=1, source_target_pairs={{0,1},{1,0},{2,3},{3,2},{4,5},{5,4},{6,7},{7,6},{8,9},{9,8},{10,11... | collective-permute-start | bytes 3145736 | tf_op jit(solution)/shard_map/ppermute | solution.py:691
  553.1 26.8 %collective-permute-start.41 = (f32[256,1024]{1,0:T(8,128)}, f32[256,1024]{1,0:T(8,128)}, u32[]{:S(2)}, u32[]{:S(2)}) collective-permute-start(f32[256,1024]{1,0:T(8,128)} %copy-done.161), channel_id=1, source_target_pairs={{0,1},{1,0},{2,3},{3,2},{4,5},{5,4},{6,7},{7,6},{8,9},{9,8},{10,11... | collective-permute-start | bytes 3145736 | tf_op jit(solution)/shard_map/ppermute | solution.py:691
  553.2 28.6 %collective-permute-start.36 = (f32[256,1024]{1,0:T(8,128)}, f32[256,1024]{1,0:T(8,128)}, u32[]{:S(2)}, u32[]{:S(2)}) collective-permute-start(f32[256,1024]{1,0:T(8,128)} %copy-done.160), channel_id=1, source_target_pairs={{0,1},{1,0},{2,3},{3,2},{4,5},{5,4},{6,7},{7,6},{8,9},{9,8},{10,11... | collective-permute-start | bytes 3145736 | tf_op jit(solution)/shard_map/ppermute | solution.py:691
  553.7 29.7 %collective-permute-start.31 = (f32[256,1024]{1,0:T(8,128)}, f32[256,1024]{1,0:T(8,128)}, u32[]{:S(2)}, u32[]{:S(2)}) collective-permute-start(f32[256,1024]{1,0:T(8,128)} %copy-done.159), channel_id=1, source_target_pairs={{0,1},{1,0},{2,3},{3,2},{4,5},{5,4},{6,7},{7,6},{8,9},{9,8},{10,11... | collective-permute-start | bytes 3145736 | tf_op jit(solution)/shard_map/ppermute | solution.py:691
  579.9 39.6 %collective-permute-start.47 = (f32[256,1024]{1,0:T(8,128)S(1)}, f32[256,1024]{1,0:T(8,128)S(1)}, u32[]{:S(2)}, u32[]{:S(2)}) collective-permute-start(f32[256,1024]{1,0:T(8,128)S(1)} %add.118.own_ref), channel_id=1, source_target_pairs={{0,1},{1,0},{2,3},{3,2},{4,5},{5,4},{6,7},{7,6},{8,9},{9,8},{10,11... | collective-permute-start | bytes 3145736 | tf_op jit(solution)/shard_map/ppermute | solution.py:691
  581.3 39.9 %collective-permute-start.42 = (f32[256,1024]{1,0:T(8,128)S(1)}, f32[256,1024]{1,0:T(8,128)S(1)}, u32[]{:S(2)}, u32[]{:S(2)}) collective-permute-start(f32[256,1024]{1,0:T(8,128)S(1)} %add.115.own_ref), channel_id=1, source_target_pairs={{0,1},{1,0},{2,3},{3,2},{4,5},{5,4},{6,7},{7,6},{8,9},{9,8},{10,11... | collective-permute-start | bytes 3145736 | tf_op jit(solution)/shard_map/ppermute | solution.py:691
  583.3 39.7 %collective-permute-start.37 = (f32[256,1024]{1,0:T(8,128)S(1)}, f32[256,1024]{1,0:T(8,128)S(1)}, u32[]{:S(2)}, u32[]{:S(2)}) collective-permute-start(f32[256,1024]{1,0:T(8,128)S(1)} %add.112.own_ref), channel_id=1, source_target_pairs={{0,1},{1,0},{2,3},{3,2},{4,5},{5,4},{6,7},{7,6},{8,9},{9,8},{10,11... | collective-permute-start | bytes 3145736 | tf_op jit(solution)/shard_map/ppermute | solution.py:691
  584.8 39.9 %collective-permute-start.32 = (f32[256,1024]{1,0:T(8,128)S(1)}, f32[256,1024]{1,0:T(8,128)S(1)}, u32[]{:S(2)}, u32[]{:S(2)}) collective-permute-start(f32[256,1024]{1,0:T(8,128)S(1)} %add.109.own_ref), channel_id=1, source_target_pairs={{0,1},{1,0},{2,3},{3,2},{4,5},{5,4},{6,7},{7,6},{8,9},{9,8},{10,11... | collective-permute-start | bytes 3145736 | tf_op jit(solution)/shard_map/ppermute | solution.py:691
  (159 other events, 818.3 us)
Sparse Core Ops, SparseCore 0:
  147.3 61.9 all-gather.4
  419.2 65.0 reduce-scatter.12
  488.4 87.4 reduce-scatter.16
  579.7 63.3 reduce-scatter.10
  647.2 62.3 reduce-scatter.8
  713.5 62.3 reduce-scatter.6
  780.5 86.9 reduce-scatter.14

commit v2 on v0

v2 whole, which is shorter than its diff:
```python
import functools

import jax
import jax.numpy as jnp
from jax import lax
from jax.experimental import pallas as pl
from jax.experimental.pallas import tpu as pltpu
from jax.sharding import PartitionSpec as P

F32 = jnp.float32
BF16 = jnp.bfloat16
HEAD_DIM = 64
FAR = -1e30
EPS = 1e-06
CLIP = 10.0
SCALE = HEAD_DIM**-0.5
ROOT_HALF = 0.5**0.5
BELL = 0.3989422804014327
GROUP = 4
DOCS = 4
MIB = 1 << 20
RING = (0, 2, 4, 6, 7, 5, 3, 1)
OWNERS = tuple(
    tuple(RING[(RING.index(r) + way * (1 + n)) % 8] for n in range(8) for way in (-1, 1))
    for r in range(8)
)
ANY = pl.BlockSpec(memory_space=pl.ANY)
RESIDENT = pl.BlockSpec(memory_space=pltpu.VMEM)


def dot(left, right, left_dim=1, right_dim=0):
    return lax.dot_general(
        left, right, (((left_dim,), (right_dim,)), ((), ())), preferred_element_type=F32
    )


def normalize(total):
    average = jnp.mean(total, axis=-1, keepdims=True)
    centred = total - average
    variance = jnp.mean(centred * centred, axis=-1, keepdims=True)
    scaled = lax.rsqrt(variance + EPS)
    return centred * scaled, scaled


def norm_back(upstream, normed, scaled, gain):
    weighted = upstream * gain
    first = jnp.mean(weighted, axis=-1, keepdims=True)
    second = jnp.mean(weighted * normed, axis=-1, keepdims=True)
    return scaled * (weighted - first - normed * second)


def lanes(width):
    lane = lax.broadcasted_iota(jnp.int32, (1, width), 1)
    return lane // HEAD_DIM, lane % HEAD_DIM


def mask_terms(ids, width):
    _, lane = lanes(width)
    equal = ids == lane
    document = lane < DOCS
    queries = jnp.where(document & equal, FAR, 0.0).astype(BF16)
    keys = jnp.where(document & equal, 0.0, jnp.where(lane < DOCS + 3, 1.0, 0.0)).astype(BF16)
    return queries, keys


def split(value):
    high = value.astype(BF16)
    rest = value - high.astype(F32)
    middle = rest.astype(BF16)
    return high, middle, (rest - middle.astype(F32)).astype(BF16)


def pick(head, owner, own, spare, zero):
    return jnp.where(owner == head, own, jnp.where(owner == (head + 1) % GROUP, spare, zero))


def shape(dims, dtype):
    return jax.ShapeDtypeStruct(tuple(dims), dtype)


def whole_block(array):
    zeros = (0,) * len(array.shape)
    return pl.BlockSpec(tuple(array.shape), lambda i, w: zeros)


def rows_block(rows, columns):
    return pl.BlockSpec((rows, columns), lambda i, w: (i, 0))


class Order:
    def __init__(self):
        self.token, self.stored = None, False

    def taken(self):
        if self.token is None:
            return []
        if self.stored:
            return [pltpu.with_memory_space_constraint(self.token, pltpu.HBM)]
        return [self.token]

    def give(self, results, stored):
        sizes = [r.size * r.dtype.itemsize for r in results]
        index = sizes.index(min(sizes))
        self.token, self.stored = results[index], index in stored


def launch(
    kernel, name, where, inputs, in_specs, outs, out_specs, grid, vmem, after,
    scratch=(), aliases=None, streamed=(), stored=(),
):
    count = len(inputs)
    tokens = after.taken()
    inputs = [
        pltpu.with_memory_space_constraint(value, pltpu.HBM) if i in streamed else value
        for i, value in enumerate(inputs)
    ]
    outs = [
        pltpu.HBM(value.shape, value.dtype) if i in stored else value
        for i, value in enumerate(outs)
    ]

    def run(where_ref, *refs):
        kernel(where_ref, *refs[:count], *refs[count + len(tokens) :])

    results = pl.pallas_call(
        run,
        grid_spec=pltpu.PrefetchScalarGridSpec(
            num_scalar_prefetch=1,
            grid=grid,
            in_specs=list(in_specs) + [ANY] * len(tokens),
            out_specs=list(out_specs),
            scratch_shapes=list(scratch),
        ),
        out_shape=outs,
        input_output_aliases=aliases or {},
        compiler_params=pltpu.CompilerParams(
            vmem_limit_bytes=vmem * MIB, dimension_semantics=("arbitrary",) * len(grid)
        ),
        cost_estimate=pl.CostEstimate(flops=1, bytes_accessed=1, transcendentals=0),
        name=name,
    )(where, *inputs, *tokens)
    after.give(results, stored)
    return results


def gate_kernel(*refs):
    del refs


def gate(where, *values, after):
    outs = [shape(v.shape, v.dtype) for v in values]
    return launch(
        gate_kernel, "gate", where, values, [ANY] * len(values), outs, [ANY] * len(values), (1,),
        2, after, aliases={i + 1: i for i in range(len(values))},
    )


def parts_kernel(where_ref, value_ref, left_ref, right_ref, slices_ref):
    rows, half = left_ref.shape
    left_ref[...] = value_ref[0:rows, 0:half]
    right_ref[...] = value_ref[0:rows, half:]
    slices_ref[...] = value_ref[rows:, 0 : slices_ref.shape[1]]


def parts(where, value, rows, columns, after):
    depth = value.shape[1]
    outs = [shape((rows, depth // 2), F32)] * 2 + [shape((value.shape[0] - rows, columns), F32)]
    return launch(
        parts_kernel, "parts", where, (value,), [whole_block(value)], outs,
        [whole_block(o) for o in outs], (1,), 8, after,
    )


def widen_heads_kernel(where_ref, wq_ref, wk_ref, wv_ref, wo_ref, sq, sk, sv, own, wide, wo):
    width = wq_ref.shape[1]
    for index, ref in enumerate((wq_ref, wk_ref, wv_ref)):
        columns = slice(index * width, (index + 1) * width)
        value = ref[...]
        own[:, columns] = value
        wide[:, columns] = value.astype(F32)
    rows, depth = wo_ref.shape
    for index, ref in enumerate((sq, sk, sv)):
        wo[rows:, index * width : (index + 1) * width] = ref[...].astype(F32)
    wo[rows:, 3 * width :] = jnp.zeros((wo.shape[0] - rows, depth - 3 * width), F32)
    for index in range(depth // width):
        wide[index * rows : (index + 1) * rows, 3 * width :] = wo_ref[
            :, index * width : (index + 1) * width
        ].astype(F32)
    wo[0:rows, :] = wo_ref[...].astype(F32)


def widen_heads(where, wq, wk, wv, wo, part, after):
    depth, width = wq.shape
    rows = pl.BlockSpec((part, width), lambda i, w: (w[3], 0))
    outs = [
        shape((depth, 3 * width), BF16),
        shape((depth, 4 * width), F32),
        shape((wo.shape[0] + part, depth), F32),
    ]
    inputs = (wq, wk, wv, wo)
    return launch(
        widen_heads_kernel, "widen_heads", where, (*inputs, wq, wk, wv),
        [whole_block(a) for a in inputs] + [rows] * 3, outs, [whole_block(o) for o in outs], (1,),
        12, after, streamed=range(7),
    )


def assemble_kernel(where_ref, own_ref, near_ref, *refs):
    *halves, out_ref = refs
    rows, depth = own_ref.shape
    half = depth // 2
    mine = where_ref[2] * 2 * rows
    other = (1 - where_ref[2]) * 2 * rows
    out_ref[pl.ds(pl.multiple_of(mine, rows), rows), :] = own_ref[...]
    out_ref[pl.ds(pl.multiple_of(mine + rows, rows), rows), :] = near_ref[...]
    for start, left, right in ((other, *halves[0:2]), (other + rows, *halves[2:4])):
        place = pl.ds(pl.multiple_of(start, rows), rows)
        out_ref[place, 0:half] = left[...].astype(BF16)
        out_ref[place, half:] = right[...].astype(BF16)


def assemble(where, own, near, far, both, after):
    rows, columns = own.shape
    out = shape((4 * rows, columns), BF16)
    inputs = (own, near, *far, *both)
    return launch(
        assemble_kernel, "assemble", where, inputs, [whole_block(a) for a in inputs], [out],
        [whole_block(out)], (1,), 14, after,
    )[0]


def narrow_near_kernel(where_ref, wide_ref, heads_ref, wo_ref):
    width = heads_ref.shape[1] // 3
    heads_ref[...] = wide_ref[:, 0 : 3 * width].astype(BF16)
    rows, depth = wo_ref.shape
    for index in range(depth // width):
        wo_ref[:, index * width : (index + 1) * width] = wide_ref[
            index * rows : (index + 1) * rows, 3 * width :
        ].astype(BF16)


def narrow_near(where, wide, wo, after):
    depth, columns = wide.shape
    outs = [shape((depth, 3 * columns // 4), BF16), shape(wo.shape, BF16)]
    return launch(
        narrow_near_kernel, "narrow_near", where, (wide,), [whole_block(wide)], outs,
        [whole_block(o) for o in outs], (1,), 14, after,
    )


def convert_kernel(where_ref, *refs):
    half = len(refs) // 2
    for source, target in zip(refs[:half], refs[half:]):
        target[...] = source[...].astype(target.dtype)


def convert(where, *values, dtype, after):
    specs = [rows_block(v.shape[0] // 4, v.shape[1]) for v in values]
    held = range(len(values))
    return launch(
        convert_kernel, "convert", where, values, specs, [shape(v.shape, dtype) for v in values],
        specs, (4,), 10, after, streamed=held if dtype == F32 else (), stored=held,
    )


def narrow_kernel(where_ref, wide_ref, left_ref, right_ref):
    width = left_ref.shape[1]
    left_ref[...] = wide_ref[:, 0:width].astype(BF16)
    right_ref[...] = wide_ref[:, width:].astype(BF16)


def narrow(where, wide, after):
    rows, width = wide.shape[0] // 4, wide.shape[1] // 2
    return launch(
        narrow_kernel, "narrow", where, (wide,), [rows_block(rows, 2 * width)],
        [shape((4 * rows, width), BF16)] * 2, [rows_block(rows, width)] * 2, (4,), 8, after,
        streamed=(0,),
    )


def project_group(x, weights):
    width = weights.shape[1] // 3
    q = (dot(x, weights[:, 0:width]).astype(BF16) * SCALE).astype(BF16)
    k = dot(x, weights[:, width : 2 * width]).astype(BF16)
    v = dot(x, weights[:, 2 * width : 3 * width]).astype(BF16)
    return q, k, v


def attend_kernel(
    where_ref, x_ref, own_ref, near_ref, col_ref, low_ref, qkv_ref, top_ref, *rest
):
    *o_refs, sums_ref = rest
    x = x_ref[0]
    length = x.shape[0]
    width = own_ref.shape[1] // 3
    owner, _ = lanes(width)
    mask_q, mask_k = mask_terms(col_ref[0][:, 0:1], width)
    zero = jnp.zeros((), BF16)
    sums_ref[...] = jnp.zeros_like(sums_ref)
    for group, weights in enumerate((own_ref, near_ref)):
        queries, keys, values = project_group(x, weights)
        for index, value in enumerate((queries, keys, values)):
            start = (3 * group + index) * width
            qkv_ref[0, :, start : start + width] = value
        total = jnp.zeros(queries.shape, F32)
        for head in range(GROUP):
            mine = owner == head
            scores = dot(
                pick(head, owner, queries, mask_q, zero), jnp.where(mine, keys, mask_k), 1, 1
            )
            top = jnp.max(scores, axis=-1, keepdims=True)
            raised = jnp.exp(scores - top)
            summed = jnp.sum(raised, axis=-1, keepdims=True)
            chances = raised * (1.0 / summed)
            total = total + dot(chances.astype(BF16), jnp.where(mine, values, zero))
            row = group * GROUP + head
            sums_ref[:, row : row + 1] = top + jnp.log(summed)
            top_ref[0, row : row + 1, :] = jnp.broadcast_to(
                jnp.max(top, axis=0, keepdims=True), (1, top_ref.shape[2])
            )
        low = total.astype(BF16)
        low_ref[0, :, group * width : (group + 1) * width] = low
        for index, o_ref in enumerate(o_refs):

            @pl.when(pl.program_id(0) == index)
            def _(o_ref=o_ref):
                o_ref[0:length, group * width : (group + 1) * width] = low.astype(F32)

    for index, o_ref in enumerate(o_refs):

        @pl.when(pl.program_id(0) == index)
        def _(o_ref=o_ref):
            o_ref[length:, :] = sums_ref[...].T[0:8, :]


def sequence(i, dims):
    return pl.BlockSpec((1, *dims), lambda g, w: (2 * w[1] + i, 0, 0))


def attend(where, x, own, near, seg_col, after):
    count, length, depth = x.shape
    both = 2 * own.shape[1] // 3
    outs = [
        shape((count // 2, length, both), BF16),
        shape((count // 2, length, 3 * both), BF16),
        shape((count // 2, both // HEAD_DIM, 128), F32),
    ]
    out_specs = [pl.BlockSpec((1, *o.shape[1:]), lambda i, w: (i, 0, 0)) for o in outs]
    outs += [shape((length + 8, both), F32)] * (count // 2)
    out_specs += [whole_block(o) for o in outs[3:]]
    return launch(
        attend_kernel, "attend", where, (x, own, near, seg_col),
        [
            pl.BlockSpec((1, length, depth), lambda i, w: (2 * w[1] + i, 0, 0)),
            RESIDENT,
            RESIDENT,
            pl.BlockSpec((1, length, 128), lambda i, w: (2 * w[1] + i, 0, 0)),
        ],
        outs, out_specs, (count // 2,), 20, after, streamed=(0, 3), stored=(0, 1),
        scratch=[pltpu.VMEM((length, 128), F32)],
    )


def project_kernel(where_ref, x_ref, far_ref, both_ref, out_ref):
    width = far_ref.shape[1] // 3
    for group, weights in enumerate((far_ref, both_ref)):
        for index, value in enumerate(project_group(x_ref[0], weights)):
            start = (3 * group + index) * width
            out_ref[0, :, start : start + width] = value


def project(where, x, far, both, after):
    count, length, depth = x.shape
    width = far.shape[1]
    return launch(
        project_kernel, "project", where, (x, far, both),
        [
            pl.BlockSpec((1, length, depth), lambda i, w: (2 * w[1] + i, 0, 0)),
            RESIDENT,
            RESIDENT,
        ],
        [shape((count // 2, length, 2 * width), BF16)],
        [pl.BlockSpec((1, length, 2 * width), lambda i, w: (i, 0, 0))],
        (count // 2,), 12, after, streamed=(0,), stored=(0,),
    )[0]


def fetch(sources, held_ref, arrived):
    first = pl.program_id(0) == 0
    copies = [
        pltpu.make_async_copy(source, held_ref.at[n], arrived.at[n])
        for n, source in enumerate(sources)
    ]

    @pl.when(first)
    def _():
        for copy in copies:
            copy.start()

    def get(n):
        @pl.when(first)
        def _():
            copies[n].wait()

        return held_ref[n]

    return get


def forward_kernel(
    where_ref, x_ref, mixed_ref, mixed_far_ref, wo_ref, gain_ref,
    shift_ref, up_own, up_near, down_own, down_near,
    normed_ref, scaled_ref, low_ref, active_ref, pull_ref, *rest,
):
    *part_refs, both_ref, held_ref, arrived = rest
    weight = fetch((up_own, down_own, up_near, down_near), held_ref, arrived)
    width = mixed_ref.shape[1]
    chip = where_ref[2]
    both_ref[:, pl.ds(pl.multiple_of(chip * width, width), width)] = mixed_ref[...].astype(BF16)
    both_ref[:, pl.ds(pl.multiple_of((1 - chip) * width, width), width)] = mixed_far_ref[
        ...
    ].astype(BF16)
    normed, scaled = normalize(x_ref[0].astype(F32) + dot(both_ref[...], wo_ref[...]))
    normed_ref[...] = normed
    scaled_ref[...] = jnp.broadcast_to(scaled, scaled_ref.shape)
    low = (normed * gain_ref[...] + shift_ref[...]).astype(BF16)
    low_ref[...] = low
    hidden = up_own.shape[1]
    parts = []
    for group in range(2):
        columns = slice(group * hidden, (group + 1) * hidden)
        before = dot(low, weight(2 * group))
        chance = 0.5 * (1.0 + lax.erf(before * ROOT_HALF))
        active = (before * chance).astype(BF16)
        active_ref[:, columns] = active
        pull_ref[:, columns] = chance + before * (jnp.exp(-0.5 * before * before) * BELL)
        parts.append(dot(active, weight(2 * group + 1)))
    total = parts[0] + parts[1]
    if len(part_refs) == 1:
        part_refs[0][...] = total
        return
    for index, ref in enumerate(part_refs):

        @pl.when(pl.program_id(0) == index)
        def _(ref=ref):
            ref[...] = total


def fetched(array):
    return [pltpu.VMEM((4, *array.shape), array.dtype), pltpu.SemaphoreType.DMA((4,))]


def forward(i, where, x, mixed, mixed_far, wo, gain, shift, ups, downs, after, halves):
    _, length, depth = x.shape
    width = mixed.shape[1]
    hidden = 2 * ups[0].shape[1]
    half = length // 2
    pieces = rows_block(half, width)
    outs = [
        shape((length, depth), F32),
        shape((length, 128), F32),
        shape((length, depth), BF16),
        shape((length, hidden), BF16),
        shape((length, hidden), F32),
    ]
    out_specs = [rows_block(half, o.shape[1]) for o in outs]
    if halves:
        outs += [shape((half, depth), F32)] * 2
        out_specs += [whole_block(o) for o in outs[5:]]
    else:
        outs.append(shape((length, depth), F32))
        out_specs.append(rows_block(half, depth))
    return launch(
        forward_kernel, "forward", where, (x, mixed, mixed_far, wo, gain, shift, *ups, *downs),
        [
            pl.BlockSpec((1, half, depth), lambda g, w: (2 * w[1] + i, g, 0)),
            pieces,
            pieces,
            RESIDENT,
            whole_block(gain),
            whole_block(shift),
            *[ANY] * 4,
        ],
        outs, out_specs, (2,), 30, after,
        streamed=(0, 6, 7, 8, 9), stored=(0, 1, 2, 3, 4),
        scratch=[pltpu.VMEM((half, 2 * width), BF16), *fetched(ups[0])],
    )


def backward_kernel(
    where_ref, normed_ref, gain_ref, shift_ref, grad_ref, second_gain_ref, second_shift_ref,
    pull_ref, up_own, up_near, down_own, down_near, *rest, halves,
):
    (
        final_ref, out_ref, slope_ref, slope_low_ref, before_ref, sums_ref, part_out_ref, held_ref,
        arrived,
    ) = rest[-9:]
    weight = fetch((down_own, up_own, down_near, up_near), held_ref, arrived)
    step = pl.program_id(0)
    hidden = normed_ref[...] * gain_ref[...] + shift_ref[...]
    if halves:
        first, second, far_first, far_second = rest[:4]
        total = jnp.where(step == 0, first[...] + far_first[...], second[...] + far_second[...])
    else:
        total = rest[0][...] + rest[1][...]
    normed, scaled = normalize(hidden + total)
    out = (normed * second_gain_ref[...] + second_shift_ref[...]).astype(BF16)
    final_ref[0] = out
    out_ref[...] = out.astype(F32)
    upstream = grad_ref[0].astype(F32)

    @pl.when(step == 0)
    def _():
        sums_ref[...] = jnp.zeros_like(sums_ref)

    sums_ref[0:1, :] += jnp.sum(upstream * normed, axis=0, keepdims=True)
    sums_ref[1:2, :] += jnp.sum(upstream, axis=0, keepdims=True)
    slope = norm_back(upstream, normed, scaled, second_gain_ref[...])
    slope_ref[...] = slope
    low = slope.astype(BF16)
    slope_low_ref[...] = low
    units = up_own.shape[1]
    parts = []
    for group in range(2):
        columns = slice(group * units, (group + 1) * units)
        before = (dot(low, weight(2 * group), 1, 1) * pull_ref[:, columns]).astype(BF16)
        before_ref[:, columns] = before
        parts.append(dot(before, weight(2 * group + 1), 1, 1))
    part_out_ref[...] = parts[0] + parts[1]


def backward(
    i, where, normed, gain, shift, part, part_far, out_grad, second_gain, second_shift, pull,
    ups, downs, final, after,
):
    count, length, depth = out_grad.shape
    hidden = 2 * ups[0].shape[1]
    half = length // 2
    outs = [
        shape((length, depth), F32),
        shape((length, depth), F32),
        shape((length, depth), BF16),
        shape((length, hidden), BF16),
        shape((8, depth), F32),
        shape((length, depth), F32),
    ]
    out_specs = [rows_block(half, o.shape[1]) for o in outs]
    out_specs[4] = whole_block(outs[4])
    block = pl.BlockSpec((1, half, depth), lambda g, w: (2 * w[1] + i, g, 0))
    vector = whole_block(gain)
    rows = rows_block(half, depth)
    carried = [] if final is None else [final]
    halves = len(part) == 2
    last = 11 + 2 * len(part)
    return launch(
        functools.partial(backward_kernel, halves=halves), "backward", where,
        (
            normed, gain, shift, out_grad, second_gain, second_shift, pull, *ups, *downs, *part,
            *part_far, *carried,
        ),
        [
            rows,
            vector,
            vector,
            block,
            vector,
            vector,
            rows_block(half, hidden),
            *[ANY] * 4,
            *[whole_block(a) if halves else rows for a in (*part, *part_far)],
            *[ANY] * len(carried),
        ],
        [shape((count, length, depth), BF16), *outs], [block, *out_specs], (2,), 34, after,
        streamed=(0, 3, *range(6, 11), *[last] * len(carried)), stored=(0, 1, 2, 3, 4),
        scratch=fetched(ups[0]), aliases={last + 1: 0} if carried else {},
    )


def products_kernel(where_ref, *refs):
    *terms, kept_ref, sent_ref = refs
    count = len(terms) // 2
    width = kept_ref.shape[1]
    for group, out_ref in enumerate((kept_ref, sent_ref)):
        columns = slice(group * width, (group + 1) * width)
        total = dot(terms[0][...], terms[count][:, columns], 0, 0)
        for left, right in zip(terms[1:count], terms[count + 1 :]):
            total = total + dot(left[...], right[:, columns], 0, 0)
        out_ref[...] = total


def products(where, lefts, rights, after):
    length, depth = lefts[0].shape
    width = rights[0].shape[1] // 2
    count = len(lefts)
    tile = depth // 4
    return launch(
        products_kernel, "products", where, (*lefts, *rights),
        [pl.BlockSpec((length, tile), lambda i, w: (0, i))] * count
        + [whole_block(r) for r in rights],
        [shape((depth, width), F32)] * 2, [rows_block(tile, width)] * 2, (4,), 18, after,
        streamed=range(2 * count), stored=(0, 1),
    )


def first_kernel(
    where_ref, part_ref, part_far_ref, slope_ref, normed_ref, scaled_ref, gain_ref,
    wo_ref, one_ref, low_ref, mixed_ref, mixed_far_ref, sums_ref,
):
    step = pl.program_id(0)
    upstream = slope_ref[...] + (part_ref[...] + part_far_ref[...])
    normed = normed_ref[...]

    @pl.when(step == 0)
    def _():
        sums_ref[...] = jnp.zeros_like(sums_ref)

    sums_ref[0:1, :] += jnp.sum(upstream * normed, axis=0, keepdims=True)
    sums_ref[1:2, :] += jnp.sum(upstream, axis=0, keepdims=True)
    slope = norm_back(upstream, normed, scaled_ref[:, 0:1], gain_ref[...])
    one_ref[...] = slope
    low = slope.astype(BF16)
    low_ref[...] = low
    width = mixed_ref.shape[1]
    for ref, chip in ((mixed_ref, where_ref[2]), (mixed_far_ref, 1 - where_ref[2])):
        weights = wo_ref[pl.ds(pl.multiple_of(chip * width, width), width), :]
        ref[...] = dot(low, weights, 1, 1).astype(BF16)


def first(where, part, part_far, slope, normed, scaled, gain, wo, after):
    length, depth = slope.shape
    both = wo.shape[0] // 2
    half = length // 2
    outs = [
        shape((length, depth), F32),
        shape((length, depth), BF16),
        shape((length, both), BF16),
        shape((length, both), BF16),
        shape((8, depth), F32),
    ]
    out_specs = [rows_block(half, o.shape[1]) for o in outs]
    out_specs[4] = whole_block(outs[4])
    rows = rows_block(half, depth)
    return launch(
        first_kernel, "first", where, (part, part_far, slope, normed, scaled, gain, wo),
        [rows, rows, rows, rows, rows_block(half, 128), whole_block(gain), RESIDENT],
        outs, out_specs, (2,), 18, after, streamed=(2, 3, 4), stored=(0, 1),
    )


def attend_back_kernel(where_ref, qkv_ref, go_ref, sums_ref, col_ref, own_ref, near_ref, *rest):
    *extra, out_ref, grads_ref, key_slope, value_slope = rest
    if extra:
        part_ref, one_ref, *_, final_ref = extra
    length = out_ref.shape[0]
    width = own_ref.shape[1] // 3
    owner, lane = lanes(width)
    mask_q, mask_k = mask_terms(col_ref[0][:, 0:1], width)
    zero = jnp.zeros((), BF16)
    term = lane - DOCS
    sums = split(sums_ref[...])
    for group, weights in enumerate((own_ref, near_ref)):
        start = 3 * group * width
        queries, keys, values = (
            qkv_ref[0, :, start + n * width : start + (n + 1) * width] for n in range(3)
        )
        upstream = go_ref[:, group * width : (group + 1) * width]
        row = lax.broadcasted_iota(jnp.int32, (8, 1), 0)
        spare_q = jnp.zeros(queries.shape, F32)
        for n, value in enumerate(sums):
            target = (row // GROUP == group) & ((row % GROUP + 1) % GROUP == owner) & (term == n)
            spare_q = spare_q + dot(value, jnp.where(target, -1.0, 0.0).astype(BF16), 0, 0)
        spare_q = spare_q.astype(BF16) + mask_q
        queries_t = queries.T
        upstream_t = upstream.T
        query_slope = jnp.zeros(queries.shape, F32)
        for head in range(GROUP):
            mine = owner == head
            place = slice(head * HEAD_DIM, (head + 1) * HEAD_DIM)
            chances = jnp.exp(
                dot(pick(head, owner, queries, spare_q, zero), jnp.where(mine, keys, mask_k), 1, 1)
            )
            drift = dot(jnp.where(mine, upstream, zero), values, 1, 1)
            slopes = chances * (drift - jnp.sum(drift * chances, axis=-1, keepdims=True))
            slopes = slopes.astype(BF16)
            query_slope = query_slope + dot(slopes, jnp.where(mine, keys, zero))
            key_slope[place, :] = dot(queries_t[place, :], slopes)
            value_slope[place, :] = dot(upstream_t[place, :], chances.astype(BF16))
        grads_ref[:, start : start + width] = (query_slope * SCALE).astype(BF16)
        grads_ref[:, start + width : start + 2 * width] = key_slope[...].T.astype(BF16)
        grads_ref[:, start + 2 * width : start + 3 * width] = value_slope[...].T.astype(BF16)
        part = dot(grads_ref[:, start : start + 3 * width], weights[...], 1, 1)
        if group == 0:
            out_ref[...] = part
        else:
            out_ref[...] += part
    if extra:
        final = (one_ref[...] + (part_ref[...] + out_ref[...])).astype(BF16)
        final_ref[0] = final
        out_ref[...] = final.astype(F32)


def attend_back(
    i, where, qkv, index, go, mixed, seg_col, own, near, after, extra=(), final=None, count=0
):
    _, length, columns = qkv.shape
    depth, width = own.shape
    out = shape((length, depth), F32)
    grads = shape((length, columns), BF16)
    outs = [out, grads]
    out_specs = [whole_block(o) for o in outs]
    carried = [] if final is None else [final]
    if extra:
        outs = [shape((count, length, depth), BF16), out]
        out_specs = [sequence(i, (length, depth)), whole_block(out)]
    scratch = [pltpu.VMEM((width // 3, length), F32)] * 2
    if extra:
        scratch = [pltpu.VMEM((length, columns), BF16), *scratch]
    return launch(
        attend_back_kernel, "attend_back", where,
        (qkv, go, mixed, seg_col, own, near, *extra, *carried),
        [
            pl.BlockSpec((1, length, columns), lambda g, w: (index, 0, 0)),
            whole_block(go),
            pl.BlockSpec((8, columns // 3), lambda g, w: (length // 8, 0)),
            sequence(i, (length, 128)),
            RESIDENT,
            RESIDENT,
            *[whole_block(e) for e in extra],
            *[ANY] * len(carried),
        ],
        outs, out_specs, (1,), 22, after, scratch=scratch,
        streamed=(0, 3, *range(8, 8 + len(carried))), stored=(0, 1) if extra else (1,),
        aliases={9: 0} if carried else {},
    )


def head_products_kernel(where_ref, *refs, count):
    def take():
        nonlocal refs
        taken, refs = refs[:count], refs[count:]
        return taken

    x_refs, one_refs, grad_refs, mixed_refs, first_refs, second_refs = (take() for _ in range(6))
    tile = x_refs[0].shape[2]
    width = mixed_refs[0].shape[2] // 2
    heads = dot(x_refs[0][0], grad_refs[0][...], 0, 0)
    mixed = dot(one_refs[0][...], mixed_refs[0][0], 0, 0)
    for n in range(1, count):
        heads = heads + dot(x_refs[n][0], grad_refs[n][...], 0, 0)
        mixed = mixed + dot(one_refs[n][...], mixed_refs[n][0], 0, 0)
    for group, (left, right) in enumerate((refs[0:2], refs[2:4])):
        start = 3 * group * width
        left[0, 0:tile, :] = heads[:, start : start + width]
        left[0, tile:, :] = heads[:, start + width : start + 2 * width]
        right[0, 0:tile, :] = heads[:, start + 2 * width : start + 3 * width]
        right[0, tile : 2 * tile, :] = mixed[:, group * width : (group + 1) * width]
        right[0, 2 * tile :, :] = jnp.zeros((8, width), F32)
        for row, sums in ((0, first_refs), (2, second_refs)):
            total = sums[0][0:2, :]
            for ref in sums[1:]:
                total = total + ref[0:2, :]
            right[0, 2 * tile + row : 2 * tile + row + 2, 0:tile] = total


def head_products(where, x, ones, grads, mixed, firsts, seconds, after):
    _, length, depth = x.shape
    count = len(ones)
    width = mixed.shape[2] // 2
    tile = 128
    outs = [shape((depth // tile, 2 * tile + rows, width), F32) for rows in (0, 8)] * 2
    return launch(
        functools.partial(head_products_kernel, count=count), "head_products", where,
        (*[x] * count, *ones, *grads, *[mixed] * count, *firsts, *seconds),
        [
            pl.BlockSpec((1, length, tile), lambda b, w, i=i: (2 * w[1] + i, 0, b))
            for i in range(count)
        ]
        + [pl.BlockSpec((length, tile), lambda b, w: (0, b))] * count
        + [whole_block(a) for a in grads]
        + [pl.BlockSpec((1, *mixed.shape[1:]), lambda b, w, i=i: (i, 0, 0)) for i in range(count)]
        + [pl.BlockSpec((8, tile), lambda b, w: (0, b))] * (2 * count),
        outs, [pl.BlockSpec((1, *o.shape[1:]), lambda b, w: (b, 0, 0)) for o in outs],
        (depth // tile,), 14, after, streamed=range(4 * count), stored=range(4),
    )


def ring_kernel(where_ref, *refs, arrivals, blocks, passed):
    outs = refs[len(refs) - 2 - passed :]
    for way in range(2):
        total = None
        for ref in refs[way : arrivals + blocks : 2]:
            value = ref[0] if len(ref.shape) == 3 else ref[...]
            total = value if total is None else total + value
        if total is not None:
            outs[way][...] = total
    for way in range(passed):
        outs[len(outs) - passed + way][...] = refs[arrivals + blocks + way][0]


def ring_step(owners, n, arrived, blocks, following, after):
    def block(array, way, step):
        return pl.BlockSpec((1, *array.shape[1:]), lambda i, w: (w[2 * step + way], 0, 0))

    specs = [whole_block(a) for a in arrived]
    specs += [block(array, i % 2, n) for i, array in enumerate(blocks)]
    specs += [block(array, i % 2, n + 1) for i, array in enumerate(following)]
    inputs = (*arrived, *blocks, *following)
    outs = [shape(array.shape[1:], F32) for array in (*blocks, *following)[0:2]]
    outs += [shape(array.shape[1:], F32) for array in following]
    return launch(
        functools.partial(
            ring_kernel, arrivals=len(arrived), blocks=len(blocks), passed=len(following)
        ),
        "ring_step", owners, inputs, specs, outs, [whole_block(o) for o in outs],
        (1,), 8, after, streamed=range(len(arrived), len(inputs)),
    )


def finish_kernel(where_ref, value_ref, final_ref, out_ref):
    del final_ref
    out_ref[0] = value_ref[0].astype(BF16)


def finish(i, where, values, final, after):
    _, length, depth = values.shape
    half = length // 2
    return launch(
        finish_kernel, "finish", where, (values, final),
        [pl.BlockSpec((1, half, depth), lambda g, w: (1 - w[1], g, 0)), ANY],
        [shape(final.shape, BF16)],
        [pl.BlockSpec((1, half, depth), lambda g, w: (2 * (1 - w[1]) + i, g, 0))],
        (2,), 8, after, aliases={2: 0}, stored=(0,), streamed=(0, 1),
    )[0]


def solution(mesh):
    ranks = mesh.shape["dp"]
    group = mesh.shape["tensor"]
    assert group == 4 and ranks % 8 == 0
    near_pairs = [(t, t ^ 1) for t in range(group)]
    far_pairs = [(t, t ^ 2) for t in range(group)]
    turns = (
        [(RING[p], RING[(p + 1) % 8]) for p in range(8)],
        [(RING[p], RING[(p - 1) % 8]) for p in range(8)],
    )

    def near(value):
        return lax.ppermute(value, "tensor", near_pairs)

    cores = [[0, 1], [2, 3]]

    def both_cores(value):
        return lax.all_gather(value, "tensor", axis=0, axis_index_groups=cores)

    def scatter(value):
        return lax.psum_scatter(value, "dp", scatter_dimension=0, tiled=True)

    def far(value):
        return lax.ppermute(value, "tensor", far_pairs)

    def body(
        block_input, segment_ids, query_weight, key_weight, value_weight, output_weight,
        first_gain, first_shift, up_weight, down_weight, second_gain, second_shift, out_grad,
    ):
        count, length, depth = block_input.shape
        width = query_weight.shape[1]
        part = depth // ranks
        mine = range(count // 2)
        me = lax.axis_index("tensor")
        rank = lax.axis_index("dp")
        where = jnp.stack([me, me % 2, me // 2, rank]).astype(jnp.int32)
        seg_col = jnp.broadcast_to(segment_ids[:, :, None], (count, length, 128))
        gain_one, shift_one = first_gain[None], first_shift[None]
        gain_two, shift_two = second_gain[None], second_shift[None]
        order = Order()

        def then(call, *args, **kwargs):
            return call(*args, after=order, **kwargs)

        own_low, own_wide, wo_wide = then(
            widen_heads, where, query_weight, key_weight, value_weight, output_weight, part
        )
        near_wide, wo_far = near(own_wide), far(wo_wide)
        near_low, wo_near = then(narrow_near, where, near_wide, output_weight)
        wide = then(convert, where, up_weight, down_weight, dtype=F32)
        wide_near = [near(w) for w in wide]
        mixed_low, qkv, tops, *mixed = then(
            attend, where, block_input, own_low, near_low, seg_col
        )
        mixed_far = [far(m) for m in mixed]
        *wo_far, slices = then(parts, where, wo_far, output_weight.shape[0], 3 * width)
        wo_both = [near(w) for w in wo_far]
        others = lax.all_gather(
            jnp.concatenate([slices, near(slices)], axis=1), "dp", axis=0, tiled=True
        )
        up_near, down_near = then(convert, where, *wide_near, dtype=BF16)
        ups, downs = (up_weight, up_near), (down_weight, down_near)
        wo = then(assemble, where, output_weight, wo_near, wo_far, wo_both)

        forwards, part_far = [], []
        for i in mine:
            forwards.append(
                then(
                    forward, i, where, block_input, mixed[i], mixed_far[i], wo, gain_one,
                    shift_one, ups, downs, halves=i == 0,
                )
            )
            part_far.append([far(p) for p in forwards[i][5:]])

        heads_own = width // HEAD_DIM
        peak = jnp.max(tops, axis=0)
        peak = jnp.maximum(peak[:heads_own], near(peak)[heads_own:])
        step = 1
        while step < ranks:
            peak = jnp.maximum(peak, lax.ppermute(peak, "dp", [(i, i ^ step) for i in range(ranks)]))
            step *= 2
        (peak,) = then(gate, where, peak)

        written = {"layer_out": None, "input_grad": None}
        backs, slope_far = [], []
        for i in mine:
            normed, scaled, low, active, pull, *part_sum = forwards[i]
            backs.append(
                then(
                    backward, i, where, normed, gain_one, shift_one, part_sum, part_far[i],
                    out_grad, gain_two, shift_two, pull, ups, downs, written["layer_out"],
                )
            )
            written["layer_out"], *backs[i] = backs[i]
            slope_far.append(far(backs[i][5]))
            if i == 0:
                far_low, both_low = then(narrow, where, others)
                qkv_far = then(project, where, block_input, far_low, both_low)

        lows, actives = [f[2] for f in forwards], [f[3] for f in forwards]
        slope_lows, befores = [b[2] for b in backs], [b[3] for b in backs]
        up_kept, up_sent = then(products, where, lows, befores)
        down_kept, down_sent = then(products, where, slope_lows, actives)

        def ring_of(blocks, following=(), nears=()):
            held = then(ring_step, owners, 0, nears, blocks, following)
            for n in range(1, 8):
                arrived = [lax.ppermute(h, "dp", t) for h, t in zip(held, turns)]
                arrived += [near(h) for h in held[2:]]
                yield None
                held = then(
                    ring_step, owners, n, arrived, blocks, following if n < 7 else ()
                )
            yield held

        if ranks == 8:
            owners = lax.dynamic_index_in_dim(jnp.asarray(OWNERS, jnp.int32), rank, 0, False)
            following, blocks = [
                [a.reshape(8, part, a.shape[1]) for a in pair]
                for pair in ((up_sent, down_sent), (up_kept, down_kept))
            ]
            passed = then(ring_step, owners, -1, (), (), following)
            ring = ring_of(blocks, following, [near(p) for p in passed[2:]])
            next(ring)
        else:
            ring = iter(())
            up_grad = scatter(up_kept + near(up_sent))
            down_grad = scatter(down_kept + near(down_sent))

        def write(which, i, value):
            written[which] = then(finish, i, where, value, written[which])

        def first_back(i):
            return then(
                first, where, backs[i][5], slope_far[i], backs[i][1], *forwards[i][:2], gain_one,
                wo,
            )

        def own_back(i, go):
            return then(
                attend_back, i, where, qkv, i, go, mixed[i], seg_col, own_low, near_low,
            )

        def far_back(i, go_far, own_part, one):
            written["input_grad"], result = then(
                attend_back, i, where, qkv_far, i, go_far, mixed_far[i], seg_col, far_low,
                both_low, extra=(own_part, one), final=written["input_grad"], count=count,
            )
            return both_cores(result)

        firsts, owns = [], []
        firsts.append(first_back(0))
        next(ring, None)
        owns.append(own_back(0, firsts[0][2]))
        next(ring, None)
        inputs = [far_back(0, firsts[0][3], owns[0][0], firsts[0][0])]
        next(ring, None)
        firsts.append(first_back(1))
        layers = [both_cores(v) for v in then(gate, where, *[b[0] for b in backs])]
        owns.append(own_back(1, firsts[1][2]))
        next(ring, None)
        left, right, *sent = then(
            head_products, where, block_input, [f[1] for f in firsts], [o[1] for o in owns],
            mixed_low, [f[4] for f in firsts], [b[4] for b in backs],
        )
        sent = [near(a) for a in sent]
        if ranks == 8:
            *_, (up_grad, down_grad) = ring
            ring = ring_of((left, right, *sent))
            next(ring)
        write("layer_out", 0, layers[0])
        next(ring, None)
        write("layer_out", 1, layers[1])
        next(ring, None)
        inputs.append(far_back(1, firsts[1][3], owns[1][0], firsts[1][0]))
        next(ring, None)
        write("input_grad", 0, inputs[0])
        next(ring, None)
        next(ring, None)
        write("input_grad", 1, inputs[1])

        tile = 128
        if ranks == 8:
            *_, (left, right) = ring
            query_grad, key_grad = left[:tile], left[tile:]
            value_grad, output_grad = right[:tile], right[tile : 2 * tile].T
            gains = right[2 * tile : 2 * tile + 4, :tile]
        else:
            left, right = left + sent[0], right + sent[1]

            def rows_of(value, n):
                return scatter(value[:, n * tile : (n + 1) * tile].reshape(depth, width))

            query_grad, key_grad, value_grad = rows_of(left, 0), rows_of(left, 1), rows_of(right, 0)
            output_grad = rows_of(right, 1).T
            gains = right[:, 2 * tile : 2 * tile + 4, :tile].transpose(0, 2, 1)
            gains = scatter(gains.reshape(depth, 4)).T

        factor = jnp.sqrt(CLIP / jnp.maximum(peak[:, 0], CLIP))
        column_factor = jnp.repeat(factor, HEAD_DIM)
        query_clipped = query_weight.astype(F32) * column_factor[None, :]
        key_clipped = key_weight.astype(F32) * column_factor[None, :]
        return (
            written["layer_out"], written["input_grad"], query_grad, key_grad, value_grad, output_grad,
            gains[0], gains[1], up_grad, down_grad.T, gains[2], gains[3],
            query_clipped, key_clipped,
        )

    batch = P("dp", None, None)
    in_specs = (
        batch, P("dp", None), P(None, "tensor"), P(None, "tensor"), P(None, "tensor"),
        P("tensor", None), P(), P(), P(None, "tensor"), P("tensor", None), P(), P(), batch,
    )
    out_specs = (
        batch, batch, P("dp", "tensor"), P("dp", "tensor"), P("dp", "tensor"), P("tensor", "dp"),
        P("dp"), P("dp"), P("dp", "tensor"), P("tensor", "dp"), P("dp"), P("dp"),
        P(None, "tensor"), P(None, "tensor"),
    )
    return jax.shard_map(body, mesh=mesh, in_specs=in_specs, out_specs=out_specs, check_vma=False)
```

time: 1350 us -> 486 us (0.36)
  waiting for transfers between devices: 940 us -> 143 us
  Pallas kernels: 0 us -> 244 us
  matrix products: 175 us -> 0 us
  other arithmetic: 74.3 us -> 2.66 us
  blocking collectives: 54.6 us -> 0 us
  local copies, waits for them, and re-layouts: 73.9 us -> 21.9 us
  starting transfers between devices: 0.67 us -> 51.7 us
    psum x4 -> x0, waiting for transfers between devices: 615 us -> none  [the longest x2 309 us: settle(): total = lax.psum(partial_sum, 'tensor')]
    reduce_scatter x6 -> x0, waiting for transfers between devices: 326 us -> none  [the longest x1 92.7 us: reduce_grads(): lax.psum_scatter(column_terms[1], 'dp', scatter_dimension=1, tiled=True)]
    pallas_call x0 -> x45, Pallas kernels: none -> 244 us  [launch(): pl.pallas_call(run, grid_spec=pltpu.PrefetchScalarGridSpec(num_scalar_pre...]
    dot_general x46 -> x0, matrix products: 175 us -> none  [the longest x1 24 us: body(): before = jnp.dot(hidden_low, up_weight, preferred_element_type=jnp.float32)]
    ppermute x0 -> x64, waiting for transfers between devices: none -> 142 us  [the longest x28 60.4 us: ring_of(): arrived = [lax.ppermute(h, 'dp', t) for h, t in zip(held, turns)]]
    ppermute x0 -> x64, starting transfers between devices: none -> 51.5 us  [the longest x28 30.1 us: ring_of(): arrived = [lax.ppermute(h, 'dp', t) for h, t in zip(held, turns)]]
    reduce_sum x6 -> x0, other arithmetic: 34.2 us -> none  [the longest x1 14.4 us: body(): first_gain_part = jnp.sum(hidden_slope * normed_one, axis=(0, 1))]
    unnamed x1 -> x0, blocking collectives: 33.2 us -> none
  transfers between devices with their start and end apart: 10 -> 69, of which waited for: 9 -> 30; matrix products, arithmetic and copies ran while one was open for 5% -> 1% of each run, Pallas kernels for 0% -> 48%
where the time goes in v2:
time: 486 us; the launch traced here: 479 us
  Pallas kernels  244 us (50%)
  waiting for transfers between devices  143 us (29%)
  starting transfers between devices  51.7 us (11%)
  local copies, waits for them, and re-layouts  21.9 us (5%)
  between operations  14.9 us (3%)
    pallas_call x45, Pallas kernels, launch(): pl.pallas_call(run, grid_spec=pltpu.PrefetchScalarGridSpec(num_scalar_pre...  244 us
    ppermute x28, waiting for transfers between devices, ring_of(): arrived = [lax.ppermute(h, 'dp', t) for h, t in zip(held, turns)]  60.4 us
    ppermute x8, waiting for transfers between devices, far(): return lax.ppermute(value, 'tensor', far_pairs)  54.1 us
    ppermute x28, starting transfers between devices, ring_of(): arrived = [lax.ppermute(h, 'dp', t) for h, t in zip(held, turns)]  30.1 us
    ppermute x25, waiting for transfers between devices, near(): return lax.ppermute(value, 'tensor', near_pairs)  20.7 us
    unnamed x112, local copies, waits for them, and re-layouts  18.4 us
    ppermute x8, starting transfers between devices, far(): return lax.ppermute(value, 'tensor', far_pairs)  12.1 us
  transfers between devices with their start and end apart: 69, of which 30 were waited for; matrix products, arithmetic and copies ran while one was open for 1% of the time, Pallas kernels for 48%

profile of v2, /device:TPU:0, one launch (start us, length us, event | category | flops | bytes accessed | tf_op | source)
XLA Modules:
  0.0 478.5 jit_solution(11373904532053203819)
XLA Ops:
  7.3 2.6 widen_heads.1
  10.4 2.6 collective-permute-start.2
  13.0 4.2 collective-permute-done.refs_0_
  18.0 6.5 %convert.2 = (f32[1024,1024]{1,0:T(8,128)}, f32[1024,1024]{1,0:T(8,128)}) custom-call(s32[4]{0:T(128)S(1)} %pad_add_fusion.where_ref, bf16[1024,1024]{1,0:T(8,128)(2,1)} %refs_7_.3, bf16[1024,1024]{1,0:T(8,128)(2,1)} %refs_9_.3, bf16[256,1024]{1,0:T(8,128)(2,1)S(1)} %get-tuple-element.140.refs_2_.refs_1_), custom_call_target="tpu_custom_call" | custom-call | flops 1 | bytes 1 | tf_op jit(solution)/shard_map/convert/pallas_call | solution.py:125
  25.8 16.7 %attend.1 = (bf16[2,512,512]{2,1,0:T(8,128)(2,1)}, bf16[2,512,1536]{2,1,0:T(8,128)(2,1)}, f32[2,8,128]{2,1,0:T(8,128)S(1)}, f32[520,512]{1,0:T(8,128)S(1)}, f32[520,512]{1,0:T(8,128)}) custom-call(s32[4]{0:T(128)S(1)} %pad_add_fusion.where_ref, bf16[4,512,1024]{2,1,0:T(8,128)(2,1)} %refs_1_.5, bf16[1024,768]{1,0:T(8,128)(2,1)S(1)} %get-tuple-element.137.refs_1_.refs_4_, ...), custom_call_target="tpu_custom_call" | custom-call | flops 1 | bytes 1 | tf_op jit(solution)/shard_map/attend/pallas_call | solution.py:125
  42.6 5.4 %collective-permute-done.2.refs_0_ = f32[384,1024]{1,0:T(8,128)S(1)} collective-permute-done((f32[384,1024]{1,0:T(8,128)S(1)}, f32[384,1024]{1,0:T(8,128)S(1)}, u32[]{:S(2)}, u32[]{:S(2)}) %collective-permute-start.2) | collective-permute-done | bytes 1572896 | tf_op jit(solution)/shard_map/ppermute | solution.py:859
  55.6 4.8 %collective-permute-done.5.refs_0_ = f32[1024,1024]{1,0:T(8,128)S(1)} collective-permute-done((f32[1024,1024]{1,0:T(8,128)}, f32[1024,1024]{1,0:T(8,128)S(1)}, u32[]{:S(2)}, u32[]{:S(2)}) %collective-permute-start.5) | collective-permute-done | bytes 4194336 | tf_op jit(solution)/shard_map/ppermute | solution.py:848
  60.6 7.3 %collective-permute-done.6.refs_1_ = f32[1024,1024]{1,0:T(8,128)S(1)} collective-permute-done((f32[1024,1024]{1,0:T(8,128)}, f32[1024,1024]{1,0:T(8,128)S(1)}, u32[]{:S(2)}, u32[]{:S(2)}) %collective-permute-start.6) | collective-permute-done | bytes 4194336 | tf_op jit(solution)/shard_map/ppermute | solution.py:848
  67.9 3.3 convert.3
  72.0 7.9 %collective-permute-done.1.refs_2_ = f32[520,512]{1,0:T(8,128)S(1)} collective-permute-done((f32[520,512]{1,0:T(8,128)S(1)}, f32[520,512]{1,0:T(8,128)S(1)}, u32[]{:S(2)}, u32[]{:S(2)}) %collective-permute-start.1) | collective-permute-done | bytes 1064992 | tf_op jit(solution)/shard_map/ppermute | solution.py:859
  79.9 15.2 %forward.2 = (f32[512,1024]{1,0:T(8,128)}, f32[512,128]{1,0:T(8,128)}, bf16[512,1024]{1,0:T(8,128)(2,1)}, bf16[512,2048]{1,0:T(8,128)(2,1)}, f32[512,2048]{1,0:T...) custom-call(s32[4]{0:T(128)S(1)} %pad_add_fusion.where_ref, bf16[4,512,1024]{2,1,0:T(8,128)(2,1)} %refs_1_.5, ...), custom_call_target="tpu_custom_call" | custom-call | flops 1 | bytes 1 | tf_op jit(solution)/shard_map/forward/pallas_call | solution.py:125
  97.2 5.5 %collective-permute-done.13.refs_2_ = f32[520,512]{1,0:T(8,128)S(1)} collective-permute-done((f32[520,512]{1,0:T(8,128)}, f32[520,512]{1,0:T(8,128)S(1)}, u32[]{:S(2)}, u32[]{:S(2)}) %collective-permute-start.13) | collective-permute-done | bytes 1064992 | tf_op jit(solution)/shard_map/ppermute | solution.py:859
  102.7 13.0 %forward.3 = (f32[512,1024]{1,0:T(8,128)}, f32[512,128]{1,0:T(8,128)}, bf16[512,1024]{1,0:T(8,128)(2,1)}, bf16[512,2048]{1,0:T(8,128)(2,1)}, f32[512,2048]{1,0:T(8,128)}, /*index=5*/f32[512,1024]{1,0:T(8,128)}) custom-call(s32[4]{0:T(128)S(1)} %pad_add_fusion.where_ref, bf16[4,512,1024]{2,1,0:T(8,128)(2,1)} %refs_1_.5, ...), custom_call_target="tpu_custom_call" | custom-call | flops 1 | bytes 1 | tf_op jit(solution)/shard_map/forward/pallas_call | solution.py:125
  120.3 2.0 collective-permute-done.10
  123.9 2.5 collective-permute-done.11
  126.4 2.1 collective-permute-start.12
  128.5 2.4 collective-permute-done.12
  131.5 16.2 %collective-permute-done.8.refs_14_ = f32[256,1024]{1,0:T(8,128)} collective-permute-done((f32[256,1024]{1,0:T(8,128)}, f32[256,1024]{1,0:T(8,128)}, u32[]{:S(2)}, u32[]{:S(2)}) %collective-permute-start.8) | collective-permute-done | bytes 1048608 | tf_op jit(solution)/shard_map/ppermute | solution.py:859
  147.8 14.7 %backward.2 = (bf16[4,512,1024]{2,1,0:T(8,128)(2,1)}, f32[512,1024]{1,0:T(8,128)}, f32[512,1024]{1,0:T(8,128)}, bf16[512,1024]{1,0:T(8,128)(2,1)}, bf16[512,2048...) custom-call(s32[4]{0:T(128)S(1)} %pad_add_fusion.where_ref, ...), custom_call_target="tpu_custom_call" | custom-call | flops 1 | bytes 1 | tf_op jit(solution)/shard_map/backward/pallas_call | solution.py:125
  165.0 4.1 narrow.1
  169.1 7.1 %project.1.refs_14_.refs_0_ = bf16[2,512,1536]{2,1,0:T(8,128)(2,1)} custom-call(s32[4]{0:T(128)S(1)} %pad_add_fusion.where_ref, bf16[4,512,1024]{2,1,0:T(8,128)(2,1)} %refs_1_.5, bf16[1024,768]{1,0:T(8,128)(2,1)S(1)} %get-tuple-element.164.refs_1_.refs_3_.refs_4_, bf16[1024,768]{1,0:T(8,128)(2,1)S(1)} %get-tuple-element.165.refs_2_.refs_5_, ...), custom_call_target="tpu_custom_call" | custom-call | flops 1 | bytes 1 | tf_op jit(solution)/shard_map/project/pallas_call | solution.py:125
  176.2 16.5 %collective-permute-done.14.refs_12_ = f32[512,1024]{1,0:T(8,128)} collective-permute-done((f32[512,1024]{1,0:T(8,128)}, f32[512,1024]{1,0:T(8,128)}, u32[]{:S(2)}, u32[]{:S(2)}) %collective-permute-start.14) | collective-permute-done | bytes 2097184 | tf_op jit(solution)/shard_map/ppermute | solution.py:859
  192.7 14.3 %backward.3 = (bf16[4,512,1024]{2,1,0:T(8,128)(2,1)}, f32[512,1024]{1,0:T(8,128)}, f32[512,1024]{1,0:T(8,128)}, bf16[512,1024]{1,0:T(8,128)(2,1)}, bf16[512,2048...) custom-call(s32[4]{0:T(128)S(1)} %pad_add_fusion.where_ref, ...), custom_call_target="tpu_custom_call", output_to_operand_aliasing={{0}: (14, {})} | custom-call | flops 1 | bytes 1 | tf_op jit(solution)/shard_map/backward/pallas_call | solution.py:125
  207.0 9.2 %products.2 = (f32[1024,1024]{1,0:T(8,128)}, f32[1024,1024]{1,0:T(8,128)}) custom-call(s32[4]{0:T(128)S(1)} %pad_add_fusion.where_ref, bf16[512,1024]{1,0:T(8,128)(2,1)} %get-tuple-element.169.refs_0_, bf16[512,1024]{1,0:T(8,128)(2,1)} %get-tuple-element.170.refs_1_, bf16[512,2048]{1,0:T(8,128)(2,1)} %get-tuple-element.171.refs_2_, ...), custom_call_target="tpu_custom_call" | custom-call | flops 1 | bytes 1 | tf_op jit(solution)/shard_map/products/pallas_call | solution.py:125
  216.2 9.3 %products.3 = (f32[1024,1024]{1,0:T(8,128)}, f32[1024,1024]{1,0:T(8,128)}) custom-call(s32[4]{0:T(128)S(1)} %pad_add_fusion.where_ref, bf16[512,1024]{1,0:T(8,128)(2,1)} %get-tuple-element.175.refs_0_, bf16[512,1024]{1,0:T(8,128)(2,1)} %get-tuple-element.176.refs_1_, bf16[512,2048]{1,0:T(8,128)(2,1)} %get-tuple-element.177.refs_2_, ...), custom_call_target="tpu_custom_call" | custom-call | flops 1 | bytes 1 | tf_op jit(solution)/shard_map/products/pallas_call | solution.py:125
  225.5 2.5 ring_step.17
  230.7 2.3 ring_step.18
  233.0 1.9 collective-permute-start.19
  235.0 2.6 collective-permute-done.23.refs_1_
  237.7 6.4 %first.2 = (f32[512,1024]{1,0:T(8,128)}, bf16[512,1024]{1,0:T(8,128)(2,1)}, bf16[512,512]{1,0:T(8,128)(2,1)S(1)}, bf16[512,512]{1,0:T(8,128)(2,1)S(1)}, f32[8,1024]{1,0:T(8,128)S(1)}) custom-call(s32[4]{0:T(128)S(1)} %pad_add_fusion.where_ref, f32[512,1024]{1,0:T(8,128)} %get-tuple-element.189.refs_0_, f32[512,1024]{1,0:T(8,128)} %collective-permute-done.23.refs_1_, ...), custom_call_target="tpu_custom_call" | custom-call | flops 1 | bytes 1 | tf_op jit(solution)/shard_map/first/pallas_call | solution.py:125
  244.0 3.0 collective-permute-done.19.refs_0_
  248.5 2.6 ring_step.19
  254.1 11.9 %attend_back.4 = (f32[512,1024]{1,0:T(8,128)S(1)}, bf16[512,1536]{1,0:T(8,128)(2,1)}) custom-call(s32[4]{0:T(128)S(1)} %pad_add_fusion.where_ref, bf16[2,512,1536]{2,1,0:T(8,128)(2,1)} %get-tuple-element.196.refs_0_, bf16[512,512]{1,0:T(8,128)(2,1)S(1)} %get-tuple-element.197.refs_1_, f32[520,512]{1,0:T(8,128)S(1)} %get-tuple-element.142.refs_1_.refs_2_, ...), custom_call_target="tpu_custom_call" | custom-call | flops 1 | bytes 1 | tf_op jit(solution)/shard_map/attend_back/pallas_call | solution.py:125
  266.0 2.6 ring_step.20
  271.4 13.1 %attend_back.5 = (bf16[4,512,1024]{2,1,0:T(8,128)(2,1)}, f32[512,1024]{1,0:T(8,128)}) custom-call(s32[4]{0:T(128)S(1)} %pad_add_fusion.where_ref, bf16[2,512,1536]{2,1,0:T(8,128)(2,1)} %project.1.refs_14_.refs_0_, bf16[512,512]{1,0:T(8,128)(2,1)S(1)} %get-tuple-element.203.refs_1_, f32[520,512]{1,0:T(8,128)S(1)} %copy-done.16, ...), custom_call_target="tpu_custom_call" | custom-call | flops 1 | bytes 1 | tf_op jit(solution)/shard_map/attend_back/pallas_call | solution.py:125
  288.1 2.3 ring_step.21
  292.8 6.6 %first.3 = (f32[512,1024]{1,0:T(8,128)}, bf16[512,1024]{1,0:T(8,128)(2,1)}, bf16[512,512]{1,0:T(8,128)(2,1)S(1)}, bf16[512,512]{1,0:T(8,128)(2,1)S(1)}, f32[8,1024]{1,0:T(8,128)S(1)}) custom-call(s32[4]{0:T(128)S(1)} %pad_add_fusion.where_ref, f32[512,1024]{1,0:T(8,128)} %get-tuple-element.167.refs_0_, f32[512,1024]{1,0:T(8,128)} %collective-permute-done.16.refs_1_, ...), custom_call_target="tpu_custom_call" | custom-call | flops 1 | bytes 1 | tf_op jit(solution)/shard_map/first/pallas_call | solution.py:125
  310.1 12.3 %attend_back.6 = (f32[512,1024]{1,0:T(8,128)S(1)}, bf16[512,1536]{1,0:T(8,128)(2,1)}) custom-call(s32[4]{0:T(128)S(1)} %pad_add_fusion.where_ref, bf16[2,512,1536]{2,1,0:T(8,128)(2,1)} %get-tuple-element.196.refs_0_, bf16[512,512]{1,0:T(8,128)(2,1)S(1)} %copy-done.30, f32[520,512]{1,0:T(8,128)} %get-tuple-element.155.refs_1_.refs_2_, ...), custom_call_target="tpu_custom_call" | custom-call | flops 1 | bytes 1 | tf_op jit(solution)/shard_map/attend_back/pallas_call | solution.py:125
  322.4 2.4 ring_step.22
  327.4 12.6 %head_products.1 = (f32[8,256,256]{2,1,0:T(8,128)}, f32[8,264,256]{2,1,0:T(8,128)}, f32[8,256,256]{2,1,0:T(8,128)}, f32[8,264,256]{2,1,0:T(8,128)}) custom-call(s32[4]{0:T(128)S(1)} %pad_add_fusion.where_ref, bf16[4,512,1024]{2,1,0:T(8,128)(2,1)} %refs_1_.5, bf16[4,512,1024]{2,1,0:T(8,128)(2,1)} %refs_1_.5, bf16[512,1024]{1,0:T(8,128)(2,1)} %get-tuple-element.212.refs_2_, ...), custom_call_target="tpu_custom_call" | custom-call | flops 1 | bytes 1 | tf_op jit(solution)/shard_map/head_products/pallas_call | solution.py:125
  340.2 2.4 ring_step.23
  344.9 12.1 %collective-permute-done.42.refs_0_ = f32[128,1024]{1,0:T(8,128)S(1)} collective-permute-done((f32[128,1024]{1,0:T(8,128)S(1)}, f32[128,1024]{1,0:T(8,128)S(1)}, u32[]{:S(2)}, u32[]{:S(2)}) %collective-permute-start.42) | collective-permute-done | bytes 524320 | tf_op jit(solution)/shard_map/ppermute | solution.py:943
  358.9 2.3 ring_step.24
  363.3 11.9 %collective-permute-done.46.refs_0_ = f32[128,1024]{1,0:T(8,128)S(1)} collective-permute-done((f32[128,1024]{1,0:T(8,128)S(1)}, f32[128,1024]{1,0:T(8,128)S(1)}, u32[]{:S(2)}, u32[]{:S(2)}) %collective-permute-start.46) | collective-permute-done | bytes 524320 | tf_op jit(solution)/shard_map/ppermute | solution.py:943
  377.1 2.7 ring_step.25
  386.8 2.9 finish.4.refs_6_.refs_1_
  389.7 3.5 collective-permute-done.50.refs_0_
  393.3 1.8 ring_step.27
  397.4 2.9 finish.5.refs_6_
  400.4 3.3 collective-permute-done.52.refs_0_
  403.7 1.8 ring_step.28
  405.6 13.2 %attend_back.7 = (bf16[4,512,1024]{2,1,0:T(8,128)(2,1)}, f32[512,1024]{1,0:T(8,128)}) custom-call(s32[4]{0:T(128)S(1)} %pad_add_fusion.where_ref, bf16[2,512,1536]{2,1,0:T(8,128)(2,1)} %project.1.refs_14_.refs_0_, bf16[512,512]{1,0:T(8,128)(2,1)S(1)} %copy-done.27, f32[520,512]{1,0:T(8,128)S(1)} %copy-done.18, ...), custom_call_target="tpu_custom_call", output_to_operand_aliasing={{0}: (9, {})} | custom-call | flops 1 | bytes 1 | tf_op jit(solution)/shard_map/attend_back/pallas_call | solution.py:125
  420.9 5.9 %collective-permute-done.54.refs_0_ = f32[256,256]{1,0:T(8,128)S(1)} collective-permute-done((f32[256,256]{1,0:T(8,128)S(1)}, f32[256,256]{1,0:T(8,128)S(1)}, u32[]{:S(2)}, u32[]{:S(2)}) %collective-permute-start.54) | collective-permute-done | bytes 262176 | tf_op jit(solution)/shard_map/ppermute | solution.py:943
  426.8 2.0 ring_step.29
  430.9 2.9 finish.6.refs_6_.refs_1_
  433.8 3.0 collective-permute-done.56.refs_0_
  436.8 1.8 ring_step.30
  440.7 7.1 %collective-permute-done.58.refs_0_ = f32[256,256]{1,0:T(8,128)S(1)} collective-permute-done((f32[256,256]{1,0:T(8,128)S(1)}, f32[256,256]{1,0:T(8,128)S(1)}, u32[]{:S(2)}, u32[]{:S(2)}) %collective-permute-start.58) | collective-permute-done | bytes 262176 | tf_op jit(solution)/shard_map/ppermute | solution.py:943
  452.0 3.0 finish.7.refs_6_
  454.9 4.4 collective-permute-done.60.refs_0_
  459.3 1.8 ring_step.32
  461.2 2.0 collective-permute-start.62
  465.7 1.9 collective-permute-done.62.refs_0_
  467.7 1.8 ring_step.33
  (251 shorter events, 84.5 us)
Async XLA Ops:
  7.2 157.8 %all-gather.10.cloned.1.call-start = ((), (), s32[]{:S(2)}) async-start(), calls=%async_computation | async-start | bytes 7077888 | tf_op jit(solution)/shard_map/all_gather | solution.py:893
  9.9 7.3 %collective-permute-start = (f32[1024,1024]{1,0:T(8,128)S(1)}, f32[1024,1024]{1,0:T(8,128)S(1)}, u32[]{:S(2)}, u32[]{:S(2)}) collective-permute-start(f32[1024,1024]{1,0:T(8,128)S(1)} %get-tuple-element.138), channel_id=1, source_target_pairs={{0,1},{1,0},{2,3},{3,2},{4,5},{5,4},{6,7},{7,6},{8,9},{9,8},{10,11... | collective-permute-start | bytes 12582920 | tf_op jit(solution)/shard_map/ppermute | solution.py:848
  10.4 37.6 %collective-permute-start.2 = (f32[384,1024]{1,0:T(8,128)S(1)}, f32[384,1024]{1,0:T(8,128)S(1)}, u32[]{:S(2)}, u32[]{:S(2)}) collective-permute-start(f32[384,1024]{1,0:T(8,128)S(1)} %get-tuple-element.143), channel_id=1, source_target_pairs={{0,2},{1,3},{2,0},{3,1},{4,6},{5,7},{6,4},{7,5},{8,10},{9,11},{10,... | collective-permute-start | bytes 4718600 | tf_op jit(solution)/shard_map/ppermute | solution.py:859
  52.9 333.8 %all-gather.14.cloned.1.call-start = ((), (), s32[]{:S(2)}) async-start(), calls=%async_computation.2 | async-start | bytes 6291456 | tf_op jit(solution)/shard_map/all_gather | solution.py:853
  53.0 7.4 %collective-permute-start.5 = (f32[1024,1024]{1,0:T(8,128)}, f32[1024,1024]{1,0:T(8,128)S(1)}, u32[]{:S(2)}, u32[]{:S(2)}) collective-permute-start(f32[1024,1024]{1,0:T(8,128)} %get-tuple-element.141.refs_4_), channel_id=1, source_target_pairs={{0,1},{1,0},{2,3},{3,2},{4,5},{5,4},{6,7},{7,6},{8,9},{9,8},{10,11... | collective-permute-start | bytes 12582920 | tf_op jit(solution)/shard_map/ppermute | solution.py:848
  53.2 14.7 %collective-permute-start.6 = (f32[1024,1024]{1,0:T(8,128)}, f32[1024,1024]{1,0:T(8,128)S(1)}, u32[]{:S(2)}, u32[]{:S(2)}) collective-permute-start(f32[1024,1024]{1,0:T(8,128)} %get-tuple-element.147), channel_id=1, source_target_pairs={{0,1},{1,0},{2,3},{3,2},{4,5},{5,4},{6,7},{7,6},{8,9},{9,8},{10,11... | collective-permute-start | bytes 12582920 | tf_op jit(solution)/shard_map/ppermute | solution.py:848
  53.5 26.4 %collective-permute-start.1 = (f32[520,512]{1,0:T(8,128)S(1)}, f32[520,512]{1,0:T(8,128)S(1)}, u32[]{:S(2)}, u32[]{:S(2)}) collective-permute-start(f32[520,512]{1,0:T(8,128)S(1)} %get-tuple-element.142.refs_1_.refs_2_), channel_id=1, source_target_pairs={{0,2},{1,3},{2,0},{3,1},{4,6},{5,7},{6,4},{7,5},{8,10},{9,11},{10,... | collective-permute-start | bytes 3194888 | tf_op jit(solution)/shard_map/ppermute | solution.py:859
  55.3 47.4 %collective-permute-start.13 = (f32[520,512]{1,0:T(8,128)}, f32[520,512]{1,0:T(8,128)S(1)}, u32[]{:S(2)}, u32[]{:S(2)}) collective-permute-start(f32[520,512]{1,0:T(8,128)} %get-tuple-element.155.refs_1_.refs_2_), channel_id=1, source_target_pairs={{0,2},{1,3},{2,0},{3,1},{4,6},{5,7},{6,4},{7,5},{8,10},{9,11},{10,... | collective-permute-start | bytes 3194888 | tf_op jit(solution)/shard_map/ppermute | solution.py:859
  55.6 15.7 %collective-permute-start.3 = (f32[256,512]{1,0:T(8,128)S(1)}, f32[256,512]{1,0:T(8,128)S(1)}, u32[]{:S(2)}, u32[]{:S(2)}) collective-permute-start(f32[256,512]{1,0:T(8,128)S(1)} %copy-done.36), channel_id=1, source_target_pairs={{0,1},{1,0},{2,3},{3,2},{4,5},{5,4},{6,7},{7,6},{8,9},{9,8},{10,11... | collective-permute-start | bytes 1572872 | tf_op jit(solution)/shard_map/ppermute | solution.py:848
  60.4 10.8 %collective-permute-start.4 = (f32[256,512]{1,0:T(8,128)S(1)}, f32[256,512]{1,0:T(8,128)S(1)}, u32[]{:S(2)}, u32[]{:S(2)}) collective-permute-start(f32[256,512]{1,0:T(8,128)S(1)} %copy-done.39), channel_id=1, source_target_pairs={{0,1},{1,0},{2,3},{3,2},{4,5},{5,4},{6,7},{7,6},{8,9},{9,8},{10,11... | collective-permute-start | bytes 1572872 | tf_op jit(solution)/shard_map/ppermute | solution.py:848
  95.1 36.4 %collective-permute-start.7 = (f32[256,1024]{1,0:T(8,128)}, f32[256,1024]{1,0:T(8,128)}, u32[]{:S(2)}, u32[]{:S(2)}) collective-permute-start(f32[256,1024]{1,0:T(8,128)} %get-tuple-element.153.refs_11_), channel_id=1, source_target_pairs={{0,2},{1,3},{2,0},{3,1},{4,6},{5,7},{6,4},{7,5},{8,10},{9,11},{10,... | collective-permute-start | bytes 3145736 | tf_op jit(solution)/shard_map/ppermute | solution.py:859
  97.0 50.8 %collective-permute-start.8 = (f32[256,1024]{1,0:T(8,128)}, f32[256,1024]{1,0:T(8,128)}, u32[]{:S(2)}, u32[]{:S(2)}) collective-permute-start(f32[256,1024]{1,0:T(8,128)} %get-tuple-element.154.refs_12_), channel_id=1, source_target_pairs={{0,2},{1,3},{2,0},{3,1},{4,6},{5,7},{6,4},{7,5},{8,10},{9,11},{10,... | collective-permute-start | bytes 3145736 | tf_op jit(solution)/shard_map/ppermute | solution.py:859
  115.7 77.0 %collective-permute-start.14 = (f32[512,1024]{1,0:T(8,128)}, f32[512,1024]{1,0:T(8,128)}, u32[]{:S(2)}, u32[]{:S(2)}) collective-permute-start(f32[512,1024]{1,0:T(8,128)} %get-tuple-element.161.refs_11_), channel_id=1, source_target_pairs={{0,2},{1,3},{2,0},{3,1},{4,6},{5,7},{6,4},{7,5},{8,10},{9,11},{10,... | collective-permute-start | bytes 6291464 | tf_op jit(solution)/shard_map/ppermute | solution.py:859
  118.7 3.6 collective-permute-start.10
  122.3 4.1 collective-permute-start.11
  126.4 4.5 collective-permute-start.12
  162.5 75.2 %collective-permute-start.23 = (f32[512,1024]{1,0:T(8,128)}, f32[512,1024]{1,0:T(8,128)}, u32[]{:S(2)}, u32[]{:S(2)}) collective-permute-start(f32[512,1024]{1,0:T(8,128)} %get-tuple-element.189.refs_0_), channel_id=1, source_target_pairs={{0,2},{1,3},{2,0},{3,1},{4,6},{5,7},{6,4},{7,5},{8,10},{9,11},{10,... | collective-permute-start | bytes 6291464 | tf_op jit(solution)/shard_map/ppermute | solution.py:859
  228.0 2.7 collective-permute-start.18
  228.6 63.5 %collective-permute-start.16 = (f32[512,1024]{1,0:T(8,128)}, f32[512,1024]{1,0:T(8,128)}, u32[]{:S(2)}, u32[]{:S(2)}) collective-permute-start(f32[512,1024]{1,0:T(8,128)} %get-tuple-element.167.refs_0_), channel_id=1, source_target_pairs={{0,2},{1,3},{2,0},{3,1},{4,6},{5,7},{6,4},{7,5},{8,10},{9,11},{10,... | collective-permute-start | bytes 6291464 | tf_op jit(solution)/shard_map/ppermute | solution.py:859
  233.0 14.0 %collective-permute-start.19 = (f32[128,1024]{1,0:T(8,128)S(1)}, f32[128,1024]{1,0:T(8,128)S(1)}, u32[]{:S(2)}, u32[]{:S(2)}) collective-permute-start(f32[128,1024]{1,0:T(8,128)S(1)} %get-tuple-element.185.refs_7_), channel_id=1, source_target_pairs={{0,8},{8,16},{16,24},{24,28},{28,20},{20,12},{12,4},{4,0},{1,9},{9... | collective-permute-start | bytes 1572872 | tf_op jit(solution)/shard_map/ppermute | solution.py:943
  234.8 13.7 %collective-permute-start.20 = (f32[128,1024]{1,0:T(8,128)S(1)}, f32[128,1024]{1,0:T(8,128)S(1)}, u32[]{:S(2)}, u32[]{:S(2)}) collective-permute-start(f32[128,1024]{1,0:T(8,128)S(1)} %get-tuple-element.186), channel_id=1, source_target_pairs={{0,4},{8,0},{16,8},{24,16},{28,24},{20,28},{12,20},{4,12},{1,5},{9... | collective-permute-start | bytes 1572872 | tf_op jit(solution)/shard_map/ppermute | solution.py:943
  235.0 13.5 %collective-permute-start.21 = (f32[128,1024]{1,0:T(8,128)S(1)}, f32[128,1024]{1,0:T(8,128)S(1)}, u32[]{:S(2)}, u32[]{:S(2)}) collective-permute-start(f32[128,1024]{1,0:T(8,128)S(1)} %get-tuple-element.187), channel_id=1, source_target_pairs={{0,1},{1,0},{2,3},{3,2},{4,5},{5,4},{6,7},{7,6},{8,9},{9,8},{10,11... | collective-permute-start | bytes 1572872 | tf_op jit(solution)/shard_map/ppermute | solution.py:848
  237.6 10.9 %collective-permute-start.22 = (f32[128,1024]{1,0:T(8,128)S(1)}, f32[128,1024]{1,0:T(8,128)S(1)}, u32[]{:S(2)}, u32[]{:S(2)}) collective-permute-start(f32[128,1024]{1,0:T(8,128)S(1)} %get-tuple-element.188), channel_id=1, source_target_pairs={{0,1},{1,0},{2,3},{3,2},{4,5},{5,4},{6,7},{7,6},{8,9},{9,8},{10,11... | collective-permute-start | bytes 1572872 | tf_op jit(solution)/shard_map/ppermute | solution.py:848
  251.1 14.9 %collective-permute-start.24 = (f32[128,1024]{1,0:T(8,128)S(1)}, f32[128,1024]{1,0:T(8,128)S(1)}, u32[]{:S(2)}, u32[]{:S(2)}) collective-permute-start(f32[128,1024]{1,0:T(8,128)S(1)} %get-tuple-element.192.refs_6_), channel_id=1, source_target_pairs={{0,8},{8,16},{16,24},{24,28},{28,20},{20,12},{12,4},{4,0},{1,9},{9... | collective-permute-start | bytes 1572872 | tf_op jit(solution)/shard_map/ppermute | solution.py:943
  252.8 13.2 %collective-permute-start.25 = (f32[128,1024]{1,0:T(8,128)S(1)}, f32[128,1024]{1,0:T(8,128)S(1)}, u32[]{:S(2)}, u32[]{:S(2)}) collective-permute-start(f32[128,1024]{1,0:T(8,128)S(1)} %get-tuple-element.193), channel_id=1, source_target_pairs={{0,4},{8,0},{16,8},{24,16},{28,24},{20,28},{12,20},{4,12},{1,5},{9... | collective-permute-start | bytes 1572872 | tf_op jit(solution)/shard_map/ppermute | solution.py:943
  253.6 12.4 %collective-permute-start.26 = (f32[128,1024]{1,0:T(8,128)S(1)}, f32[128,1024]{1,0:T(8,128)S(1)}, u32[]{:S(2)}, u32[]{:S(2)}) collective-permute-start(f32[128,1024]{1,0:T(8,128)S(1)} %get-tuple-element.194), channel_id=1, source_target_pairs={{0,1},{1,0},{2,3},{3,2},{4,5},{5,4},{6,7},{7,6},{8,9},{9,8},{10,11... | collective-permute-start | bytes 1572872 | tf_op jit(solution)/shard_map/ppermute | solution.py:848
  253.6 12.4 %collective-permute-start.27 = (f32[128,1024]{1,0:T(8,128)S(1)}, f32[128,1024]{1,0:T(8,128)S(1)}, u32[]{:S(2)}, u32[]{:S(2)}) collective-permute-start(f32[128,1024]{1,0:T(8,128)S(1)} %get-tuple-element.195), channel_id=1, source_target_pairs={{0,1},{1,0},{2,3},{3,2},{4,5},{5,4},{6,7},{7,6},{8,9},{9,8},{10,11... | collective-permute-start | bytes 1572872 | tf_op jit(solution)/shard_map/ppermute | solution.py:848
  268.6 15.8 %collective-permute-start.28 = (f32[128,1024]{1,0:T(8,128)S(1)}, f32[128,1024]{1,0:T(8,128)S(1)}, u32[]{:S(2)}, u32[]{:S(2)}) collective-permute-start(f32[128,1024]{1,0:T(8,128)S(1)} %get-tuple-element.199.refs_8_), channel_id=1, source_target_pairs={{0,8},{8,16},{16,24},{24,28},{28,20},{20,12},{12,4},{4,0},{1,9},{9... | collective-permute-start | bytes 1572872 | tf_op jit(solution)/shard_map/ppermute | solution.py:943
  270.3 14.2 %collective-permute-start.29 = (f32[128,1024]{1,0:T(8,128)S(1)}, f32[128,1024]{1,0:T(8,128)S(1)}, u32[]{:S(2)}, u32[]{:S(2)}) collective-permute-start(f32[128,1024]{1,0:T(8,128)S(1)} %get-tuple-element.200), channel_id=1, source_target_pairs={{0,4},{8,0},{16,8},{24,16},{28,24},{20,28},{12,20},{4,12},{1,5},{9... | collective-permute-start | bytes 1572872 | tf_op jit(solution)/shard_map/ppermute | solution.py:943
  270.8 13.6 %collective-permute-start.30 = (f32[128,1024]{1,0:T(8,128)S(1)}, f32[128,1024]{1,0:T(8,128)S(1)}, u32[]{:S(2)}, u32[]{:S(2)}) collective-permute-start(f32[128,1024]{1,0:T(8,128)S(1)} %get-tuple-element.201), channel_id=1, source_target_pairs={{0,1},{1,0},{2,3},{3,2},{4,5},{5,4},{6,7},{7,6},{8,9},{9,8},{10,11... | collective-permute-start | bytes 1572872 | tf_op jit(solution)/shard_map/ppermute | solution.py:848
  270.8 14.4 %collective-permute-start.31 = (f32[128,1024]{1,0:T(8,128)S(1)}, f32[128,1024]{1,0:T(8,128)S(1)}, u32[]{:S(2)}, u32[]{:S(2)}) collective-permute-start(f32[128,1024]{1,0:T(8,128)S(1)} %get-tuple-element.202), channel_id=1, source_target_pairs={{0,1},{1,0},{2,3},{3,2},{4,5},{5,4},{6,7},{7,6},{8,9},{9,8},{10,11... | collective-permute-start | bytes 1572872 | tf_op jit(solution)/shard_map/ppermute | solution.py:848
  303.2 94.2 %all-gather.12.cloned.1.call-start = ((), (), s32[]{:S(2)}) async-start(), calls=%async_computation.1 | async-start | bytes 6291456 | tf_op jit(solution)/shard_map/all_gather | solution.py:853
  304.0 126.9 %all-gather.18.cloned.1.call-start = ((), (), s32[]{:S(2)}) async-start(), calls=%async_computation.4 | async-start | bytes 6291456 | tf_op jit(solution)/shard_map/all_gather | solution.py:853
  304.5 147.4 %all-gather.16.cloned.1.call-start = ((), (), s32[]{:S(2)}) async-start(), calls=%async_computation.3 | async-start | bytes 6291456 | tf_op jit(solution)/shard_map/all_gather | solution.py:853
  304.6 17.8 %collective-permute-start.32 = (f32[128,1024]{1,0:T(8,128)}, f32[128,1024]{1,0:T(8,128)S(1)}, u32[]{:S(2)}, u32[]{:S(2)}) collective-permute-start(f32[128,1024]{1,0:T(8,128)} %copy-done.41), channel_id=1, source_target_pairs={{0,8},{8,16},{16,24},{24,28},{28,20},{20,12},{12,4},{4,0},{1,9},{9... | collective-permute-start | bytes 1572872 | tf_op jit(solution)/shard_map/ppermute | solution.py:943
  306.3 16.1 %collective-permute-start.33 = (f32[128,1024]{1,0:T(8,128)}, f32[128,1024]{1,0:T(8,128)S(1)}, u32[]{:S(2)}, u32[]{:S(2)}) collective-permute-start(f32[128,1024]{1,0:T(8,128)} %copy-done.48), channel_id=1, source_target_pairs={{0,4},{8,0},{16,8},{24,16},{28,24},{20,28},{12,20},{4,12},{1,5},{9... | collective-permute-start | bytes 1572872 | tf_op jit(solution)/shard_map/ppermute | solution.py:943
  306.9 15.5 %collective-permute-start.34 = (f32[128,1024]{1,0:T(8,128)}, f32[128,1024]{1,0:T(8,128)S(1)}, u32[]{:S(2)}, u32[]{:S(2)}) collective-permute-start(f32[128,1024]{1,0:T(8,128)} %copy-done.47), channel_id=1, source_target_pairs={{0,1},{1,0},{2,3},{3,2},{4,5},{5,4},{6,7},{7,6},{8,9},{9,8},{10,11... | collective-permute-start | bytes 1572872 | tf_op jit(solution)/shard_map/ppermute | solution.py:848
  306.9 15.5 %collective-permute-start.35 = (f32[128,1024]{1,0:T(8,128)}, f32[128,1024]{1,0:T(8,128)S(1)}, u32[]{:S(2)}, u32[]{:S(2)}) collective-permute-start(f32[128,1024]{1,0:T(8,128)} %copy-done.46), channel_id=1, source_target_pairs={{0,1},{1,0},{2,3},{3,2},{4,5},{5,4},{6,7},{7,6},{8,9},{9,8},{10,11... | collective-permute-start | bytes 1572872 | tf_op jit(solution)/shard_map/ppermute | solution.py:848
  324.8 15.3 %collective-permute-start.38 = (f32[128,1024]{1,0:T(8,128)S(1)}, f32[128,1024]{1,0:T(8,128)S(1)}, u32[]{:S(2)}, u32[]{:S(2)}) collective-permute-start(f32[128,1024]{1,0:T(8,128)S(1)} %get-tuple-element.220.refs_12_), channel_id=1, source_target_pairs={{0,8},{8,16},{16,24},{24,28},{28,20},{20,12},{12,4},{4,0},{1,9},{9... | collective-permute-start | bytes 1572872 | tf_op jit(solution)/shard_map/ppermute | solution.py:943
  326.5 13.6 %collective-permute-start.39 = (f32[128,1024]{1,0:T(8,128)S(1)}, f32[128,1024]{1,0:T(8,128)S(1)}, u32[]{:S(2)}, u32[]{:S(2)}) collective-permute-start(f32[128,1024]{1,0:T(8,128)S(1)} %get-tuple-element.225), channel_id=1, source_target_pairs={{0,4},{8,0},{16,8},{24,16},{28,24},{20,28},{12,20},{4,12},{1,5},{9... | collective-permute-start | bytes 1572872 | tf_op jit(solution)/shard_map/ppermute | solution.py:943
  326.9 13.2 %collective-permute-start.40 = (f32[128,1024]{1,0:T(8,128)S(1)}, f32[128,1024]{1,0:T(8,128)S(1)}, u32[]{:S(2)}, u32[]{:S(2)}) collective-permute-start(f32[128,1024]{1,0:T(8,128)S(1)} %get-tuple-element.226), channel_id=1, source_target_pairs={{0,1},{1,0},{2,3},{3,2},{4,5},{5,4},{6,7},{7,6},{8,9},{9,8},{10,11... | collective-permute-start | bytes 1572872 | tf_op jit(solution)/shard_map/ppermute | solution.py:848
  326.9 13.2 %collective-permute-start.41 = (f32[128,1024]{1,0:T(8,128)S(1)}, f32[128,1024]{1,0:T(8,128)S(1)}, u32[]{:S(2)}, u32[]{:S(2)}) collective-permute-start(f32[128,1024]{1,0:T(8,128)S(1)} %get-tuple-element.227), channel_id=1, source_target_pairs={{0,1},{1,0},{2,3},{3,2},{4,5},{5,4},{6,7},{7,6},{8,9},{9,8},{10,11... | collective-permute-start | bytes 1572872 | tf_op jit(solution)/shard_map/ppermute | solution.py:848
  340.1 39.8 %collective-permute-start.37 = (f32[8,264,256]{2,1,0:T(8,128)}, f32[8,264,256]{2,1,0:T(8,128)S(1)}, u32[]{:S(2)}, u32[]{:S(2)}) collective-permute-start(f32[8,264,256]{2,1,0:T(8,128)} %get-tuple-element.224), channel_id=1, source_target_pairs={{0,1},{1,0},{2,3},{3,2},{4,5},{5,4},{6,7},{7,6},{8,9},{9,8},{10,11... | collective-permute-start | bytes 6488072 | tf_op jit(solution)/shard_map/ppermute | solution.py:848
  342.6 14.4 %collective-permute-start.42 = (f32[128,1024]{1,0:T(8,128)S(1)}, f32[128,1024]{1,0:T(8,128)S(1)}, u32[]{:S(2)}, u32[]{:S(2)}) collective-permute-start(f32[128,1024]{1,0:T(8,128)S(1)} %get-tuple-element.228.refs_8_), channel_id=1, source_target_pairs={{0,8},{8,16},{16,24},{24,28},{28,20},{20,12},{12,4},{4,0},{1,9},{9... | collective-permute-start | bytes 1572872 | tf_op jit(solution)/shard_map/ppermute | solution.py:943
  344.2 35.6 %collective-permute-start.36 = (f32[8,256,256]{2,1,0:T(8,128)S(1)}, f32[8,256,256]{2,1,0:T(8,128)S(1)}, u32[]{:S(2)}, u32[]{:S(2)}) collective-permute-start(f32[8,256,256]{2,1,0:T(8,128)S(1)} %copy-done.54), channel_id=1, source_target_pairs={{0,1},{1,0},{2,3},{3,2},{4,5},{5,4},{6,7},{7,6},{8,9},{9,8},{10,11... | collective-permute-start | bytes 6291464 | tf_op jit(solution)/shard_map/ppermute | solution.py:848
  344.4 14.1 %collective-permute-start.43 = (f32[128,1024]{1,0:T(8,128)S(1)}, f32[128,1024]{1,0:T(8,128)S(1)}, u32[]{:S(2)}, u32[]{:S(2)}) collective-permute-start(f32[128,1024]{1,0:T(8,128)S(1)} %get-tuple-element.229), channel_id=1, source_target_pairs={{0,4},{8,0},{16,8},{24,16},{28,24},{20,28},{12,20},{4,12},{1,5},{9... | collective-permute-start | bytes 1572872 | tf_op jit(solution)/shard_map/ppermute | solution.py:943
  344.9 13.6 %collective-permute-start.44 = (f32[128,1024]{1,0:T(8,128)S(1)}, f32[128,1024]{1,0:T(8,128)S(1)}, u32[]{:S(2)}, u32[]{:S(2)}) collective-permute-start(f32[128,1024]{1,0:T(8,128)S(1)} %get-tuple-element.230), channel_id=1, source_target_pairs={{0,1},{1,0},{2,3},{3,2},{4,5},{5,4},{6,7},{7,6},{8,9},{9,8},{10,11... | collective-permute-start | bytes 1572872 | tf_op jit(solution)/shard_map/ppermute | solution.py:848
  361.2 14.0 %collective-permute-start.46 = (f32[128,1024]{1,0:T(8,128)S(1)}, f32[128,1024]{1,0:T(8,128)S(1)}, u32[]{:S(2)}, u32[]{:S(2)}) collective-permute-start(f32[128,1024]{1,0:T(8,128)S(1)} %get-tuple-element.232.refs_6_), channel_id=1, source_target_pairs={{0,8},{8,16},{16,24},{24,28},{28,20},{20,12},{12,4},{4,0},{1,9},{9... | collective-permute-start | bytes 1572872 | tf_op jit(solution)/shard_map/ppermute | solution.py:943
  362.8 13.7 %collective-permute-start.47 = (f32[128,1024]{1,0:T(8,128)S(1)}, f32[128,1024]{1,0:T(8,128)S(1)}, u32[]{:S(2)}, u32[]{:S(2)}) collective-permute-start(f32[128,1024]{1,0:T(8,128)S(1)} %get-tuple-element.233), channel_id=1, source_target_pairs={{0,4},{8,0},{16,8},{24,16},{28,24},{20,28},{12,20},{4,12},{1,5},{9... | collective-permute-start | bytes 1572872 | tf_op jit(solution)/shard_map/ppermute | solution.py:943
  363.3 13.2 %collective-permute-start.48 = (f32[128,1024]{1,0:T(8,128)S(1)}, f32[128,1024]{1,0:T(8,128)S(1)}, u32[]{:S(2)}, u32[]{:S(2)}) collective-permute-start(f32[128,1024]{1,0:T(8,128)S(1)} %get-tuple-element.234), channel_id=1, source_target_pairs={{0,1},{1,0},{2,3},{3,2},{4,5},{5,4},{6,7},{7,6},{8,9},{9,8},{10,11... | collective-permute-start | bytes 1572872 | tf_op jit(solution)/shard_map/ppermute | solution.py:848
  384.7 8.6 %collective-permute-start.51 = (f32[264,256]{1,0:T(8,128)S(1)}, f32[264,256]{1,0:T(8,128)S(1)}, u32[]{:S(2)}, u32[]{:S(2)}) collective-permute-start(f32[264,256]{1,0:T(8,128)S(1)} %get-tuple-element.238), channel_id=1, source_target_pairs={{0,4},{8,0},{16,8},{24,16},{28,24},{20,28},{12,20},{4,12},{1,5},{9... | collective-permute-start | bytes 811016 | tf_op jit(solution)/shard_map/ppermute | solution.py:943
  385.1 8.1 %collective-permute-start.50 = (f32[256,256]{1,0:T(8,128)S(1)}, f32[256,256]{1,0:T(8,128)S(1)}, u32[]{:S(2)}, u32[]{:S(2)}) collective-permute-start(f32[256,256]{1,0:T(8,128)S(1)} %get-tuple-element.237.refs_2_), channel_id=1, source_target_pairs={{0,8},{8,16},{16,24},{24,28},{28,20},{20,12},{12,4},{4,0},{1,9},{9... | collective-permute-start | bytes 786440 | tf_op jit(solution)/shard_map/ppermute | solution.py:943
  395.1 8.6 %collective-permute-start.53 = (f32[264,256]{1,0:T(8,128)S(1)}, f32[264,256]{1,0:T(8,128)S(1)}, u32[]{:S(2)}, u32[]{:S(2)}) collective-permute-start(f32[264,256]{1,0:T(8,128)S(1)} %get-tuple-element.244), channel_id=1, source_target_pairs={{0,4},{8,0},{16,8},{24,16},{28,24},{20,28},{12,20},{4,12},{1,5},{9... | collective-permute-start | bytes 811016 | tf_op jit(solution)/shard_map/ppermute | solution.py:943
  396.8 6.9 %collective-permute-start.52 = (f32[256,256]{1,0:T(8,128)S(1)}, f32[256,256]{1,0:T(8,128)S(1)}, u32[]{:S(2)}, u32[]{:S(2)}) collective-permute-start(f32[256,256]{1,0:T(8,128)S(1)} %get-tuple-element.239.refs_2_), channel_id=1, source_target_pairs={{0,8},{8,16},{16,24},{24,28},{28,20},{20,12},{12,4},{4,0},{1,9},{9... | collective-permute-start | bytes 786440 | tf_op jit(solution)/shard_map/ppermute | solution.py:943
  418.8 8.0 %collective-permute-start.55 = (f32[264,256]{1,0:T(8,128)S(1)}, f32[264,256]{1,0:T(8,128)S(1)}, u32[]{:S(2)}, u32[]{:S(2)}) collective-permute-start(f32[264,256]{1,0:T(8,128)S(1)} %get-tuple-element.248), channel_id=1, source_target_pairs={{0,4},{8,0},{16,8},{24,16},{28,24},{20,28},{12,20},{4,12},{1,5},{9... | collective-permute-start | bytes 811016 | tf_op jit(solution)/shard_map/ppermute | solution.py:943
  420.4 6.4 %collective-permute-start.54 = (f32[256,256]{1,0:T(8,128)S(1)}, f32[256,256]{1,0:T(8,128)S(1)}, u32[]{:S(2)}, u32[]{:S(2)}) collective-permute-start(f32[256,256]{1,0:T(8,128)S(1)} %get-tuple-element.245.refs_9_), channel_id=1, source_target_pairs={{0,8},{8,16},{16,24},{24,28},{28,20},{20,12},{12,4},{4,0},{1,9},{9... | collective-permute-start | bytes 786440 | tf_op jit(solution)/shard_map/ppermute | solution.py:943
  428.8 8.0 %collective-permute-start.57 = (f32[264,256]{1,0:T(8,128)S(1)}, f32[264,256]{1,0:T(8,128)S(1)}, u32[]{:S(2)}, u32[]{:S(2)}) collective-permute-start(f32[264,256]{1,0:T(8,128)S(1)} %get-tuple-element.250), channel_id=1, source_target_pairs={{0,4},{8,0},{16,8},{24,16},{28,24},{20,28},{12,20},{4,12},{1,5},{9... | collective-permute-start | bytes 811016 | tf_op jit(solution)/shard_map/ppermute | solution.py:943
  430.4 6.4 %collective-permute-start.56 = (f32[256,256]{1,0:T(8,128)S(1)}, f32[256,256]{1,0:T(8,128)S(1)}, u32[]{:S(2)}, u32[]{:S(2)}) collective-permute-start(f32[256,256]{1,0:T(8,128)S(1)} %get-tuple-element.249.refs_2_), channel_id=1, source_target_pairs={{0,8},{8,16},{16,24},{24,28},{28,20},{20,12},{12,4},{4,0},{1,9},{9... | collective-permute-start | bytes 786440 | tf_op jit(solution)/shard_map/ppermute | solution.py:943
  438.6 9.2 %collective-permute-start.59 = (f32[264,256]{1,0:T(8,128)S(1)}, f32[264,256]{1,0:T(8,128)S(1)}, u32[]{:S(2)}, u32[]{:S(2)}) collective-permute-start(f32[264,256]{1,0:T(8,128)S(1)} %get-tuple-element.252), channel_id=1, source_target_pairs={{0,4},{8,0},{16,8},{24,16},{28,24},{20,28},{12,20},{4,12},{1,5},{9... | collective-permute-start | bytes 811016 | tf_op jit(solution)/shard_map/ppermute | solution.py:943
  440.3 7.5 %collective-permute-start.58 = (f32[256,256]{1,0:T(8,128)S(1)}, f32[256,256]{1,0:T(8,128)S(1)}, u32[]{:S(2)}, u32[]{:S(2)}) collective-permute-start(f32[256,256]{1,0:T(8,128)S(1)} %get-tuple-element.251.refs_6_), channel_id=1, source_target_pairs={{0,8},{8,16},{16,24},{24,28},{28,20},{20,12},{12,4},{4,0},{1,9},{9... | collective-permute-start | bytes 786440 | tf_op jit(solution)/shard_map/ppermute | solution.py:943
  449.6 9.7 %collective-permute-start.61 = (f32[264,256]{1,0:T(8,128)S(1)}, f32[264,256]{1,0:T(8,128)S(1)}, u32[]{:S(2)}, u32[]{:S(2)}) collective-permute-start(f32[264,256]{1,0:T(8,128)S(1)} %get-tuple-element.254), channel_id=1, source_target_pairs={{0,4},{8,0},{16,8},{24,16},{28,24},{20,28},{12,20},{4,12},{1,5},{9... | collective-permute-start | bytes 811016 | tf_op jit(solution)/shard_map/ppermute | solution.py:943
  450.4 8.9 %collective-permute-start.60 = (f32[256,256]{1,0:T(8,128)S(1)}, f32[256,256]{1,0:T(8,128)S(1)}, u32[]{:S(2)}, u32[]{:S(2)}) collective-permute-start(f32[256,256]{1,0:T(8,128)S(1)} %get-tuple-element.253.refs_2_), channel_id=1, source_target_pairs={{0,8},{8,16},{16,24},{24,28},{28,20},{20,12},{12,4},{4,0},{1,9},{9... | collective-permute-start | bytes 786440 | tf_op jit(solution)/shard_map/ppermute | solution.py:943
  461.1 6.5 %collective-permute-start.63 = (f32[264,256]{1,0:T(8,128)S(1)}, f32[264,256]{1,0:T(8,128)S(1)}, u32[]{:S(2)}, u32[]{:S(2)}) collective-permute-start(f32[264,256]{1,0:T(8,128)S(1)} %get-tuple-element.256), channel_id=1, source_target_pairs={{0,4},{8,0},{16,8},{24,16},{28,24},{20,28},{12,20},{4,12},{1,5},{9... | collective-permute-start | bytes 811016 | tf_op jit(solution)/shard_map/ppermute | solution.py:943
  461.2 6.4 %collective-permute-start.62 = (f32[256,256]{1,0:T(8,128)S(1)}, f32[256,256]{1,0:T(8,128)S(1)}, u32[]{:S(2)}, u32[]{:S(2)}) collective-permute-start(f32[256,256]{1,0:T(8,128)S(1)} %get-tuple-element.255.refs_6_), channel_id=1, source_target_pairs={{0,8},{8,16},{16,24},{24,28},{28,20},{20,12},{12,4},{4,0},{1,9},{9... | collective-permute-start | bytes 786440 | tf_op jit(solution)/shard_map/ppermute | solution.py:943
  (60 other events, 569.2 us)
Sparse Core Ops, SparseCore 0:
  53.0 100.6 all-gather.9
  303.3 13.9 all-gather.13
  318.9 14.8 all-gather.11
  335.2 17.0 all-gather.17
  418.9 14.3 all-gather.15
